TPU v7x, 32 devices: a whole 2x2x4 slice. The times are simulated.
32 devices in a mesh: grp: 2 (over y), seq: 4 (over z), row: 2 (over x), col: 2 (over core).
Axes of the slice: x: 2, y: 2, z: 4, core: 2. Of those that a mesh axis runs over, the one named last changes fastest.
Arguments:
- acts: bfloat16 [1024, 4096], P(('grp', 'seq'), ('row', 'col')), parts along dimension 0, may hold values from -6 to 6
- grads: bfloat16 [1024, 4096], P(('grp', 'seq'), ('row', 'col')), parts along dimension 0, may hold values from -0.25 to 0.25
- source_ids: int32 [1024], P(('grp', 'seq')), parts along dimension 0, may hold values from 0 to 7
- basis_in: bfloat16 [4096, 4096], P('seq', ('row', 'col')), may hold values from -0.09375 to 0.09375
- basis_out: bfloat16 [4096, 4096], P('seq', ('row', 'col')), may hold values from -0.09375 to 0.09375
- eigvals: float32 [4096, 4096], P('seq', ('row', 'col')), may hold values from 0.5 to 8
Outputs:
- precond: float32 [8192, 4096], P(('grp', 'seq'), ('row', 'col')), parts along dimension 0
- scores: float32 [1024], P(('grp', 'seq')), parts along dimension 0
- influence: float32 [16], P('grp'), parts along dimension 0
There are 2 independent parts, one for each index of `grp`. A program takes and returns all parts, laid end to end along the dimension named above; an argument that names none is the same for every part. Nothing has to cross between parts.
All inputs are finite; a program needn't handle non-finite values.
Results may differ from a plain program's by a relative error of at most 0.0085.
Values may be sent and summed in bfloat16 or wider, within the bound.
No kernel may reach another device: no remote copies, remote signals or barrier semaphores. Data moves between devices by JAX's collectives and lax.ppermute only.
A program may use at most 128 MiB of HBM per device.

v0:
```python
import jax
import jax.numpy as jnp
from jax import lax
from jax.sharding import PartitionSpec as P

SOURCES = 8


def local(acts, grads, source_ids, basis_in, basis_out, eigvals):
    seq_count = lax.axis_size("seq")
    tok_rows = acts.shape[0]
    total_tokens = tok_rows * seq_count
    acts_full, grads_full = (
        lax.all_gather(acts, ("row", "col"), axis=1, tiled=True),
        lax.all_gather(grads, ("row", "col"), axis=1, tiled=True),
    )
    width = acts_full.shape[1]
    new_a = jnp.dot(
        acts_full,
        lax.all_gather(basis_in, "seq", axis=0, tiled=True),
        preferred_element_type=jnp.float32,
    )
    new_g = jnp.dot(
        grads_full,
        lax.all_gather(basis_out, "seq", axis=0, tiled=True),
        preferred_element_type=jnp.float32,
    )
    own_acts = new_a.astype(jnp.bfloat16)
    own_grads = new_g.astype(jnp.bfloat16)
    rotated_full = lax.all_gather(own_acts, ("row", "col"), axis=1, tiled=True)
    outer = lax.psum_scatter(
        lax.dot_general(
            rotated_full, own_grads, (((0,), (0,)), ((), ())), preferred_element_type=jnp.float32
        ).astype(jnp.bfloat16),
        "seq",
        scatter_dimension=0,
        tiled=True,
    ).astype(jnp.float32)
    precond = outer / eigvals
    precond_rounded = precond.astype(jnp.bfloat16)
    scale_score = float(total_tokens) / float(width * width)
    act_columns = lax.all_to_all(rotated_full, "seq", split_axis=1, concat_axis=0, tiled=True)
    grad_columns = lax.all_gather(own_grads, "seq", axis=0, tiled=True)
    mapped = lax.dot_general(
        grad_columns, precond_rounded, (((1,), (1,)), ((), ())), preferred_element_type=jnp.float32
    )
    partial_value = jnp.sum(mapped * act_columns.astype(jnp.float32), axis=1)
    local_sum = lax.psum_scatter(partial_value, "seq", scatter_dimension=0, tiled=True)
    summed = lax.psum(local_sum, ("row", "col"))
    scores = summed * scale_score
    onehot = (source_ids[:, None] == jnp.arange(SOURCES, dtype=jnp.int32)[None, :]).astype(
        jnp.float32
    )
    local_influence = jnp.sum(onehot * scores[:, None], axis=0)
    influence = lax.psum(local_influence, "seq") * (float(SOURCES) / float(total_tokens))
    return (precond, scores, influence)


def solution(mesh):
    in_specs = (
        P(("grp", "seq"), ("row", "col")),
        P(("grp", "seq"), ("row", "col")),
        P(("grp", "seq")),
        P("seq", ("row", "col")),
        P("seq", ("row", "col")),
        P("seq", ("row", "col")),
    )
    out_specs = (P(("grp", "seq"), ("row", "col")), P(("grp", "seq")), P("grp"))
    return jax.shard_map(local, mesh=mesh, in_specs=in_specs, out_specs=out_specs, check_vma=False)
```

profile of v0, /device:TPU:0, one launch (start us, length us, event | category | flops | bytes accessed | tf_op | source)
XLA Modules:
  0.0 602.9 jit_solution(17065203587380950930)
XLA Ops:
  7.2 0.0 all-gather.7.cloned.1.call-start
  7.2 0.7 all-gather.7.cloned.1.call-update
  7.9 0.0 all-gather.9.cloned.1.call-start
  7.9 0.7 all-gather.9.cloned.1.call-update
  8.6 0.0 all-gather.13.cloned.1.call-start
  8.7 0.7 all-gather.13.cloned.1.call-update
  9.4 0.0 all-gather.15.cloned.1.call-start
  9.4 0.5 all-gather.15.cloned.1.call-update
  10.0 0.0 all-gather.11.cloned.1.call-start
  10.0 19.0 %all-gather.7.cloned.1.call-done = bf16[128,4096]{1,0:T(8,128)(2,1)} async-done(((bf16[128,1024]{1,0:T(8,128)(2,1)}), bf16[128,4096]{1,0:T(8,128)(2,1)}) %all-gather.7.cloned.1.call-update) | async-done | bytes 1048592 | tf_op jit(solution)/shard_map/all_gather | solution.py:14
  29.0 151.2 %all-gather.9.cloned.1.call-done = bf16[4096,1024]{1,0:T(8,128)(2,1)} async-done(((bf16[1024,1024]{1,0:T(8,128)(2,1)}), bf16[4096,1024]{1,0:T(8,128)(2,1)}) %all-gather.9.cloned.1.call-update) | async-done | bytes 8388624 | tf_op jit(solution)/shard_map/all_gather | solution.py:20
  180.3 5.7 convolution_convert_fusion.2
  185.9 0.0 all-gather.11.cloned.1.call-update
  186.0 0.0 reduce-scatter.2.cloned.1.call-start
  186.0 10.8 %all-gather.13.cloned.1.call-done = bf16[128,4096]{1,0:T(8,128)(2,1)} async-done(((bf16[128,1024]{1,0:T(8,128)(2,1)}), bf16[128,4096]{1,0:T(8,128)(2,1)}) %all-gather.13.cloned.1.call-update) | async-done | bytes 1048592 | tf_op jit(solution)/shard_map/all_gather | solution.py:15
  196.8 151.1 %all-gather.15.cloned.1.call-done = bf16[4096,1024]{1,0:T(8,128)(2,1)} async-done(((bf16[1024,1024]{1,0:T(8,128)(2,1)}), bf16[4096,1024]{1,0:T(8,128)(2,1)}) %all-gather.15.cloned.1.call-update) | async-done | bytes 8388624 | tf_op jit(solution)/shard_map/all_gather | solution.py:25
  347.9 5.0 convolution_convert_fusion.1
  352.9 0.0 copy-start.1
  352.9 12.0 %all-gather.11.cloned.1.call-done = bf16[128,4096]{1,0:T(8,128)(2,1)} async-done(((bf16[128,1024]{1,0:T(8,128)(2,1)}), bf16[128,4096]{1,0:T(8,128)(2,1)}) %all-gather.11.cloned.1.call-update) | async-done | bytes 1048592 | tf_op jit(solution)/shard_map/all_gather | solution.py:30
  364.9 6.8 %convolution_convert_fusion = bf16[4096,1024]{1,0:T(8,128)(2,1)} fusion(bf16[128,4096]{1,0:T(8,128)(2,1)} %all-gather.11.cloned.1.call-done, bf16[128,1024]{1,0:T(8,128)(2,1)S(1)} %convolution_convert_fusion.1), kind=kOutput, calls=%fused_computation | convolution fusion | flops 1077936128 | bytes 9699328 | tf_op jit(solution)/shard_map/dot_general | solution.py:32
  371.7 0.0 copy-done.1
  371.7 0.0 copy-start
  371.7 0.0 reduce-scatter.2.cloned.1.call-update
  371.7 0.0 copy-start.3
  371.7 0.0 all-gather.17.cloned.1.call-start
  371.8 0.7 all-gather.17.cloned.1.call-update
  372.5 0.4 copy-done
  372.9 1.1 copy.14
  374.0 4.6 all-to-all-start
  378.6 0.0 copy-done.3
  378.6 0.6 dynamic-slice
  379.8 153.2 %reduce-scatter.2.cloned.1.call-done = bf16[1024,1024]{1,0:T(8,128)(2,1)} async-done(((bf16[4096,1024]{1,0:T(8,128)(2,1)}), bf16[1024,1024]{1,0:T(8,128)(2,1)}) %reduce-scatter.2.cloned.1.call-update) | async-done | bytes 2097168 | tf_op jit(solution)/shard_map/reduce_scatter | solution.py:31
  533.1 5.9 convert_divide_fusion
  539.0 0.0 copy-start.2
  539.0 28.1 %all-gather.17.cloned.1.call-done = bf16[512,1024]{1,0:T(8,128)(2,1)} async-done(((bf16[128,1024]{1,0:T(8,128)(2,1)}), bf16[512,1024]{1,0:T(8,128)(2,1)}) %all-gather.17.cloned.1.call-update) | async-done | bytes 1048592 | tf_op jit(solution)/shard_map/all_gather | solution.py:43
  567.1 0.0 all-to-all-done
  567.1 3.9 fusion
  571.0 10.3 %all-reduce = f32[512]{0:T(512)S(1)} all-reduce(f32[512]{0:T(512)S(1)} %fusion), channel_id=3, replica_groups=mesh['grp'=2,'seq'=4,'row'=2,'col'=2] {'seq'}, use_global_device_ids=true, to_apply=%region_2.0.clone | all-reduce | flops 512 | bytes 4096
  581.3 0.1 dynamic-slice.1
  581.3 5.6 psum.14
  587.0 0.0 copy-done.2
  587.0 0.0 copy-start.4
  587.0 0.1 select_reduce_fusion
  587.1 8.5 %psum.15 = f32[8]{0:T(128)S(1)} all-reduce(f32[8]{0:T(128)S(1)} %select_reduce_fusion), channel_id=1, replica_groups=mesh['grp'=2,'seq'=4,'row'=2,'col'=2] {'seq'}, use_global_device_ids=true, to_apply=%region_5.0 | all-reduce | flops 8 | bytes 64 | tf_op jit(solution)/shard_map/psum | solution.py:55
  595.6 0.5 broadcast_multiply_fusion
  596.1 0.0 copy-done.4
  (1 shorter events, 0.0 us)
Async XLA Ops:
  7.2 21.9 %all-gather.7.cloned.1.call-start = ((), (), s32[]{:S(2)}) async-start(), calls=%async_computation.2 | async-start | bytes 1310720 | tf_op jit(solution)/shard_map/all_gather | solution.py:14
  7.9 172.4 %all-gather.9.cloned.1.call-start = ((), (), s32[]{:S(2)}) async-start(), calls=%async_computation.3 | async-start | bytes 10485760 | tf_op jit(solution)/shard_map/all_gather | solution.py:20
  8.6 188.2 %all-gather.13.cloned.1.call-start = ((), (), s32[]{:S(2)}) async-start(), calls=%async_computation.5 | async-start | bytes 1310720 | tf_op jit(solution)/shard_map/all_gather | solution.py:15
  9.4 338.5 %all-gather.15.cloned.1.call-start = ((), (), s32[]{:S(2)}) async-start(), calls=%async_computation.6 | async-start | bytes 10485760 | tf_op jit(solution)/shard_map/all_gather | solution.py:25
  10.0 354.9 %all-gather.11.cloned.1.call-start = ((), (), s32[]{:S(2)}) async-start(), calls=%async_computation.4 | async-start | bytes 1310720 | tf_op jit(solution)/shard_map/all_gather | solution.py:30
  186.0 347.1 %reduce-scatter.2.cloned.1.call-start = ((), (), s32[]{:S(2)}) async-start(), calls=%async_computation.7 | async-start | bytes 10485760 | tf_op jit(solution)/shard_map/reduce_scatter | solution.py:31
  352.9 18.8 %copy-start.1 = (bf16[128,1024]{1,0:T(8,128)(2,1)}, bf16[128,1024]{1,0:T(8,128)(2,1)S(1)}, u32[]{:S(2)}) copy-start(bf16[128,1024]{1,0:T(8,128)(2,1)S(1)} %convolution_convert_fusion.1) | copy-start | bytes 786436
  371.7 1.2 copy-start
  371.7 6.9 %copy-start.3 = (u32[32]{0:T(128)S(1)}, u32[32]{0:T(128)}, u32[]{:S(2)}) copy-start(u32[32]{0:T(128)} %constant.9) | copy-start | bytes 388
  371.7 195.4 %all-gather.17.cloned.1.call-start = ((), (), s32[]{:S(2)}) async-start(), calls=%async_computation.8 | async-start | bytes 1310720 | tf_op jit(solution)/shard_map/all_gather | solution.py:43
  374.0 193.1 %all-to-all-start = ((bf16[128,4,1024]{2,0,1:T(8,128)(2,1)}), bf16[128,4,1024]{2,0,1:T(8,128)(2,1)S(1)}, u32[]{:S(2)}, u32[]{:S(2)}) async-start(bf16[128,4,1024]{2,0,1:T(8,128)(2,1)} %bitcast.17), calls=%async_computation.1 | async-start | bytes 2097152 | tf_op jit(solution)/shard_map/all_to_all | solution.py:42
  539.0 48.0 %copy-start.2 = (s32[128]{0:T(128)S(1)}, s32[128]{0:T(128)}, u32[]{:S(2)}) copy-start(s32[128]{0:T(128)} %param.8) | copy-start | bytes 1540
  587.0 9.1 %copy-start.4 = (f32[128]{0:T(128)}, f32[128]{0:T(128)S(1)}, u32[]{:S(2)}) copy-start(f32[128]{0:T(128)S(1)} %broadcast_multiply_fusion.1) | copy-start | bytes 1540
Sparse Core Ops, SparseCore 0:
  9.6 19.4 all-gather.6
  30.6 149.6 all-gather.8
  181.8 14.9 all-gather.12
  198.2 149.6 all-gather.14
  349.9 14.9 all-gather.10
  371.8 161.1 reduce-scatter.1
  534.6 32.4 all-gather.16
where the time goes:
time: 603 us
  waiting for transfers between devices  529 us (88%)
  blocking collectives  24.4 us (4%)
  matrix products  21.3 us (4%)
  between operations  14.8 us (2%)
  other arithmetic  6.56 us (1%)
    reduce_scatter x1, waiting for transfers between devices, local(): lax.psum_scatter(lax.dot_general(rotated_full, own_grads, (((0,), (0,)),...  153 us
    all_gather x1, waiting for transfers between devices, local(): lax.all_gather(basis_in, 'seq', axis=0, tiled=True)  151 us
    all_gather x1, waiting for transfers between devices, local(): lax.all_gather(basis_out, 'seq', axis=0, tiled=True)  151 us
    all_gather x1, waiting for transfers between devices, local(): grad_columns = lax.all_gather(own_grads, 'seq', axis=0, tiled=True)  28.1 us
    all_gather x1, waiting for transfers between devices, local(): lax.all_gather(acts, ('row', 'col'), axis=1, tiled=True)  19 us
  transfers between devices with their start and end apart: 8, of which 7 were waited for; matrix products, arithmetic and copies ran while one was open for 3% of the time, Pallas kernels for 0%

commit v1 on v0

v1 whole, which is shorter than its diff:
```python
import jax
import jax.numpy as jnp
from jax import lax
from jax.sharding import PartitionSpec as P

SOURCES = 8
PLANE = ("seq", "row", "col")


def turn(x, pairs):
    return lax.ppermute(x, PLANE, pairs)


def local(acts, grads, source_ids, basis_in, basis_out, eigvals):
    seqs, rows, cols = (lax.axis_size(name) for name in PLANE)
    s = lax.axis_index("seq")
    tok = acts.shape[0]
    total_tokens = tok * seqs
    width = acts.shape[1] * rows * cols
    u = lax.axis_index("col") * rows + lax.axis_index("row")

    def place(seq, block):
        return (seq * rows + block % rows) * cols + block // rows

    def device(seq, feature):
        return seq * rows * cols + feature

    def along(axis, size, step):
        return [(i, i ^ step) for i in range(size)]

    def plane_gather(x):
        held = [x] + [lax.ppermute(x, "row", along("row", rows, j)) for j in range(1, rows)]
        slots = list(held)
        for j in range(1, cols):
            slots += [lax.ppermute(h, "col", along("col", cols, j)) for h in held]
        return slots

    def turned(x):
        pairs = [(device(b, f), place(f, b)) for b in range(seqs) for f in range(rows * cols)]
        return plane_gather(turn(x, pairs))

    def rotate(slots, basis):
        whole = jnp.stack(slots)
        pieces = []
        for k in range(seqs):
            x = lax.dynamic_index_in_dim(whole, u ^ s ^ k, keepdims=False)
            pieces.append(jnp.dot(x, basis, preferred_element_type=jnp.float32).astype(jnp.bfloat16))
        return pieces

    def total(parts):
        out = parts[0].astype(jnp.float32)
        for part in parts[1:]:
            out = out + part.astype(jnp.float32)
        return out

    grad_slots = turned(grads)
    act_slots = turned(acts)
    ids = [source_ids] + [lax.ppermute(source_ids, "seq", along("seq", seqs, k)) for k in range(1, seqs)]

    grad_pieces = rotate(grad_slots, basis_out)
    got = [grad_pieces[0]] + [
        lax.ppermute(grad_pieces[k], "seq", along("seq", seqs, k)) for k in range(1, seqs)
    ]
    own_grads = total(got).astype(jnp.bfloat16)
    rg = [own_grads] + [lax.ppermute(own_grads, "seq", along("seq", seqs, k)) for k in range(1, seqs)]

    act_pieces = rotate(act_slots, basis_in)
    got = []
    for k in range(seqs):
        pairs = [(device(b, f), place(f, b ^ k)) for b in range(seqs) for f in range(rows * cols)]
        got.append(turn(act_pieces[k], pairs))
    own_acts = total(got).astype(jnp.bfloat16)
    whole = jnp.stack(plane_gather(own_acts))
    ra = [lax.dynamic_index_in_dim(whole, u ^ s ^ k, keepdims=False) for k in range(seqs)]

    outer = jnp.zeros(eigvals.shape, jnp.float32)
    for k in range(seqs):
        partial = lax.dot_general(
            ra[k], rg[k], (((0,), (0,)), ((), ())), preferred_element_type=jnp.float32
        )
        outer = outer + partial.astype(jnp.bfloat16).astype(jnp.float32)
    precond = outer / eigvals
    precond_rounded = precond.astype(jnp.bfloat16)
    all_ra, all_rg = jnp.concatenate(ra), jnp.concatenate(rg)
    mapped = lax.dot_general(
        all_rg, precond_rounded, (((1,), (1,)), ((), ())), preferred_element_type=jnp.float32
    )
    partial_value = jnp.sum(mapped * all_ra.astype(jnp.float32), axis=1)
    near = partial_value
    for axis, size in (("col", cols), ("row", rows)):
        near = total([near] + [lax.ppermute(near, axis, along(axis, size, j)) for j in range(1, size)])
    all_ids = jnp.concatenate(ids)
    onehot = (all_ids[:, None] == jnp.arange(SOURCES, dtype=jnp.int32)[None, :]).astype(jnp.float32)
    near_influence = jnp.sum(onehot * near[:, None], axis=0)
    blocks = near.reshape(seqs, tok)
    far = [jnp.concatenate([blocks[k], near_influence]) for k in range(seqs)]
    summed = total([far[0]] + [lax.ppermute(far[k], "seq", along("seq", seqs, k)) for k in range(1, seqs)])
    scale_score = float(total_tokens) / float(width * width)
    scores = summed[:tok] * scale_score
    influence = summed[tok:] * (scale_score * (float(SOURCES) / float(total_tokens)))
    return (precond, scores, influence)


def solution(mesh):
    in_specs = (
        P(("grp", "seq"), ("row", "col")),
        P(("grp", "seq"), ("row", "col")),
        P(("grp", "seq")),
        P("seq", ("row", "col")),
        P("seq", ("row", "col")),
        P("seq", ("row", "col")),
    )
    out_specs = (P(("grp", "seq"), ("row", "col")), P(("grp", "seq")), P("grp"))
    return jax.shard_map(local, mesh=mesh, in_specs=in_specs, out_specs=out_specs, check_vma=False)
```

time: 603 us -> 158 us (0.26)
  waiting for transfers between devices: 529 us -> 38 us
  starting transfers between devices: 4.87 us -> 107 us
  blocking collectives: 24.4 us -> 0 us
  between operations: 14.8 us -> 0.89 us
  matrix products: 21.3 us -> 8.46 us
    all_gather x6 -> x0, waiting for transfers between devices: 372 us -> none  [the longest x1 151 us: local(): lax.all_gather(basis_in, 'seq', axis=0, tiled=True)]
    reduce_scatter x1 -> x0, waiting for transfers between devices: 153 us -> none  [local(): lax.psum_scatter(lax.dot_general(rotated_full, own_grads, (((0,), (0,)),...]
    ppermute x0 -> x29, starting transfers between devices: none -> 107 us  [the longest x3 29.6 us: local(): lax.ppermute(grad_pieces[k], 'seq', along('seq', seqs, k))]
    ppermute x0 -> x29, waiting for transfers between devices: none -> 38 us  [the longest x3 16.2 us: local(): lax.ppermute(own_grads, 'seq', along('seq', seqs, k))]
    psum x2 -> x0, blocking collectives: 14.1 us -> none  [the longest x1 8.47 us: local(): lax.psum(local_influence, 'seq') * (float(SOURCES) / float(total_tokens))]
    dot_general x4 -> x13, matrix products: 21.3 us -> 8.46 us  [the longest x8 3.56 us: rotate(): jnp.dot(x, basis, preferred_element_type=jnp.float32).astype(jnp.bfloat16)]
    unnamed x1 -> x0, blocking collectives: 10.3 us -> none
  transfers between devices with their start and end apart: 8 -> 29, of which waited for: 7 -> 9; matrix products, arithmetic and copies ran while one was open for 3% -> 4% of each run, Pallas kernels for 0% -> 0%
where the time goes in v1:
time: 158 us
  starting transfers between devices  107 us (68%)
  waiting for transfers between devices  38 us (24%)
  matrix products  8.46 us (5%)
  other arithmetic  2.85 us (2%)
    ppermute x3, starting transfers between devices, local(): lax.ppermute(grad_pieces[k], 'seq', along('seq', seqs, k))  29.6 us
    ppermute x3, starting transfers between devices, plane_gather(): lax.ppermute(x, 'row', along('row', rows, j))  27 us
    ppermute x6, starting transfers between devices, plane_gather(): slots += [lax.ppermute(h, 'col', along('col', cols, j)) for h in held]  23.3 us
    ppermute x3, waiting for transfers between devices, local(): lax.ppermute(own_grads, 'seq', along('seq', seqs, k))  16.2 us
    ppermute x6, waiting for transfers between devices, turn(): return lax.ppermute(x, PLANE, pairs)  15.1 us
    ppermute x6, starting transfers between devices, turn(): return lax.ppermute(x, PLANE, pairs)  9.32 us
    ppermute x3, starting transfers between devices, local(): lax.ppermute(own_grads, 'seq', along('seq', seqs, k))  6.98 us
    ppermute x3, starting transfers between devices, local(): lax.ppermute(source_ids, 'seq', along('seq', seqs, k))  5.99 us
  transfers between devices with their start and end apart: 29, of which 9 were waited for; matrix products, arithmetic and copies ran while one was open for 4% of the time, Pallas kernels for 0%

profile of v1, /device:TPU:0, one launch (start us, length us, event | category | flops | bytes accessed | tf_op | source)
XLA Modules:
  0.0 157.8 jit_solution(2407428178331474787)
XLA Ops:
  0.6 0.0 copy-start
  0.6 1.7 %collective-permute-start.11 = (bf16[128,1024]{1,0:T(8,128)(2,1)}, bf16[128,1024]{1,0:T(8,128)(2,1)S(1)}, u32[]{:S(2)}, u32[]{:S(2)}) collective-permute-start(bf16[128,1024]{1,0:T(8,128)(2,1)} %param.7), channel_id=1, source_target_pairs={{0,0},{1,4},{2,8},{3,12},{4,2},{5,6},{6,10},{7,14},{8,1},{9,5},{10... | collective-permute-start | bytes 786440 | tf_op jit(solution)/shard_map/ppermute | solution.py:11
  2.4 1.6 %collective-permute-start = (bf16[128,1024]{1,0:T(8,128)(2,1)}, bf16[128,1024]{1,0:T(8,128)(2,1)S(1)}, u32[]{:S(2)}, u32[]{:S(2)}) collective-permute-start(bf16[128,1024]{1,0:T(8,128)(2,1)} %param.6), channel_id=1, source_target_pairs={{0,0},{1,4},{2,8},{3,12},{4,2},{5,6},{6,10},{7,14},{8,1},{9,5},{10... | collective-permute-start | bytes 786440 | tf_op jit(solution)/shard_map/ppermute | solution.py:11
  4.0 0.0 collective-permute-done.11
  4.0 11.5 %collective-permute-start.12 = (bf16[128,1024]{1,0:T(8,128)(2,1)S(1)}, bf16[128,1024]{1,0:T(8,128)(2,1)S(1)}, u32[]{:S(2)}, u32[]{:S(2)}) collective-permute-start(bf16[128,1024]{1,0:T(8,128)(2,1)S(1)} %collective-permute-done.11), channel_id=1, source_target_pairs={{0,2},{2,0},{1,3},{3,1},{4,6},{6,4},{5,7},{7,5},{8,10},{10,8},{9,1... | collective-permute-start | bytes 786440 | tf_op jit(solution)/shard_map/ppermute | solution.py:32
  15.5 0.0 collective-permute-done
  15.5 5.5 %collective-permute-start.1 = (bf16[128,1024]{1,0:T(8,128)(2,1)S(1)}, bf16[128,1024]{1,0:T(8,128)(2,1)S(1)}, u32[]{:S(2)}, u32[]{:S(2)}) collective-permute-start(bf16[128,1024]{1,0:T(8,128)(2,1)S(1)} %collective-permute-done), channel_id=1, source_target_pairs={{0,2},{2,0},{1,3},{3,1},{4,6},{6,4},{5,7},{7,5},{8,10},{10,8},{9,1... | collective-permute-start | bytes 786440 | tf_op jit(solution)/shard_map/ppermute | solution.py:32
  21.0 9.0 %collective-permute-start.13 = (bf16[128,1024]{1,0:T(8,128)(2,1)S(1)}, bf16[128,1024]{1,0:T(8,128)(2,1)S(1)}, u32[]{:S(2)}, u32[]{:S(2)}) collective-permute-start(bf16[128,1024]{1,0:T(8,128)(2,1)S(1)} %collective-permute-done.11), channel_id=1, source_target_pairs={{0,1},{1,0},{2,3},{3,2},{4,5},{5,4},{6,7},{7,6},{8,9},{9,8},{10,11... | collective-permute-start | bytes 786440 | tf_op jit(solution)/shard_map/ppermute | solution.py:35
  30.1 0.3 collective-permute-start.14
  30.3 0.3 collective-permute-start.2
  30.6 0.0 collective-permute-done.1
  30.6 4.7 %collective-permute-start.3 = (bf16[128,1024]{1,0:T(8,128)(2,1)S(1)}, bf16[128,1024]{1,0:T(8,128)(2,1)S(1)}, u32[]{:S(2)}, u32[]{:S(2)}) collective-permute-start(bf16[128,1024]{1,0:T(8,128)(2,1)S(1)} %collective-permute-done.1), channel_id=1, source_target_pairs={{0,1},{1,0},{2,3},{3,2},{4,5},{5,4},{6,7},{7,6},{8,9},{9,8},{10,11... | collective-permute-start | bytes 786440 | tf_op jit(solution)/shard_map/ppermute | solution.py:35
  35.3 0.0 collective-permute-done.14
  35.3 1.1 pad_maximum_fusion.2
  36.4 0.4 convolution_convert_fusion.2
  36.8 0.4 convolution_convert_fusion.1
  37.3 0.1 pad_maximum_fusion
  37.5 0.4 convolution_convert_fusion.6
  37.9 0.4 convolution_convert_fusion.5
  38.4 4.3 %collective-permute-start.15 = (bf16[128,1024]{1,0:T(8,128)(2,1)S(1)}, bf16[128,1024]{1,0:T(8,128)(2,1)S(1)}, u32[]{:S(2)}, u32[]{:S(2)}) collective-permute-start(bf16[128,1024]{1,0:T(8,128)(2,1)S(1)} %convolution_convert_fusion.2), channel_id=1, source_target_pairs={{0,4},{4,0},{8,12},{12,8},{1,5},{5,1},{9,13},{13,9},{2,6},{6,2},{1... | collective-permute-start | bytes 786440 | tf_op jit(solution)/shard_map/ppermute | solution.py:62
  42.6 1.8 %collective-permute-start.5 = (bf16[128,1024]{1,0:T(8,128)(2,1)S(1)}, bf16[128,1024]{1,0:T(8,128)(2,1)S(1)}, u32[]{:S(2)}, u32[]{:S(2)}) collective-permute-start(bf16[128,1024]{1,0:T(8,128)(2,1)S(1)} %convolution_convert_fusion.6), channel_id=1, source_target_pairs={{0,2},{1,6},{2,10},{3,14},{4,0},{5,4},{6,8},{7,12},{8,3},{9,7},{10... | collective-permute-start | bytes 786440 | tf_op jit(solution)/shard_map/ppermute | solution.py:11
  44.5 0.4 convolution_convert_fusion.4
  44.9 3.5 %collective-permute-start.7 = (bf16[128,1024]{1,0:T(8,128)(2,1)S(1)}, bf16[128,1024]{1,0:T(8,128)(2,1)S(1)}, u32[]{:S(2)}, u32[]{:S(2)}) collective-permute-start(bf16[128,1024]{1,0:T(8,128)(2,1)S(1)} %convolution_convert_fusion.4), channel_id=1, source_target_pairs={{0,3},{1,7},{2,11},{3,15},{4,1},{5,5},{6,9},{7,13},{8,2},{9,6},{10... | collective-permute-start | bytes 786440 | tf_op jit(solution)/shard_map/ppermute | solution.py:11
  48.4 0.4 convolution_convert_fusion.7
  48.9 0.7 collective-permute-start.4
  49.6 0.4 convolution_convert_fusion
  50.0 6.2 %collective-permute-done.5 = bf16[128,1024]{1,0:T(8,128)(2,1)S(1)} collective-permute-done((bf16[128,1024]{1,0:T(8,128)(2,1)S(1)}, bf16[128,1024]{1,0:T(8,128)(2,1)S(1)}, u32[]{:S(2)}, u32[]{:S(2)}) %collective-permute-start.5) | collective-permute-done | bytes 262176 | tf_op jit(solution)/shard_map/ppermute | solution.py:11
  56.2 25.3 %collective-permute-start.16 = (bf16[128,1024]{1,0:T(8,128)(2,1)S(1)}, bf16[128,1024]{1,0:T(8,128)(2,1)S(1)}, u32[]{:S(2)}, u32[]{:S(2)}) collective-permute-start(bf16[128,1024]{1,0:T(8,128)(2,1)S(1)} %convolution_convert_fusion.1), channel_id=1, source_target_pairs={{0,8},{4,12},{8,0},{12,4},{1,9},{5,13},{9,1},{13,5},{2,10},{6,14},... | collective-permute-start | bytes 786440 | tf_op jit(solution)/shard_map/ppermute | solution.py:62
  81.5 8.9 %collective-permute-done.6 = bf16[128,1024]{1,0:T(8,128)(2,1)S(1)} collective-permute-done((bf16[128,1024]{1,0:T(8,128)(2,1)S(1)}, bf16[128,1024]{1,0:T(8,128)(2,1)S(1)}, u32[]{:S(2)}, u32[]{:S(2)}) %collective-permute-start.6) | collective-permute-done | bytes 262176 | tf_op jit(solution)/shard_map/ppermute | solution.py:11
  90.4 0.2 add_convert_fusion.1
  90.6 9.9 %collective-permute-start.8 = (bf16[128,1024]{1,0:T(8,128)(2,1)S(1)}, bf16[128,1024]{1,0:T(8,128)(2,1)S(1)}, u32[]{:S(2)}, u32[]{:S(2)}) collective-permute-start(bf16[128,1024]{1,0:T(8,128)(2,1)S(1)} %add_convert_fusion.1), channel_id=1, source_target_pairs={{0,2},{2,0},{1,3},{3,1},{4,6},{6,4},{5,7},{7,5},{8,10},{10,8},{9,1... | collective-permute-start | bytes 786440 | tf_op jit(solution)/shard_map/ppermute | solution.py:32
  100.5 0.4 fusion.2
  101.0 4.0 %collective-permute-start.9 = (bf16[128,1024]{1,0:T(8,128)(2,1)S(1)}, bf16[128,1024]{1,0:T(8,128)(2,1)S(1)}, u32[]{:S(2)}, u32[]{:S(2)}) collective-permute-start(bf16[128,1024]{1,0:T(8,128)(2,1)S(1)} %add_convert_fusion.1), channel_id=1, source_target_pairs={{0,1},{1,0},{2,3},{3,2},{4,5},{5,4},{6,7},{7,6},{8,9},{9,8},{10,11... | collective-permute-start | bytes 786440 | tf_op jit(solution)/shard_map/ppermute | solution.py:35
  105.0 5.0 %collective-permute-start.10 = (bf16[128,1024]{1,0:T(8,128)(2,1)S(1)}, bf16[128,1024]{1,0:T(8,128)(2,1)S(1)}, u32[]{:S(2)}, u32[]{:S(2)}) collective-permute-start(bf16[128,1024]{1,0:T(8,128)(2,1)S(1)} %collective-permute-done.8), channel_id=1, source_target_pairs={{0,1},{1,0},{2,3},{3,2},{4,5},{5,4},{6,7},{7,6},{8,9},{9,8},{10,11... | collective-permute-start | bytes 786440 | tf_op jit(solution)/shard_map/ppermute | solution.py:35
  110.0 0.0 collective-permute-done.16
  110.1 0.1 add_convert_fusion
  110.2 4.5 %collective-permute-start.18 = (bf16[128,1024]{1,0:T(8,128)(2,1)S(1)}, bf16[128,1024]{1,0:T(8,128)(2,1)S(1)}, u32[]{:S(2)}, u32[]{:S(2)}) collective-permute-start(bf16[128,1024]{1,0:T(8,128)(2,1)S(1)} %add_convert_fusion), channel_id=1, source_target_pairs={{0,4},{4,0},{8,12},{12,8},{1,5},{5,1},{9,13},{13,9},{2,6},{6,2},{1... | collective-permute-start | bytes 786440 | tf_op jit(solution)/shard_map/ppermute | solution.py:65
  114.8 2.4 %collective-permute-start.20 = (bf16[128,1024]{1,0:T(8,128)(2,1)S(1)}, bf16[128,1024]{1,0:T(8,128)(2,1)S(1)}, u32[]{:S(2)}, u32[]{:S(2)}) collective-permute-start(bf16[128,1024]{1,0:T(8,128)(2,1)S(1)} %add_convert_fusion), channel_id=1, source_target_pairs={{0,12},{4,8},{8,4},{12,0},{1,13},{5,9},{9,5},{13,1},{2,14},{6,10},... | collective-permute-start | bytes 786440 | tf_op jit(solution)/shard_map/ppermute | solution.py:65
  117.2 0.1 pad_maximum_fusion.1
  117.3 0.1 dynamic-slice_bitcast_fusion
  117.4 0.7 fusion.41
  118.2 5.3 %collective-permute-done.18 = bf16[128,1024]{1,0:T(8,128)(2,1)S(1)} collective-permute-done((bf16[128,1024]{1,0:T(8,128)(2,1)S(1)}, bf16[128,1024]{1,0:T(8,128)(2,1)S(1)}, u32[]{:S(2)}, u32[]{:S(2)}) %collective-permute-start.18) | collective-permute-done | bytes 262176 | tf_op jit(solution)/shard_map/ppermute | solution.py:65
  123.4 0.7 fusion.42
  124.1 11.0 %collective-permute-done.19 = bf16[128,1024]{1,0:T(8,128)(2,1)S(1)} collective-permute-done((bf16[128,1024]{1,0:T(8,128)(2,1)S(1)}, bf16[128,1024]{1,0:T(8,128)(2,1)S(1)}, u32[]{:S(2)}, u32[]{:S(2)}) %collective-permute-start.19) | collective-permute-done | bytes 262176 | tf_op jit(solution)/shard_map/ppermute | solution.py:65
  135.1 0.7 fusion.43
  135.9 1.3 add_divide_fusion
  137.2 0.0 copy-start.4
  137.2 0.0 copy-start.2
  137.2 1.4 multiply_reduce_fusion
  138.6 0.6 copy-done.4
  139.2 3.6 %collective-permute-start.23 = (s32[128]{0:T(128)S(1)}, s32[128]{0:T(128)S(1)}, u32[]{:S(2)}, u32[]{:S(2)}) collective-permute-start(s32[128]{0:T(128)S(1)} %copy-done.2), channel_id=1, source_target_pairs={{0,4},{4,0},{8,12},{12,8},{1,5},{5,1},{9,13},{13,9},{2,6},{6,2},{1... | collective-permute-start | bytes 1544 | tf_op jit(solution)/shard_map/ppermute | solution.py:58
  142.8 2.4 %collective-permute-start.25 = (s32[128]{0:T(128)S(1)}, s32[128]{0:T(128)S(1)}, u32[]{:S(2)}, u32[]{:S(2)}) collective-permute-start(s32[128]{0:T(128)S(1)} %copy-done.2), channel_id=1, source_target_pairs={{0,12},{4,8},{8,4},{12,0},{1,13},{5,9},{9,5},{13,1},{2,14},{6,10},... | collective-permute-start | bytes 1544 | tf_op jit(solution)/shard_map/ppermute | solution.py:58
  145.2 0.2 collective-permute-start.22
  145.5 1.8 %collective-permute-done.24 = s32[128]{0:T(128)S(1)} collective-permute-done((s32[128]{0:T(128)S(1)}, s32[128]{0:T(128)S(1)}, u32[]{:S(2)}, u32[]{:S(2)}) %collective-permute-start.24) | collective-permute-done | bytes 544 | tf_op jit(solution)/shard_map/ppermute | solution.py:58
  147.2 0.9 collective-permute-done.25
  148.1 0.7 collective-permute-done.22
  148.8 0.1 select_reduce_fusion
  149.0 1.1 collective-permute-start.26
  150.1 1.3 collective-permute-start.27
  151.4 2.0 %collective-permute-start.28 = (f32[136]{0:T(256)S(1)}, f32[136]{0:T(256)S(1)}, u32[]{:S(2)}, u32[]{:S(2)}) collective-permute-start(f32[136]{0:T(256)S(1)} %get-tuple-element.13), channel_id=1, source_target_pairs={{0,12},{4,8},{8,4},{12,0},{1,13},{5,9},{9,5},{13,1},{2,14},{6,10},... | collective-permute-start | bytes 1640 | tf_op jit(solution)/shard_map/ppermute | solution.py:97
  153.4 1.1 collective-permute-done.27
  154.5 2.2 %collective-permute-done.28 = f32[136]{0:T(256)S(1)} collective-permute-done((f32[136]{0:T(256)S(1)}, f32[136]{0:T(256)S(1)}, u32[]{:S(2)}, u32[]{:S(2)}) %collective-permute-start.28) | collective-permute-done | bytes 576 | tf_op jit(solution)/shard_map/ppermute | solution.py:97
  156.7 0.5 slice_multiply_fusion
  157.2 0.5 slice_multiply_fusion.1
  (32 shorter events, 0.1 us)
Async XLA Ops:
  0.6 36.8 %copy-start = (bf16[1024,1024]{1,0:T(8,128)(2,1)S(1)}, bf16[1024,1024]{1,0:T(8,128)(2,1)}, u32[]{:S(2)}) copy-start(bf16[1024,1024]{1,0:T(8,128)(2,1)} %param.9) | copy-start | bytes 6291460
  0.6 3.3 %collective-permute-start.11 = (bf16[128,1024]{1,0:T(8,128)(2,1)}, bf16[128,1024]{1,0:T(8,128)(2,1)S(1)}, u32[]{:S(2)}, u32[]{:S(2)}) collective-permute-start(bf16[128,1024]{1,0:T(8,128)(2,1)} %param.7), channel_id=1, source_target_pairs={{0,0},{1,4},{2,8},{3,12},{4,2},{5,6},{6,10},{7,14},{8,1},{9,5},{10... | collective-permute-start | bytes 786440 | tf_op jit(solution)/shard_map/ppermute | solution.py:11
  2.4 13.1 %collective-permute-start = (bf16[128,1024]{1,0:T(8,128)(2,1)}, bf16[128,1024]{1,0:T(8,128)(2,1)S(1)}, u32[]{:S(2)}, u32[]{:S(2)}) collective-permute-start(bf16[128,1024]{1,0:T(8,128)(2,1)} %param.6), channel_id=1, source_target_pairs={{0,0},{1,4},{2,8},{3,12},{4,2},{5,6},{6,10},{7,14},{8,1},{9,5},{10... | collective-permute-start | bytes 786440 | tf_op jit(solution)/shard_map/ppermute | solution.py:11
  4.0 26.1 %collective-permute-start.12 = (bf16[128,1024]{1,0:T(8,128)(2,1)S(1)}, bf16[128,1024]{1,0:T(8,128)(2,1)S(1)}, u32[]{:S(2)}, u32[]{:S(2)}) collective-permute-start(bf16[128,1024]{1,0:T(8,128)(2,1)S(1)} %collective-permute-done.11), channel_id=1, source_target_pairs={{0,2},{2,0},{1,3},{3,1},{4,6},{6,4},{5,7},{7,5},{8,10},{10,8},{9,1... | collective-permute-start | bytes 786440 | tf_op jit(solution)/shard_map/ppermute | solution.py:32
  15.5 15.1 %collective-permute-start.1 = (bf16[128,1024]{1,0:T(8,128)(2,1)S(1)}, bf16[128,1024]{1,0:T(8,128)(2,1)S(1)}, u32[]{:S(2)}, u32[]{:S(2)}) collective-permute-start(bf16[128,1024]{1,0:T(8,128)(2,1)S(1)} %collective-permute-done), channel_id=1, source_target_pairs={{0,2},{2,0},{1,3},{3,1},{4,6},{6,4},{5,7},{7,5},{8,10},{10,8},{9,1... | collective-permute-start | bytes 786440 | tf_op jit(solution)/shard_map/ppermute | solution.py:32
  21.0 14.3 %collective-permute-start.13 = (bf16[128,1024]{1,0:T(8,128)(2,1)S(1)}, bf16[128,1024]{1,0:T(8,128)(2,1)S(1)}, u32[]{:S(2)}, u32[]{:S(2)}) collective-permute-start(bf16[128,1024]{1,0:T(8,128)(2,1)S(1)} %collective-permute-done.11), channel_id=1, source_target_pairs={{0,1},{1,0},{2,3},{3,2},{4,5},{5,4},{6,7},{7,6},{8,9},{9,8},{10,11... | collective-permute-start | bytes 786440 | tf_op jit(solution)/shard_map/ppermute | solution.py:35
  30.1 5.2 %collective-permute-start.14 = (bf16[128,1024]{1,0:T(8,128)(2,1)S(1)}, bf16[128,1024]{1,0:T(8,128)(2,1)}, u32[]{:S(2)}, u32[]{:S(2)}) collective-permute-start(bf16[128,1024]{1,0:T(8,128)(2,1)S(1)} %collective-permute-done.12), channel_id=1, source_target_pairs={{0,1},{1,0},{2,3},{3,2},{4,5},{5,4},{6,7},{7,6},{8,9},{9,8},{10,11... | collective-permute-start | bytes 786440 | tf_op jit(solution)/shard_map/ppermute | solution.py:35
  30.3 6.1 %copy-start.1 = (bf16[1024,1024]{1,0:T(8,128)(2,1)S(1)}, bf16[1024,1024]{1,0:T(8,128)(2,1)}, u32[]{:S(2)}) copy-start(bf16[1024,1024]{1,0:T(8,128)(2,1)} %param.10) | copy-start | bytes 6291460
  30.3 7.0 %collective-permute-start.2 = (bf16[128,1024]{1,0:T(8,128)(2,1)S(1)}, bf16[128,1024]{1,0:T(8,128)(2,1)S(1)}, u32[]{:S(2)}, u32[]{:S(2)}) collective-permute-start(bf16[128,1024]{1,0:T(8,128)(2,1)S(1)} %collective-permute-done), channel_id=1, source_target_pairs={{0,1},{1,0},{2,3},{3,2},{4,5},{5,4},{6,7},{7,6},{8,9},{9,8},{10,11... | collective-permute-start | bytes 786440 | tf_op jit(solution)/shard_map/ppermute | solution.py:35
  30.6 6.7 %collective-permute-start.3 = (bf16[128,1024]{1,0:T(8,128)(2,1)S(1)}, bf16[128,1024]{1,0:T(8,128)(2,1)S(1)}, u32[]{:S(2)}, u32[]{:S(2)}) collective-permute-start(bf16[128,1024]{1,0:T(8,128)(2,1)S(1)} %collective-permute-done.1), channel_id=1, source_target_pairs={{0,1},{1,0},{2,3},{3,2},{4,5},{5,4},{6,7},{7,6},{8,9},{9,8},{10,11... | collective-permute-start | bytes 786440 | tf_op jit(solution)/shard_map/ppermute | solution.py:35
  38.4 71.6 %collective-permute-start.15 = (bf16[128,1024]{1,0:T(8,128)(2,1)S(1)}, bf16[128,1024]{1,0:T(8,128)(2,1)S(1)}, u32[]{:S(2)}, u32[]{:S(2)}) collective-permute-start(bf16[128,1024]{1,0:T(8,128)(2,1)S(1)} %convolution_convert_fusion.2), channel_id=1, source_target_pairs={{0,4},{4,0},{8,12},{12,8},{1,5},{5,1},{9,13},{13,9},{2,6},{6,2},{1... | collective-permute-start | bytes 786440 | tf_op jit(solution)/shard_map/ppermute | solution.py:62
  42.6 13.6 %collective-permute-start.5 = (bf16[128,1024]{1,0:T(8,128)(2,1)S(1)}, bf16[128,1024]{1,0:T(8,128)(2,1)S(1)}, u32[]{:S(2)}, u32[]{:S(2)}) collective-permute-start(bf16[128,1024]{1,0:T(8,128)(2,1)S(1)} %convolution_convert_fusion.6), channel_id=1, source_target_pairs={{0,2},{1,6},{2,10},{3,14},{4,0},{5,4},{6,8},{7,12},{8,3},{9,7},{10... | collective-permute-start | bytes 786440 | tf_op jit(solution)/shard_map/ppermute | solution.py:11
  44.5 45.9 %collective-permute-start.6 = (bf16[128,1024]{1,0:T(8,128)(2,1)S(1)}, bf16[128,1024]{1,0:T(8,128)(2,1)S(1)}, u32[]{:S(2)}, u32[]{:S(2)}) collective-permute-start(bf16[128,1024]{1,0:T(8,128)(2,1)S(1)} %convolution_convert_fusion.5), channel_id=1, source_target_pairs={{0,1},{1,5},{2,9},{3,13},{4,3},{5,7},{6,11},{7,15},{8,0},{9,4},{10... | collective-permute-start | bytes 786440 | tf_op jit(solution)/shard_map/ppermute | solution.py:11
  44.9 45.5 %collective-permute-start.7 = (bf16[128,1024]{1,0:T(8,128)(2,1)S(1)}, bf16[128,1024]{1,0:T(8,128)(2,1)S(1)}, u32[]{:S(2)}, u32[]{:S(2)}) collective-permute-start(bf16[128,1024]{1,0:T(8,128)(2,1)S(1)} %convolution_convert_fusion.4), channel_id=1, source_target_pairs={{0,3},{1,7},{2,11},{3,15},{4,1},{5,5},{6,9},{7,13},{8,2},{9,6},{10... | collective-permute-start | bytes 786440 | tf_op jit(solution)/shard_map/ppermute | solution.py:11
  48.9 41.5 %collective-permute-start.4 = (bf16[128,1024]{1,0:T(8,128)(2,1)S(1)}, bf16[128,1024]{1,0:T(8,128)(2,1)S(1)}, u32[]{:S(2)}, u32[]{:S(2)}) collective-permute-start(bf16[128,1024]{1,0:T(8,128)(2,1)S(1)} %convolution_convert_fusion.7), channel_id=1, source_target_pairs={{0,0},{1,4},{2,8},{3,12},{4,2},{5,6},{6,10},{7,14},{8,1},{9,5},{10... | collective-permute-start | bytes 786440 | tf_op jit(solution)/shard_map/ppermute | solution.py:11
  56.2 53.9 %collective-permute-start.16 = (bf16[128,1024]{1,0:T(8,128)(2,1)S(1)}, bf16[128,1024]{1,0:T(8,128)(2,1)S(1)}, u32[]{:S(2)}, u32[]{:S(2)}) collective-permute-start(bf16[128,1024]{1,0:T(8,128)(2,1)S(1)} %convolution_convert_fusion.1), channel_id=1, source_target_pairs={{0,8},{4,12},{8,0},{12,4},{1,9},{5,13},{9,1},{13,5},{2,10},{6,14},... | collective-permute-start | bytes 786440 | tf_op jit(solution)/shard_map/ppermute | solution.py:62
  90.4 19.7 %collective-permute-start.17 = (bf16[128,1024]{1,0:T(8,128)(2,1)S(1)}, bf16[128,1024]{1,0:T(8,128)(2,1)S(1)}, u32[]{:S(2)}, u32[]{:S(2)}) collective-permute-start(bf16[128,1024]{1,0:T(8,128)(2,1)S(1)} %convolution_convert_fusion), channel_id=1, source_target_pairs={{0,12},{4,8},{8,4},{12,0},{1,13},{5,9},{9,5},{13,1},{2,14},{6,10},... | collective-permute-start | bytes 786440 | tf_op jit(solution)/shard_map/ppermute | solution.py:62
  90.6 14.4 %collective-permute-start.8 = (bf16[128,1024]{1,0:T(8,128)(2,1)S(1)}, bf16[128,1024]{1,0:T(8,128)(2,1)S(1)}, u32[]{:S(2)}, u32[]{:S(2)}) collective-permute-start(bf16[128,1024]{1,0:T(8,128)(2,1)S(1)} %add_convert_fusion.1), channel_id=1, source_target_pairs={{0,2},{2,0},{1,3},{3,1},{4,6},{6,4},{5,7},{7,5},{8,10},{10,8},{9,1... | collective-permute-start | bytes 786440 | tf_op jit(solution)/shard_map/ppermute | solution.py:32
  101.0 16.2 %collective-permute-start.9 = (bf16[128,1024]{1,0:T(8,128)(2,1)S(1)}, bf16[128,1024]{1,0:T(8,128)(2,1)S(1)}, u32[]{:S(2)}, u32[]{:S(2)}) collective-permute-start(bf16[128,1024]{1,0:T(8,128)(2,1)S(1)} %add_convert_fusion.1), channel_id=1, source_target_pairs={{0,1},{1,0},{2,3},{3,2},{4,5},{5,4},{6,7},{7,6},{8,9},{9,8},{10,11... | collective-permute-start | bytes 786440 | tf_op jit(solution)/shard_map/ppermute | solution.py:35
  105.0 12.2 %collective-permute-start.10 = (bf16[128,1024]{1,0:T(8,128)(2,1)S(1)}, bf16[128,1024]{1,0:T(8,128)(2,1)S(1)}, u32[]{:S(2)}, u32[]{:S(2)}) collective-permute-start(bf16[128,1024]{1,0:T(8,128)(2,1)S(1)} %collective-permute-done.8), channel_id=1, source_target_pairs={{0,1},{1,0},{2,3},{3,2},{4,5},{5,4},{6,7},{7,6},{8,9},{9,8},{10,11... | collective-permute-start | bytes 786440 | tf_op jit(solution)/shard_map/ppermute | solution.py:35
  110.2 13.2 %collective-permute-start.18 = (bf16[128,1024]{1,0:T(8,128)(2,1)S(1)}, bf16[128,1024]{1,0:T(8,128)(2,1)S(1)}, u32[]{:S(2)}, u32[]{:S(2)}) collective-permute-start(bf16[128,1024]{1,0:T(8,128)(2,1)S(1)} %add_convert_fusion), channel_id=1, source_target_pairs={{0,4},{4,0},{8,12},{12,8},{1,5},{5,1},{9,13},{13,9},{2,6},{6,2},{1... | collective-permute-start | bytes 786440 | tf_op jit(solution)/shard_map/ppermute | solution.py:65
  114.8 20.4 %collective-permute-start.19 = (bf16[128,1024]{1,0:T(8,128)(2,1)S(1)}, bf16[128,1024]{1,0:T(8,128)(2,1)S(1)}, u32[]{:S(2)}, u32[]{:S(2)}) collective-permute-start(bf16[128,1024]{1,0:T(8,128)(2,1)S(1)} %add_convert_fusion), channel_id=1, source_target_pairs={{0,8},{4,12},{8,0},{12,4},{1,9},{5,13},{9,1},{13,5},{2,10},{6,14},... | collective-permute-start | bytes 786440 | tf_op jit(solution)/shard_map/ppermute | solution.py:65
  114.8 21.1 %collective-permute-start.20 = (bf16[128,1024]{1,0:T(8,128)(2,1)S(1)}, bf16[128,1024]{1,0:T(8,128)(2,1)S(1)}, u32[]{:S(2)}, u32[]{:S(2)}) collective-permute-start(bf16[128,1024]{1,0:T(8,128)(2,1)S(1)} %add_convert_fusion), channel_id=1, source_target_pairs={{0,12},{4,8},{8,4},{12,0},{1,13},{5,9},{9,5},{13,1},{2,14},{6,10},... | collective-permute-start | bytes 786440 | tf_op jit(solution)/shard_map/ppermute | solution.py:65
  123.4 12.4 %copy-start.3 = (f32[1024,1024]{1,0:T(8,128)S(1)}, f32[1024,1024]{1,0:T(8,128)}, u32[]{:S(2)}) copy-start(f32[1024,1024]{1,0:T(8,128)} %param.11) | copy-start | bytes 12582916
  137.2 2.0 %copy-start.4 = (f32[1024,1024]{1,0:T(8,128)}, f32[1024,1024]{1,0:T(8,128)S(1)}, u32[]{:S(2)}) copy-start(f32[1024,1024]{1,0:T(8,128)S(1)} %add_divide_fusion) | copy-start | bytes 12582916
  137.2 2.0 %copy-start.2 = (s32[128]{0:T(128)S(1)}, s32[128]{0:T(128)}, u32[]{:S(2)}) copy-start(s32[128]{0:T(128)} %param.8) | copy-start | bytes 1540
  139.2 6.0 %collective-permute-start.21 = (f32[512]{0:T(512)S(1)}, f32[512]{0:T(512)S(1)}, u32[]{:S(2)}, u32[]{:S(2)}) collective-permute-start(f32[512]{0:T(512)S(1)} %multiply_reduce_fusion), channel_id=1, source_target_pairs={{0,1},{1,0},{2,3},{3,2},{4,5},{5,4},{6,7},{7,6},{8,9},{9,8},{10,11... | collective-permute-start | bytes 6152 | tf_op jit(solution)/shard_map/ppermute | solution.py:91
  139.2 6.2 %collective-permute-start.23 = (s32[128]{0:T(128)S(1)}, s32[128]{0:T(128)S(1)}, u32[]{:S(2)}, u32[]{:S(2)}) collective-permute-start(s32[128]{0:T(128)S(1)} %copy-done.2), channel_id=1, source_target_pairs={{0,4},{4,0},{8,12},{12,8},{1,5},{5,1},{9,13},{13,9},{2,6},{6,2},{1... | collective-permute-start | bytes 1544 | tf_op jit(solution)/shard_map/ppermute | solution.py:58
  142.8 4.4 %collective-permute-start.24 = (s32[128]{0:T(128)S(1)}, s32[128]{0:T(128)S(1)}, u32[]{:S(2)}, u32[]{:S(2)}) collective-permute-start(s32[128]{0:T(128)S(1)} %copy-done.2), channel_id=1, source_target_pairs={{0,8},{4,12},{8,0},{12,4},{1,9},{5,13},{9,1},{13,5},{2,10},{6,14},... | collective-permute-start | bytes 1544 | tf_op jit(solution)/shard_map/ppermute | solution.py:58
  142.8 5.3 %collective-permute-start.25 = (s32[128]{0:T(128)S(1)}, s32[128]{0:T(128)S(1)}, u32[]{:S(2)}, u32[]{:S(2)}) collective-permute-start(s32[128]{0:T(128)S(1)} %copy-done.2), channel_id=1, source_target_pairs={{0,12},{4,8},{8,4},{12,0},{1,13},{5,9},{9,5},{13,1},{2,14},{6,10},... | collective-permute-start | bytes 1544 | tf_op jit(solution)/shard_map/ppermute | solution.py:58
  145.2 3.6 %collective-permute-start.22 = (f32[512]{0:T(512)S(1)}, f32[512]{0:T(512)S(1)}, u32[]{:S(2)}, u32[]{:S(2)}) collective-permute-start(f32[512]{0:T(512)S(1)} %add.80), channel_id=1, source_target_pairs={{0,2},{2,0},{1,3},{3,1},{4,6},{6,4},{5,7},{7,5},{8,10},{10,8},{9,1... | collective-permute-start | bytes 6152 | tf_op jit(solution)/shard_map/ppermute | solution.py:91
  149.0 4.5 %collective-permute-start.26 = (f32[136]{0:T(256)S(1)}, f32[136]{0:T(256)S(1)}, u32[]{:S(2)}, u32[]{:S(2)}) collective-permute-start(f32[136]{0:T(256)S(1)} %get-tuple-element.11), channel_id=1, source_target_pairs={{0,4},{4,0},{8,12},{12,8},{1,5},{5,1},{9,13},{13,9},{2,6},{6,2},{1... | collective-permute-start | bytes 1640 | tf_op jit(solution)/shard_map/ppermute | solution.py:97
  150.1 4.5 %collective-permute-start.27 = (f32[136]{0:T(256)S(1)}, f32[136]{0:T(256)S(1)}, u32[]{:S(2)}, u32[]{:S(2)}) collective-permute-start(f32[136]{0:T(256)S(1)} %get-tuple-element.12), channel_id=1, source_target_pairs={{0,8},{4,12},{8,0},{12,4},{1,9},{5,13},{9,1},{13,5},{2,10},{6,14},... | collective-permute-start | bytes 1640 | tf_op jit(solution)/shard_map/ppermute | solution.py:97
  151.4 5.4 %collective-permute-start.28 = (f32[136]{0:T(256)S(1)}, f32[136]{0:T(256)S(1)}, u32[]{:S(2)}, u32[]{:S(2)}) collective-permute-start(f32[136]{0:T(256)S(1)} %get-tuple-element.13), channel_id=1, source_target_pairs={{0,12},{4,8},{8,4},{12,0},{1,13},{5,9},{9,5},{13,1},{2,14},{6,10},... | collective-permute-start | bytes 1640 | tf_op jit(solution)/shard_map/ppermute | solution.py:97

commit v2 on v1

--- a/solution.py
+++ b/solution.py
@@ -1,6 +1,8 @@
 import jax
 import jax.numpy as jnp
 from jax import lax
+from jax.experimental import pallas as pl
+from jax.experimental.pallas import tpu as pltpu
 from jax.sharding import PartitionSpec as P
 
 SOURCES = 8
@@ -11,7 +13,7 @@
     return lax.ppermute(x, PLANE, pairs)
 
 
-def local(acts, grads, source_ids, basis_in, basis_out, eigvals):
+def local_any(acts, grads, source_ids, basis_in, basis_out, eigvals):
     seqs, rows, cols = (lax.axis_size(name) for name in PLANE)
     s = lax.axis_index("seq")
     tok = acts.shape[0]
@@ -101,6 +103,221 @@
     return (precond, scores, influence)
 
 
+def swap(x, axis, step=1):
+    return lax.ppermute(x, axis, [(i, i ^ step) for i in range(lax.axis_size(axis))])
+
+
+def added(a, b):
+    return a.astype(jnp.float32) + b.astype(jnp.float32)
+
+
+def rotate_kernel(order, x0, x1, x2, x3, basis, send, keep, rows):
+    step = pl.program_id(0)
+    half = pl.num_programs(0) // 2
+    tok = x0.shape[0]
+
+    @pl.when(step == 0)
+    def _():
+        for j, x in enumerate((x0, x1, x2, x3)):
+            rows[pl.ds(j * tok, tok), :] = x[...]
+
+    block = jnp.dot(rows[...], basis[...], preferred_element_type=jnp.float32)
+
+    @pl.when(step < half)
+    def _():
+        send[...] = block.astype(jnp.bfloat16)
+
+    @pl.when(step >= half)
+    def _():
+        keep[...] = block
+
+
+def rotate(slots, basis, order):
+    tok, depth = slots[0].shape
+    blocks = order.shape[0]
+    step = basis.shape[1] // blocks
+    half = blocks // 2
+    rows = tok * len(slots)
+    whole = pl.BlockSpec((tok, depth), lambda i, order: (0, 0))
+    return pl.pallas_call(
+        rotate_kernel,
+        out_shape=(
+            jax.ShapeDtypeStruct((rows, half * step), jnp.bfloat16),
+            jax.ShapeDtypeStruct((rows, half * step), jnp.float32),
+        ),
+        grid_spec=pltpu.PrefetchScalarGridSpec(
+            num_scalar_prefetch=1,
+            grid=(blocks,),
+            in_specs=[whole] * 4 + [pl.BlockSpec((depth, step), lambda i, order: (0, order[i]))],
+            out_specs=(
+                pl.BlockSpec((rows, step), lambda i, order: (0, jnp.minimum(i, half - 1))),
+                pl.BlockSpec((rows, step), lambda i, order: (0, jnp.maximum(i - half, 0))),
+            ),
+            scratch_shapes=[pltpu.VMEM((rows, depth), jnp.bfloat16)],
+        ),
+        compiler_params=pltpu.CompilerParams(vmem_limit_bytes=24 * 2**20),
+        cost_estimate=pl.CostEstimate(
+            flops=2 * rows * depth * basis.shape[1], bytes_accessed=2 * depth * basis.shape[1], transcendentals=0
+        ),
+        name="rotate",
+    )(order, *slots, basis)
+
+
+def outer_kernel(place, a0, a1, a2, a3, g, eig, *refs):
+    precond, score = refs[-2:]
+    step = pl.program_id(0)
+    u = place[0]
+    tok = g.shape[0] // 4
+    piece = a0.shape[1]
+    total = None
+    for m, a in enumerate((a0, a1, a2, a3)):
+        outer = None
+        for j in range(4):
+            partial = lax.dot_general(
+                a[pl.ds((j ^ m) * tok, tok), :],
+                g[pl.ds(j * tok, tok), :],
+                (((0,), (0,)), ((), ())),
+                preferred_element_type=jnp.float32,
+            )
+            partial = partial.astype(jnp.bfloat16).astype(jnp.float32)
+            outer = partial if outer is None else outer + partial
+        where = pl.ds(pl.multiple_of((u ^ m) * piece, piece), piece)
+        ratio = outer / eig[where, :]
+        precond[where, :] = ratio
+        mapped = jnp.dot(a[...], ratio.astype(jnp.bfloat16), preferred_element_type=jnp.float32)
+        blocks = [mapped[j * tok : (j + 1) * tok] for j in range(4)]
+        mapped = jnp.concatenate([blocks[j ^ m] for j in range(4)])
+        total = mapped if total is None else total + mapped
+    value = total * g[...].astype(jnp.float32)
+    lanes = score.shape[1]
+    folded = value[:, :lanes]
+    for i in range(1, value.shape[1] // lanes):
+        folded = folded + value[:, i * lanes : (i + 1) * lanes]
+
+    @pl.when(step == 0)
+    def _():
+        score[...] = folded
+
+    @pl.when(step > 0)
+    def _():
+        score[...] += folded
+
+
+def outer_half(place, acts, grads, eigvals, done=None):
+    tokens, piece = acts[0].shape
+    width = eigvals.shape[0]
+    cols = 256
+    steps = grads.shape[1] // cols
+    here = lambda i, place: (0, place[1] * steps + i)
+    whole = pl.BlockSpec((tokens, piece), lambda i, place: (0, 0))
+    in_specs = [whole] * 4 + [
+        pl.BlockSpec((tokens, cols), lambda i, place: (0, i)),
+        pl.BlockSpec((width, cols), here),
+    ]
+    args = [place, *acts, grads, eigvals]
+    aliases = {}
+    if done is not None:
+        in_specs.append(pl.BlockSpec(memory_space=pl.ANY))
+        aliases = {len(args): 0}
+        args.append(done)
+    return pl.pallas_call(
+        outer_kernel,
+        out_shape=(
+            jax.ShapeDtypeStruct(eigvals.shape, jnp.float32),
+            jax.ShapeDtypeStruct((tokens, 128), jnp.float32),
+        ),
+        grid_spec=pltpu.PrefetchScalarGridSpec(
+            num_scalar_prefetch=1,
+            grid=(steps,),
+            in_specs=in_specs,
+            out_specs=(
+                pl.BlockSpec((width, cols), here),
+                pl.BlockSpec((tokens, 128), lambda i, place: (0, 0)),
+            ),
+        ),
+        input_output_aliases=aliases,
+        compiler_params=pltpu.CompilerParams(vmem_limit_bytes=24 * 2**20),
+        cost_estimate=pl.CostEstimate(
+            flops=4 * tokens * width * grads.shape[1], bytes_accessed=8 * width * grads.shape[1], transcendentals=0
+        ),
+        name="outer_half",
+    )(*args)
+
+
+def local_pairs(acts, grads, source_ids, basis_in, basis_out, eigvals):
+    seqs, rows, cols = (lax.axis_size(name) for name in PLANE)
+    y = lax.axis_index("grp")
+    s = lax.axis_index("seq")
+    x = lax.axis_index("row")
+    k = lax.axis_index("col")
+    c = x * cols + k
+    u = k * rows + x
+    low = s % 2
+    tok = acts.shape[0]
+    total_tokens = tok * seqs
+    block = acts.shape[1]
+    width = block * rows * cols
+    half, piece = block // 2, block // 4
+
+    def turned(x, flip):
+        pairs = []
+        for b in range(seqs):
+            for f in range(rows * cols):
+                pairs.append((b * rows * cols + f, ((f ^ flip) * rows + b % rows) * cols + b // rows))
+        return lax.ppermute(x, PLANE, pairs)
+
+    def plane_gather(x):
+        near = swap(x, "row")
+        return [x, near, swap(x, "col"), swap(near, "col")]
+
+    grads_here = turned(grads, 0)
+    acts_here = turned(swap(acts, "row"), cols)
+
+    own = lax.dynamic_slice_in_dim(basis_in, k * half, half, axis=1)
+    other = swap(lax.dynamic_slice_in_dim(basis_in, (1 - k) * half, half, axis=1), "col")
+    both = jnp.stack([own, other])
+    mine = lax.dynamic_slice_in_dim(both, x * piece, piece, axis=2)
+    theirs = lax.dynamic_slice(both, (0, y * half, (1 - x) * piece), (2, half, piece))
+    first = swap(theirs, "row")
+    second = swap(first, "grp")
+    upper = jnp.where(y == 0, first, second)
+    lower = jnp.where(y == 0, second, first)
+    far = jnp.concatenate([upper, lower], axis=1)
+    tiles = jnp.concatenate([mine[0], mine[1], far[0], far[1]], axis=1)
+
+    ids = jnp.stack([source_ids] + [swap(source_ids, "seq", j) for j in range(1, seqs)])
+    slot_ids = jnp.stack([lax.dynamic_index_in_dim(ids, u ^ s ^ j, keepdims=False) for j in range(seqs)])
+    onehot = (slot_ids.reshape(-1, 1) == jnp.arange(SOURCES, dtype=jnp.int32)[None, :]).astype(jnp.float32)
+
+    order_g = jnp.stack([2 - 2 * low, 3 - 2 * low, 2 * low, 2 * low + 1]).astype(jnp.int32)
+    send_g, keep_g = rotate(plane_gather(grads_here), basis_out, order_g)
+    pair_g = added(keep_g, swap(send_g, "seq", 1)).astype(jnp.bfloat16)
+    near_g = added(pair_g, swap(pair_g, "seq", 2)).astype(jnp.bfloat16)
+    far_g = swap(near_g, "seq", 1)
+
+    order_a = (jnp.array([1, 3, 0, 2], jnp.int32) ^ (c ^ s)).astype(jnp.int32)
+    send_a, keep_a = rotate(plane_gather(acts_here), tiles, order_a)
+    got_a = swap(send_a, "seq", 1)
+    cross = swap(added(keep_a[:, piece:], got_a[:, piece:]).astype(jnp.bfloat16), "seq", 2)
+    own_a = (added(keep_a[:, :piece], got_a[:, :piece]) + cross.astype(jnp.float32)).astype(jnp.bfloat16)
+    quarters = plane_gather(own_a)
+
+    precond, near_value = outer_half(jnp.stack([u, low]).astype(jnp.int32), quarters, near_g, eigvals)
+    precond, far_value = outer_half(jnp.stack([u, 1 - low]).astype(jnp.int32), quarters, far_g, eigvals, precond)
+    value = jnp.sum(near_value + far_value, axis=1)
+    part = jnp.sum(onehot * value[:, None], axis=0)
+    slots = value.reshape(seqs, tok)
+    blocks = jnp.stack([lax.dynamic_index_in_dim(slots, u ^ j, keepdims=False) for j in range(seqs)])
+    message = jnp.concatenate([blocks, jnp.broadcast_to(part[None, :], (seqs, SOURCES))], axis=1)
+    message = jnp.broadcast_to(message[:, None, :], (seqs, rows * cols, tok + SOURCES))
+    message = message.reshape(seqs * rows * cols, tok + SOURCES)
+    summed = jnp.sum(lax.all_to_all(message, PLANE, split_axis=0, concat_axis=0, tiled=True), axis=0)
+    scale_score = float(total_tokens) / float(width * width)
+    scores = summed[:tok] * scale_score
+    influence = summed[tok:] * (scale_score * (float(SOURCES) / float(total_tokens)))
+    return (precond, scores, influence)
+
+
 def solution(mesh):
     in_specs = (
         P(("grp", "seq"), ("row", "col")),
@@ -111,4 +328,6 @@
         P("seq", ("row", "col")),
     )
     out_specs = (P(("grp", "seq"), ("row", "col")), P(("grp", "seq")), P("grp"))
+    fits = (mesh.shape["seq"], mesh.shape["row"], mesh.shape["col"]) == (4, 2, 2)
+    local = local_pairs if fits else local_any
     return jax.shard_map(local, mesh=mesh, in_specs=in_specs, out_specs=out_specs, check_vma=False)

time: 158 us -> 132 us (0.84)
  starting transfers between devices: 107 us -> 28 us
  waiting for transfers between devices: 38 us -> 64.1 us
  Pallas kernels: 0 us -> 17.1 us
  blocking collectives: 0 us -> 9.86 us
  matrix products: 8.46 us -> 0 us
  local copies, waits for them, and re-layouts: 0.73 us -> 5 us
  other arithmetic: 2.85 us -> 6.66 us
    ppermute x29 -> x23, starting transfers between devices: 107 us -> 28 us  [the longest x21 22 us: swap(): lax.ppermute(x, axis, [(i, i ^ step) for i in range(lax.axis_size(axis))])]
    ppermute x29 -> x23, waiting for transfers between devices: 38 us -> 64.1 us  [the longest x21 62.7 us: swap(): lax.ppermute(x, axis, [(i, i ^ step) for i in range(lax.axis_size(axis))])]
    pallas_call x0 -> x4, Pallas kernels: none -> 17.1 us  [the longest x2 10.1 us: outer_half(): pl.pallas_call(outer_kernel, out_shape=(jax.ShapeDtypeStruct(eigvals.shap...]
    all_to_all x0 -> x1, blocking collectives: none -> 9.86 us  [local_pairs(): lax.all_to_all(message, PLANE, split_axis=0, concat_axis=0, tiled=True)]
    dot_general x13 -> x0, matrix products: 8.46 us -> none  [the longest x8 3.56 us: rotate(): jnp.dot(x, basis, preferred_element_type=jnp.float32).astype(jnp.bfloat16)]
    dynamic_slice x0 -> x3, local copies, waits for them, and re-layouts: none -> 2.68 us  [the longest x1 2.65 us: local_pairs(): lax.dynamic_slice_in_dim(basis_in, (1 - k) * half, half, axis=1)]
    another operation x3 -> x6, other arithmetic: 1.35 us -> 3.15 us  [the longest x2 2.91 us: local_pairs(): both = jnp.stack([own, other])]
  transfers between devices with their start and end apart: 29 -> 23, of which waited for: 9 -> 10; matrix products, arithmetic and copies ran while one was open for 4% -> 4% of each run, Pallas kernels for 0% -> 9%
where the time goes in v2:
time: 132 us
  waiting for transfers between devices  64.1 us (49%)
  starting transfers between devices  28 us (21%)
  Pallas kernels  17.1 us (13%)
  blocking collectives  9.86 us (7%)
  other arithmetic  6.66 us (5%)
  local copies, waits for them, and re-layouts  5 us (4%)
    ppermute x21, waiting for transfers between devices, swap(): lax.ppermute(x, axis, [(i, i ^ step) for i in range(lax.axis_size(axis))])  62.7 us
    ppermute x21, starting transfers between devices, swap(): lax.ppermute(x, axis, [(i, i ^ step) for i in range(lax.axis_size(axis))])  22 us
    pallas_call x2, Pallas kernels, outer_half(): pl.pallas_call(outer_kernel, out_shape=(jax.ShapeDtypeStruct(eigvals.shap...  10.1 us
    all_to_all x1, blocking collectives, local_pairs(): lax.all_to_all(message, PLANE, split_axis=0, concat_axis=0, tiled=True)  9.86 us
    pallas_call x2, Pallas kernels, rotate(): pl.pallas_call(rotate_kernel, out_shape=(jax.ShapeDtypeStruct((rows, half...  6.98 us
    ppermute x2, starting transfers between devices, turned(): return lax.ppermute(x, PLANE, pairs)  6.02 us
    another operation x2, other arithmetic, local_pairs(): both = jnp.stack([own, other])  2.91 us
    dynamic_slice x1, local copies, waits for them, and re-layouts, local_pairs(): lax.dynamic_slice_in_dim(basis_in, (1 - k) * half, half, axis=1)  2.65 us
  transfers between devices with their start and end apart: 23, of which 10 were waited for; matrix products, arithmetic and copies ran while one was open for 4% of the time, Pallas kernels for 9%

profile of v2, /device:TPU:0, one launch (start us, length us, event | category | flops | bytes accessed | tf_op | source)
XLA Modules:
  0.0 131.6 jit_solution(131631972780913023)
XLA Ops:
  0.6 2.7 %constant_dynamic-slice_fusion.8 = (bf16[1024,512]{1,0:T(8,128)(2,1)}, bf16[1,1024,512]{2,1,0:T(8,128)(2,1)S(1)}) fusion(bf16[1024,1024]{1,0:T(8,128)(2,1)} %param.10, s32[]{:T(128)S(6)} %select_n.62, s32[]{:T(128)S(6)} %select_n.61), kind=kLoop, calls=%fused_computation.34 | loop fusion | bytes 4194312 | tf_op jit(solution)/shard_map/dynamic_slice | solution.py:277
  3.3 0.5 collective-permute-start.5
  3.7 1.7 %collective-permute-start.13 = (bf16[128,1024]{1,0:T(8,128)(2,1)}, bf16[128,1024]{1,0:T(8,128)(2,1)S(1)}, u32[]{:S(2)}, u32[]{:S(2)}) collective-permute-start(bf16[128,1024]{1,0:T(8,128)(2,1)} %param.8), channel_id=1, source_target_pairs={{0,0},{1,4},{2,8},{3,12},{4,2},{5,6},{6,10},{7,14},{8,1},{9,5},{10... | collective-permute-start | bytes 786440 | tf_op jit(solution)/shard_map/ppermute | solution.py:267
  5.5 5.6 %collective-permute-start = (bf16[128,1024]{1,0:T(8,128)(2,1)}, bf16[128,1024]{1,0:T(8,128)(2,1)}, u32[]{:S(2)}, u32[]{:S(2)}) collective-permute-start(bf16[128,1024]{1,0:T(8,128)(2,1)} %param.7), channel_id=1, source_target_pairs={{0,2},{2,0},{1,3},{3,1},{4,6},{6,4},{5,7},{7,5},{8,10},{10,8},{9,1... | collective-permute-start | bytes 786440 | tf_op jit(solution)/shard_map/ppermute | solution.py:107
  11.1 0.0 collective-permute-done.5
  11.1 1.8 %fusion.3 = bf16[2,512,256]{2,1,0:T(8,128)(2,1)} fusion(s32[]{:T(128)S(6)} %select_n.65, s32[]{:T(128)S(6)} %select_n.66, bf16[1,1024,512]{2,1,0:T(8,128)(2,1)S(1)} %get-tuple-element.20, bf16[1,1024,512]{2,1,0:T(8,128)(2,1)} %bitcast.3), kind=kLoop, calls=%fused_computation.13 | loop fusion | flops 1048576 | bytes 2621448 | tf_op jit(solution)/shard_map/stack | solution.py:278
  12.8 0.0 collective-permute-start.6
  12.9 0.0 collective-permute-done.13.x0
  12.9 5.6 %collective-permute-start.14 = (bf16[128,1024]{1,0:T(8,128)(2,1)S(1)}, bf16[128,1024]{1,0:T(8,128)(2,1)S(1)}, u32[]{:S(2)}, u32[]{:S(2)}) collective-permute-start(bf16[128,1024]{1,0:T(8,128)(2,1)S(1)} %collective-permute-done.13.x0), channel_id=1, source_target_pairs={{0,2},{2,0},{1,3},{3,1},{4,6},{6,4},{5,7},{7,5},{8,10},{10,8},{9,1... | collective-permute-start | bytes 786440 | tf_op jit(solution)/shard_map/ppermute | solution.py:107
  18.4 4.2 %collective-permute-done = bf16[128,1024]{1,0:T(8,128)(2,1)} collective-permute-done((bf16[128,1024]{1,0:T(8,128)(2,1)}, bf16[128,1024]{1,0:T(8,128)(2,1)}, u32[]{:S(2)}, u32[]{:S(2)}) %collective-permute-start) | collective-permute-done | bytes 262176 | tf_op jit(solution)/shard_map/ppermute | solution.py:107
  22.6 4.3 %collective-permute-start.1 = (bf16[128,1024]{1,0:T(8,128)(2,1)}, bf16[128,1024]{1,0:T(8,128)(2,1)S(1)}, u32[]{:S(2)}, u32[]{:S(2)}) collective-permute-start(bf16[128,1024]{1,0:T(8,128)(2,1)} %collective-permute-done), channel_id=1, source_target_pairs={{0,8},{1,12},{2,0},{3,4},{4,10},{5,14},{6,2},{7,6},{8,9},{9,13},{1... | collective-permute-start | bytes 786440 | tf_op jit(solution)/shard_map/ppermute | solution.py:267
  26.9 0.1 collective-permute-start.15
  27.0 12.3 %collective-permute-done.14.x1 = bf16[128,1024]{1,0:T(8,128)(2,1)S(1)} collective-permute-done((bf16[128,1024]{1,0:T(8,128)(2,1)S(1)}, bf16[128,1024]{1,0:T(8,128)(2,1)S(1)}, u32[]{:S(2)}, u32[]{:S(2)}) %collective-permute-start.14) | collective-permute-done | bytes 262176 | tf_op jit(solution)/shard_map/ppermute | solution.py:107
  39.4 0.1 collective-permute-start.16
  39.5 1.4 %collective-permute-done.1.x0 = bf16[128,1024]{1,0:T(8,128)(2,1)S(1)} collective-permute-done((bf16[128,1024]{1,0:T(8,128)(2,1)}, bf16[128,1024]{1,0:T(8,128)(2,1)S(1)}, u32[]{:S(2)}, u32[]{:S(2)}) %collective-permute-start.1) | collective-permute-done | bytes 262176 | tf_op jit(solution)/shard_map/ppermute | solution.py:267
  40.9 1.1 collective-permute-start.2
  42.0 0.0 collective-permute-done.6
  42.0 1.6 %collective-permute-start.7 = (bf16[2,512,256]{2,1,0:T(8,128)(2,1)}, bf16[2,512,256]{2,1,0:T(8,128)(2,1)}, u32[]{:S(2)}, u32[]{:S(2)}) collective-permute-start(bf16[2,512,256]{2,1,0:T(8,128)(2,1)} %collective-permute-done.6), channel_id=1, source_target_pairs={{0,16},{16,0},{1,17},{17,1},{2,18},{18,2},{3,19},{19,3},{4,20},{20... | collective-permute-start | bytes 1572872 | tf_op jit(solution)/shard_map/ppermute | solution.py:107
  43.6 0.1 pad_add_fusion.2.order
  43.7 0.0 collective-permute-start.3
  43.7 0.0 collective-permute-done.15.x2
  43.7 3.9 %rotate.3 = (bf16[512,512]{1,0:T(8,128)(2,1)S(1)}, f32[512,512]{1,0:T(8,128)S(1)}) custom-call(s32[4]{0:T(128)S(1)} %pad_add_fusion.2.order, bf16[128,1024]{1,0:T(8,128)(2,1)S(1)} %collective-permute-done.13.x0, bf16[128,1024]{1,0:T(8,128)(2,1)S(1)} %collective-permute-done.14.x1, bf16[128,1024]{1,0:T(8,128)(2,1)S(1)} %collective-permute-done.15.x2, ...), custom_call_target="tpu_custom_call" | custom-call | flops 1073741824 | bytes 2097152 | tf_op jit(solution)/shard_map/rotate/pallas_call | solution.py:142
  47.7 0.1 collective-permute-start.17
  47.8 1.1 collective-permute-done.2.x1
  48.8 0.0 collective-permute-start.4
  48.8 1.1 fusion
  50.0 0.1 slice_bitcast_fusion.1
  50.0 6.3 %collective-permute-done.7 = bf16[2,512,256]{2,1,0:T(8,128)(2,1)} collective-permute-done((bf16[2,512,256]{2,1,0:T(8,128)(2,1)}, bf16[2,512,256]{2,1,0:T(8,128)(2,1)}, u32[]{:S(2)}, u32[]{:S(2)}) %collective-permute-start.7) | collective-permute-done | bytes 524320 | tf_op jit(solution)/shard_map/ppermute | solution.py:107
  56.3 1.3 broadcast_select_fusion.1
  57.6 0.1 fusion.2
  57.7 0.3 pad_maximum_fusion.basis
  57.9 0.0 collective-permute-done.3.x2
  58.0 3.0 %rotate.2 = (bf16[512,512]{1,0:T(8,128)(2,1)S(1)}, f32[512,512]{1,0:T(8,128)S(1)}) custom-call(s32[4]{0:T(128)S(1)} %broadcast_xor_fusion.order, bf16[128,1024]{1,0:T(8,128)(2,1)S(1)} %collective-permute-done.1.x0, bf16[128,1024]{1,0:T(8,128)(2,1)S(1)} %collective-permute-done.2.x1, bf16[128,1024]{1,0:T(8,128)(2,1)S(1)} %collective-permute-done.3.x2, ...), custom_call_target="tpu_custom_call" | custom-call | flops 1073741824 | bytes 2097152 | tf_op jit(solution)/shard_map/rotate/pallas_call | solution.py:142
  61.0 0.0 copy-start.5
  61.0 0.2 collective-permute-start.8
  61.3 0.8 collective-permute-done.17
  62.1 0.2 add_convert_fusion.1
  62.2 1.5 %collective-permute-start.18 = (bf16[512,512]{1,0:T(8,128)(2,1)S(1)}, bf16[512,512]{1,0:T(8,128)(2,1)S(1)}, u32[]{:S(2)}, u32[]{:S(2)}) collective-permute-start(bf16[512,512]{1,0:T(8,128)(2,1)S(1)} %add_convert_fusion.1), channel_id=1, source_target_pairs={{0,8},{4,12},{8,0},{12,4},{1,9},{5,13},{9,1},{13,5},{2,10},{6,14},... | collective-permute-start | bytes 1572872 | tf_op jit(solution)/shard_map/ppermute | solution.py:107
  63.7 20.1 %collective-permute-done.8 = bf16[512,512]{1,0:T(8,128)(2,1)S(1)} collective-permute-done((bf16[512,512]{1,0:T(8,128)(2,1)S(1)}, bf16[512,512]{1,0:T(8,128)(2,1)S(1)}, u32[]{:S(2)}, u32[]{:S(2)}) %collective-permute-start.8) | collective-permute-done | bytes 524320 | tf_op jit(solution)/shard_map/ppermute | solution.py:107
  83.8 0.1 add_convert_fusion.3
  83.9 0.1 collective-permute-start.9
  84.0 1.9 %collective-permute-start.20 = (s32[128]{0:T(128)S(1)}, s32[128]{0:T(128)S(1)}, u32[]{:S(2)}, u32[]{:S(2)}) collective-permute-start(s32[128]{0:T(128)S(1)} %copy-done.5), channel_id=1, source_target_pairs={{0,4},{4,0},{8,12},{12,8},{1,5},{5,1},{9,13},{13,9},{2,6},{6,2},{1... | collective-permute-start | bytes 1544 | tf_op jit(solution)/shard_map/ppermute | solution.py:107
  85.9 1.0 collective-permute-start.21
  86.9 1.5 %collective-permute-start.22 = (s32[128]{0:T(128)S(1)}, s32[128]{0:T(128)S(1)}, u32[]{:S(2)}, u32[]{:S(2)}) collective-permute-start(s32[128]{0:T(128)S(1)} %copy-done.5), channel_id=1, source_target_pairs={{0,12},{4,8},{8,4},{12,0},{1,13},{5,9},{9,5},{13,1},{2,14},{6,10},... | collective-permute-start | bytes 1544 | tf_op jit(solution)/shard_map/ppermute | solution.py:107
  88.4 0.1 pad_add_fusion.3.place
  88.5 10.7 %collective-permute-done.9 = bf16[512,256]{1,0:T(8,128)(2,1)S(1)} collective-permute-done((bf16[512,256]{1,0:T(8,128)(2,1)S(1)}, bf16[512,256]{1,0:T(8,128)(2,1)S(1)}, u32[]{:S(2)}, u32[]{:S(2)}) %collective-permute-start.9) | collective-permute-done | bytes 262176 | tf_op jit(solution)/shard_map/ppermute | solution.py:107
  99.3 0.1 add_convert_fusion.2.a0
  99.4 1.0 collective-permute-start.10
  100.4 0.0 collective-permute-done.18
  100.4 0.1 add_convert_fusion.g
  100.5 0.1 collective-permute-start.19
  100.6 0.1 pad_add_fusion.1.place
  100.7 0.1 collective-permute-start.11
  100.7 5.8 %collective-permute-done.10.a1 = bf16[512,256]{1,0:T(8,128)(2,1)S(1)} collective-permute-done((bf16[512,256]{1,0:T(8,128)(2,1)S(1)}, bf16[512,256]{1,0:T(8,128)(2,1)S(1)}, u32[]{:S(2)}, u32[]{:S(2)}) %collective-permute-start.10) | collective-permute-done | bytes 262176 | tf_op jit(solution)/shard_map/ppermute | solution.py:107
  106.5 0.0 collective-permute-start.12
  106.6 1.5 %collective-permute-done.12.a3 = bf16[512,256]{1,0:T(8,128)(2,1)S(1)} collective-permute-done((bf16[512,256]{1,0:T(8,128)(2,1)S(1)}, bf16[512,256]{1,0:T(8,128)(2,1)S(1)}, u32[]{:S(2)}, u32[]{:S(2)}) %collective-permute-start.12) | collective-permute-done | bytes 262176 | tf_op jit(solution)/shard_map/ppermute | solution.py:107
  108.0 2.2 %copy-done = f32[1024,1024]{1,0:T(8,128)S(1)} copy-done((f32[1024,1024]{1,0:T(8,128)S(1)}, f32[1024,1024]{1,0:T(8,128)}, u32[]{:S(2)}) %copy-start) | copy-done | bytes 4194328
  110.2 5.1 %outer_half.2 = (f32[1024,1024]{1,0:T(8,128)}, f32[512,128]{1,0:T(8,128)S(1)}) custom-call(s32[2]{0:T(128)S(1)} %pad_add_fusion.3.place, bf16[512,256]{1,0:T(8,128)(2,1)S(1)} %add_convert_fusion.2.a0, bf16[512,256]{1,0:T(8,128)(2,1)S(1)} %collective-permute-done.10.a1, bf16[512,256]{1,0:T(8,128)(2,1)S(1)} %collective-permute-done.11.a2, ...), custom_call_target="tpu_custom_call" | custom-call | flops 1073741824 | bytes 4194304 | tf_op jit(solution)/shard_map/outer_half/pallas_call | solution.py:223
  115.3 5.1 %outer_half.3 = (f32[1024,1024]{1,0:T(8,128)}, f32[512,128]{1,0:T(8,128)S(1)}) custom-call(s32[2]{0:T(128)S(1)} %pad_add_fusion.1.place, bf16[512,256]{1,0:T(8,128)(2,1)S(1)} %add_convert_fusion.2.a0, bf16[512,256]{1,0:T(8,128)(2,1)S(1)} %collective-permute-done.10.a1, ...), custom_call_target="tpu_custom_call", output_to_operand_aliasing={{0}: (7, {})} | custom-call | flops 1073741824 | bytes 4194304 | tf_op jit(solution)/shard_map/outer_half/pallas_call | solution.py:223
  120.3 0.1 add_reduce_fusion
  120.5 0.1 select_reduce_fusion
  120.7 9.9 %all_to_all.9 = f32[16,1,136]{2,1,0:T(1,128)S(1)} all-to-all(f32[16,1,136]{2,1,0:T(1,128)S(1)} %all_to_all.6), channel_id=1, replica_groups=mesh['grp'=2,'seq'=4,'row'=2,'col'=2] {'seq','row','col'}, dimensions={0} | all-to-all | bytes 17408 | tf_op jit(solution)/shard_map/all_to_all | solution.py:314
  130.6 0.5 slice_multiply_fusion
  131.1 0.5 slice_multiply_fusion.1
  (29 shorter events, 0.2 us)
Async XLA Ops:
  3.3 9.6 %copy-start.3 = (bf16[1,1024,512]{2,1,0:T(8,128)(2,1)}, bf16[1,1024,512]{2,1,0:T(8,128)(2,1)S(1)}, u32[]{:S(2)}) copy-start(bf16[1,1024,512]{2,1,0:T(8,128)(2,1)S(1)} %get-tuple-element.20) | copy-start | bytes 3145732
  3.3 38.7 %copy-start.6 = (s32[4]{0:T(128)S(1)}, s32[4]{0:T(128)}, u32[]{:S(2)}) copy-start(s32[4]{0:T(128)} %constant.68.clone) | copy-start | bytes 52
  3.3 40.4 %copy-start.2 = (bf16[1024,1024]{1,0:T(8,128)(2,1)S(1)}, bf16[1024,1024]{1,0:T(8,128)(2,1)}, u32[]{:S(2)}) copy-start(bf16[1024,1024]{1,0:T(8,128)(2,1)} %basis.1) | copy-start | bytes 6291460
  3.3 7.8 %collective-permute-start.5 = (bf16[1024,512]{1,0:T(8,128)(2,1)}, bf16[1024,512]{1,0:T(8,128)(2,1)}, u32[]{:S(2)}, u32[]{:S(2)}) collective-permute-start(bf16[1024,512]{1,0:T(8,128)(2,1)} %get-tuple-element.19), channel_id=1, source_target_pairs={{0,1},{1,0},{2,3},{3,2},{4,5},{5,4},{6,7},{7,6},{8,9},{9,8},{10,11... | collective-permute-start | bytes 3145736 | tf_op jit(solution)/shard_map/ppermute | solution.py:107
  3.7 9.1 %collective-permute-start.13 = (bf16[128,1024]{1,0:T(8,128)(2,1)}, bf16[128,1024]{1,0:T(8,128)(2,1)S(1)}, u32[]{:S(2)}, u32[]{:S(2)}) collective-permute-start(bf16[128,1024]{1,0:T(8,128)(2,1)} %param.8), channel_id=1, source_target_pairs={{0,0},{1,4},{2,8},{3,12},{4,2},{5,6},{6,10},{7,14},{8,1},{9,5},{10... | collective-permute-start | bytes 786440 | tf_op jit(solution)/shard_map/ppermute | solution.py:267
  5.5 17.1 %collective-permute-start = (bf16[128,1024]{1,0:T(8,128)(2,1)}, bf16[128,1024]{1,0:T(8,128)(2,1)}, u32[]{:S(2)}, u32[]{:S(2)}) collective-permute-start(bf16[128,1024]{1,0:T(8,128)(2,1)} %param.7), channel_id=1, source_target_pairs={{0,2},{2,0},{1,3},{3,1},{4,6},{6,4},{5,7},{7,5},{8,10},{10,8},{9,1... | collective-permute-start | bytes 786440 | tf_op jit(solution)/shard_map/ppermute | solution.py:107
  12.8 29.2 %collective-permute-start.6 = (bf16[2,512,256]{2,1,0:T(8,128)(2,1)}, bf16[2,512,256]{2,1,0:T(8,128)(2,1)}, u32[]{:S(2)}, u32[]{:S(2)}) collective-permute-start(bf16[2,512,256]{2,1,0:T(8,128)(2,1)} %fusion.3), channel_id=1, source_target_pairs={{0,2},{2,0},{1,3},{3,1},{4,6},{6,4},{5,7},{7,5},{8,10},{10,8},{9,1... | collective-permute-start | bytes 1572872 | tf_op jit(solution)/shard_map/ppermute | solution.py:107
  12.9 26.5 %collective-permute-start.14 = (bf16[128,1024]{1,0:T(8,128)(2,1)S(1)}, bf16[128,1024]{1,0:T(8,128)(2,1)S(1)}, u32[]{:S(2)}, u32[]{:S(2)}) collective-permute-start(bf16[128,1024]{1,0:T(8,128)(2,1)S(1)} %collective-permute-done.13.x0), channel_id=1, source_target_pairs={{0,2},{2,0},{1,3},{3,1},{4,6},{6,4},{5,7},{7,5},{8,10},{10,8},{9,1... | collective-permute-start | bytes 786440 | tf_op jit(solution)/shard_map/ppermute | solution.py:107
  22.6 18.3 %collective-permute-start.1 = (bf16[128,1024]{1,0:T(8,128)(2,1)}, bf16[128,1024]{1,0:T(8,128)(2,1)S(1)}, u32[]{:S(2)}, u32[]{:S(2)}) collective-permute-start(bf16[128,1024]{1,0:T(8,128)(2,1)} %collective-permute-done), channel_id=1, source_target_pairs={{0,8},{1,12},{2,0},{3,4},{4,10},{5,14},{6,2},{7,6},{8,9},{9,13},{1... | collective-permute-start | bytes 786440 | tf_op jit(solution)/shard_map/ppermute | solution.py:267
  26.9 16.8 %collective-permute-start.15 = (bf16[128,1024]{1,0:T(8,128)(2,1)S(1)}, bf16[128,1024]{1,0:T(8,128)(2,1)S(1)}, u32[]{:S(2)}, u32[]{:S(2)}) collective-permute-start(bf16[128,1024]{1,0:T(8,128)(2,1)S(1)} %collective-permute-done.13.x0), channel_id=1, source_target_pairs={{0,1},{1,0},{2,3},{3,2},{4,5},{5,4},{6,7},{7,6},{8,9},{9,8},{10,11... | collective-permute-start | bytes 786440 | tf_op jit(solution)/shard_map/ppermute | solution.py:107
  39.4 4.4 %collective-permute-start.16 = (bf16[128,1024]{1,0:T(8,128)(2,1)S(1)}, bf16[128,1024]{1,0:T(8,128)(2,1)}, u32[]{:S(2)}, u32[]{:S(2)}) collective-permute-start(bf16[128,1024]{1,0:T(8,128)(2,1)S(1)} %collective-permute-done.14.x1), channel_id=1, source_target_pairs={{0,1},{1,0},{2,3},{3,2},{4,5},{5,4},{6,7},{7,6},{8,9},{9,8},{10,11... | collective-permute-start | bytes 786440 | tf_op jit(solution)/shard_map/ppermute | solution.py:107
  40.9 7.9 %collective-permute-start.2 = (bf16[128,1024]{1,0:T(8,128)(2,1)S(1)}, bf16[128,1024]{1,0:T(8,128)(2,1)S(1)}, u32[]{:S(2)}, u32[]{:S(2)}) collective-permute-start(bf16[128,1024]{1,0:T(8,128)(2,1)S(1)} %collective-permute-done.1.x0), channel_id=1, source_target_pairs={{0,2},{2,0},{1,3},{3,1},{4,6},{6,4},{5,7},{7,5},{8,10},{10,8},{9,1... | collective-permute-start | bytes 786440 | tf_op jit(solution)/shard_map/ppermute | solution.py:107
  42.0 14.3 %collective-permute-start.7 = (bf16[2,512,256]{2,1,0:T(8,128)(2,1)}, bf16[2,512,256]{2,1,0:T(8,128)(2,1)}, u32[]{:S(2)}, u32[]{:S(2)}) collective-permute-start(bf16[2,512,256]{2,1,0:T(8,128)(2,1)} %collective-permute-done.6), channel_id=1, source_target_pairs={{0,16},{16,0},{1,17},{17,1},{2,18},{18,2},{3,19},{19,3},{4,20},{20... | collective-permute-start | bytes 1572872 | tf_op jit(solution)/shard_map/ppermute | solution.py:107
  43.7 5.2 %copy-start.4 = (bf16[1,1024,512]{2,1,0:T(8,128)(2,1)S(1)}, bf16[1,1024,512]{2,1,0:T(8,128)(2,1)}, u32[]{:S(2)}) copy-start(bf16[1,1024,512]{2,1,0:T(8,128)(2,1)} %copy-done.3) | copy-start | bytes 3145732
  43.7 14.3 %collective-permute-start.3 = (bf16[128,1024]{1,0:T(8,128)(2,1)S(1)}, bf16[128,1024]{1,0:T(8,128)(2,1)S(1)}, u32[]{:S(2)}, u32[]{:S(2)}) collective-permute-start(bf16[128,1024]{1,0:T(8,128)(2,1)S(1)} %collective-permute-done.1.x0), channel_id=1, source_target_pairs={{0,1},{1,0},{2,3},{3,2},{4,5},{5,4},{6,7},{7,6},{8,9},{9,8},{10,11... | collective-permute-start | bytes 786440 | tf_op jit(solution)/shard_map/ppermute | solution.py:107
  47.7 14.4 %collective-permute-start.17 = (bf16[512,512]{1,0:T(8,128)(2,1)S(1)}, bf16[512,512]{1,0:T(8,128)(2,1)S(1)}, u32[]{:S(2)}, u32[]{:S(2)}) collective-permute-start(bf16[512,512]{1,0:T(8,128)(2,1)S(1)} %get-tuple-element.14), channel_id=1, source_target_pairs={{0,4},{4,0},{8,12},{12,8},{1,5},{5,1},{9,13},{13,9},{2,6},{6,2},{1... | collective-permute-start | bytes 1572872 | tf_op jit(solution)/shard_map/ppermute | solution.py:107
  48.8 9.1 %collective-permute-start.4 = (bf16[128,1024]{1,0:T(8,128)(2,1)S(1)}, bf16[128,1024]{1,0:T(8,128)(2,1)S(1)}, u32[]{:S(2)}, u32[]{:S(2)}) collective-permute-start(bf16[128,1024]{1,0:T(8,128)(2,1)S(1)} %collective-permute-done.2.x1), channel_id=1, source_target_pairs={{0,1},{1,0},{2,3},{3,2},{4,5},{5,4},{6,7},{7,6},{8,9},{9,8},{10,11... | collective-permute-start | bytes 786440 | tf_op jit(solution)/shard_map/ppermute | solution.py:107
  61.0 23.0 %copy-start.5 = (s32[128]{0:T(128)S(1)}, s32[128]{0:T(128)}, u32[]{:S(2)}) copy-start(s32[128]{0:T(128)} %param.9) | copy-start | bytes 1540
  61.0 22.8 %collective-permute-start.8 = (bf16[512,512]{1,0:T(8,128)(2,1)S(1)}, bf16[512,512]{1,0:T(8,128)(2,1)S(1)}, u32[]{:S(2)}, u32[]{:S(2)}) collective-permute-start(bf16[512,512]{1,0:T(8,128)(2,1)S(1)} %get-tuple-element.12), channel_id=1, source_target_pairs={{0,4},{4,0},{8,12},{12,8},{1,5},{5,1},{9,13},{13,9},{2,6},{6,2},{1... | collective-permute-start | bytes 1572872 | tf_op jit(solution)/shard_map/ppermute | solution.py:107
  62.2 38.1 %collective-permute-start.18 = (bf16[512,512]{1,0:T(8,128)(2,1)S(1)}, bf16[512,512]{1,0:T(8,128)(2,1)S(1)}, u32[]{:S(2)}, u32[]{:S(2)}) collective-permute-start(bf16[512,512]{1,0:T(8,128)(2,1)S(1)} %add_convert_fusion.1), channel_id=1, source_target_pairs={{0,8},{4,12},{8,0},{12,4},{1,9},{5,13},{9,1},{13,5},{2,10},{6,14},... | collective-permute-start | bytes 1572872 | tf_op jit(solution)/shard_map/ppermute | solution.py:107
  83.9 15.4 %collective-permute-start.9 = (bf16[512,256]{1,0:T(8,128)(2,1)S(1)}, bf16[512,256]{1,0:T(8,128)(2,1)S(1)}, u32[]{:S(2)}, u32[]{:S(2)}) collective-permute-start(bf16[512,256]{1,0:T(8,128)(2,1)S(1)} %add_convert_fusion.3), channel_id=1, source_target_pairs={{0,8},{4,12},{8,0},{12,4},{1,9},{5,13},{9,1},{13,5},{2,10},{6,14},... | collective-permute-start | bytes 786440 | tf_op jit(solution)/shard_map/ppermute | solution.py:107
  84.0 16.7 %collective-permute-start.20 = (s32[128]{0:T(128)S(1)}, s32[128]{0:T(128)S(1)}, u32[]{:S(2)}, u32[]{:S(2)}) collective-permute-start(s32[128]{0:T(128)S(1)} %copy-done.5), channel_id=1, source_target_pairs={{0,4},{4,0},{8,12},{12,8},{1,5},{5,1},{9,13},{13,9},{2,6},{6,2},{1... | collective-permute-start | bytes 1544 | tf_op jit(solution)/shard_map/ppermute | solution.py:107
  85.9 20.6 %collective-permute-start.21 = (s32[128]{0:T(128)S(1)}, s32[128]{0:T(128)S(1)}, u32[]{:S(2)}, u32[]{:S(2)}) collective-permute-start(s32[128]{0:T(128)S(1)} %copy-done.5), channel_id=1, source_target_pairs={{0,8},{4,12},{8,0},{12,4},{1,9},{5,13},{9,1},{13,5},{2,10},{6,14},... | collective-permute-start | bytes 1544 | tf_op jit(solution)/shard_map/ppermute | solution.py:107
  86.9 19.6 %collective-permute-start.22 = (s32[128]{0:T(128)S(1)}, s32[128]{0:T(128)S(1)}, u32[]{:S(2)}, u32[]{:S(2)}) collective-permute-start(s32[128]{0:T(128)S(1)} %copy-done.5), channel_id=1, source_target_pairs={{0,12},{4,8},{8,4},{12,0},{1,13},{5,9},{9,5},{13,1},{2,14},{6,10},... | collective-permute-start | bytes 1544 | tf_op jit(solution)/shard_map/ppermute | solution.py:107
  99.4 7.1 %collective-permute-start.10 = (bf16[512,256]{1,0:T(8,128)(2,1)S(1)}, bf16[512,256]{1,0:T(8,128)(2,1)S(1)}, u32[]{:S(2)}, u32[]{:S(2)}) collective-permute-start(bf16[512,256]{1,0:T(8,128)(2,1)S(1)} %add_convert_fusion.2.a0), channel_id=1, source_target_pairs={{0,2},{2,0},{1,3},{3,1},{4,6},{6,4},{5,7},{7,5},{8,10},{10,8},{9,1... | collective-permute-start | bytes 786440 | tf_op jit(solution)/shard_map/ppermute | solution.py:107
  100.5 14.8 %collective-permute-start.19 = (bf16[512,512]{1,0:T(8,128)(2,1)S(1)}, bf16[512,512]{1,0:T(8,128)(2,1)S(1)}, u32[]{:S(2)}, u32[]{:S(2)}) collective-permute-start(bf16[512,512]{1,0:T(8,128)(2,1)S(1)} %add_convert_fusion.g), channel_id=1, source_target_pairs={{0,4},{4,0},{8,12},{12,8},{1,5},{5,1},{9,13},{13,9},{2,6},{6,2},{1... | collective-permute-start | bytes 1572872 | tf_op jit(solution)/shard_map/ppermute | solution.py:107
  100.7 5.9 %collective-permute-start.11 = (bf16[512,256]{1,0:T(8,128)(2,1)S(1)}, bf16[512,256]{1,0:T(8,128)(2,1)S(1)}, u32[]{:S(2)}, u32[]{:S(2)}) collective-permute-start(bf16[512,256]{1,0:T(8,128)(2,1)S(1)} %add_convert_fusion.2.a0), channel_id=1, source_target_pairs={{0,1},{1,0},{2,3},{3,2},{4,5},{5,4},{6,7},{7,6},{8,9},{9,8},{10,11... | collective-permute-start | bytes 786440 | tf_op jit(solution)/shard_map/ppermute | solution.py:107
  106.5 1.5 %collective-permute-start.12 = (bf16[512,256]{1,0:T(8,128)(2,1)S(1)}, bf16[512,256]{1,0:T(8,128)(2,1)S(1)}, u32[]{:S(2)}, u32[]{:S(2)}) collective-permute-start(bf16[512,256]{1,0:T(8,128)(2,1)S(1)} %collective-permute-done.10.a1), channel_id=1, source_target_pairs={{0,1},{1,0},{2,3},{3,2},{4,5},{5,4},{6,7},{7,6},{8,9},{9,8},{10,11... | collective-permute-start | bytes 786440 | tf_op jit(solution)/shard_map/ppermute | solution.py:107
  108.0 2.2 %copy-start = (f32[1024,1024]{1,0:T(8,128)S(1)}, f32[1024,1024]{1,0:T(8,128)}, u32[]{:S(2)}) copy-start(f32[1024,1024]{1,0:T(8,128)} %eig.3) | copy-start | bytes 12582916
  110.2 5.1 %copy-start.1 = (f32[1024,1024]{1,0:T(8,128)S(1)}, f32[1024,1024]{1,0:T(8,128)}, u32[]{:S(2)}) copy-start(f32[1024,1024]{1,0:T(8,128)} %eig.3) | copy-start | bytes 12582916

commit v3 on v2

--- a/solution.py
+++ b/solution.py
@@ -103,6 +103,9 @@
     return (precond, scores, influence)
 
 
+VMEM = 56 * 2**20
+
+
 def swap(x, axis, step=1):
     return lax.ppermute(x, axis, [(i, i ^ step) for i in range(lax.axis_size(axis))])
 
@@ -112,87 +115,59 @@
 
 
 def rotate_kernel(order, x0, x1, x2, x3, basis, send, keep, rows):
-    step = pl.program_id(0)
-    half = pl.num_programs(0) // 2
     tok = x0.shape[0]
-
-    @pl.when(step == 0)
-    def _():
-        for j, x in enumerate((x0, x1, x2, x3)):
-            rows[pl.ds(j * tok, tok), :] = x[...]
-
-    block = jnp.dot(rows[...], basis[...], preferred_element_type=jnp.float32)
-
-    @pl.when(step < half)
-    def _():
-        send[...] = block.astype(jnp.bfloat16)
-
-    @pl.when(step >= half)
-    def _():
-        keep[...] = block
+    half, step = 2, basis.shape[1] // 4
+    for j, x in enumerate((x0, x1, x2, x3)):
+        rows[pl.ds(j * tok, tok), :] = x[...]
+    for i in range(2 * half):
+        where = pl.ds(pl.multiple_of(order[i] * step, step), step)
+        block = jnp.dot(rows[...], basis[:, where], preferred_element_type=jnp.float32)
+        if i < half:
+            send[:, i * step : (i + 1) * step] = block.astype(jnp.bfloat16)
+        else:
+            keep[:, (i - half) * step : (i - half + 1) * step] = block
 
 
 def rotate(slots, basis, order):
     tok, depth = slots[0].shape
-    blocks = order.shape[0]
-    step = basis.shape[1] // blocks
-    half = blocks // 2
-    rows = tok * len(slots)
-    whole = pl.BlockSpec((tok, depth), lambda i, order: (0, 0))
+    rows, cols = tok * len(slots), basis.shape[1]
+    vmem = pl.BlockSpec(memory_space=pltpu.VMEM)
     return pl.pallas_call(
         rotate_kernel,
         out_shape=(
-            jax.ShapeDtypeStruct((rows, half * step), jnp.bfloat16),
-            jax.ShapeDtypeStruct((rows, half * step), jnp.float32),
+            jax.ShapeDtypeStruct((rows, cols // 2), jnp.bfloat16),
+            jax.ShapeDtypeStruct((rows, cols // 2), jnp.float32),
         ),
-        grid_spec=pltpu.PrefetchScalarGridSpec(
-            num_scalar_prefetch=1,
-            grid=(blocks,),
-            in_specs=[whole] * 4 + [pl.BlockSpec((depth, step), lambda i, order: (0, order[i]))],
-            out_specs=(
-                pl.BlockSpec((rows, step), lambda i, order: (0, jnp.minimum(i, half - 1))),
-                pl.BlockSpec((rows, step), lambda i, order: (0, jnp.maximum(i - half, 0))),
-            ),
-            scratch_shapes=[pltpu.VMEM((rows, depth), jnp.bfloat16)],
-        ),
+        in_specs=[pl.BlockSpec(memory_space=pltpu.SMEM)] + [vmem] * 5,
+        out_specs=(vmem, vmem),
+        scratch_shapes=[pltpu.VMEM((rows, depth), jnp.bfloat16)],
         compiler_params=pltpu.CompilerParams(vmem_limit_bytes=24 * 2**20),
-        cost_estimate=pl.CostEstimate(
-            flops=2 * rows * depth * basis.shape[1], bytes_accessed=2 * depth * basis.shape[1], transcendentals=0
-        ),
+        cost_estimate=pl.CostEstimate(flops=2 * rows * depth * cols, bytes_accessed=2 * depth * cols, transcendentals=0),
         name="rotate",
     )(order, *slots, basis)
 
 
-def outer_kernel(place, a0, a1, a2, a3, g, eig, *refs):
-    precond, score = refs[-2:]
-    step = pl.program_id(0)
-    u = place[0]
-    tok = g.shape[0] // 4
-    piece = a0.shape[1]
+FEATURE = (0, 2, 1, 3)
+
+
+def outer_step(place, flat, turned, g, eig, precond, score):
+    piece = flat.shape[1] // 4
     total = None
-    for m, a in enumerate((a0, a1, a2, a3)):
-        outer = None
-        for j in range(4):
-            partial = lax.dot_general(
-                a[pl.ds((j ^ m) * tok, tok), :],
-                g[pl.ds(j * tok, tok), :],
-                (((0,), (0,)), ((), ())),
-                preferred_element_type=jnp.float32,
-            )
-            partial = partial.astype(jnp.bfloat16).astype(jnp.float32)
-            outer = partial if outer is None else outer + partial
-        where = pl.ds(pl.multiple_of((u ^ m) * piece, piece), piece)
+    for m in range(4):
+        outer = jnp.dot(turned[pl.ds(m * piece, piece), :], g[...], preferred_element_type=jnp.float32)
+        where = pl.ds(pl.multiple_of((place[0] ^ FEATURE[m]) * piece, piece), piece)
         ratio = outer / eig[where, :]
         precond[where, :] = ratio
-        mapped = jnp.dot(a[...], ratio.astype(jnp.bfloat16), preferred_element_type=jnp.float32)
-        blocks = [mapped[j * tok : (j + 1) * tok] for j in range(4)]
-        mapped = jnp.concatenate([blocks[j ^ m] for j in range(4)])
+        mapped = jnp.dot(
+            flat[:, m * piece : (m + 1) * piece], ratio.astype(jnp.bfloat16), preferred_element_type=jnp.float32
+        )
         total = mapped if total is None else total + mapped
     value = total * g[...].astype(jnp.float32)
     lanes = score.shape[1]
     folded = value[:, :lanes]
     for i in range(1, value.shape[1] // lanes):
         folded = folded + value[:, i * lanes : (i + 1) * lanes]
+    step = pl.program_id(0)
 
     @pl.when(step == 0)
     def _():
@@ -203,40 +178,59 @@
         score[...] += folded
 
 
+def near_kernel(place, a0, a1, a2, a3, g, eig, precond, score, flat, turned):
+    tok = g.shape[0] // 4
+    piece = a0.shape[1]
+
+    @pl.when(pl.program_id(0) == 0)
+    def _():
+        for m, a in enumerate((a0, a1, a2, a3)):
+            for j in range(4):
+                flat[pl.ds(j * tok, tok), m * piece : (m + 1) * piece] = a[pl.ds((j ^ m) * tok, tok), :]
+            turned[pl.ds(m * piece, piece), :] = flat[:, m * piece : (m + 1) * piece].T
+
+    outer_step(place, flat, turned, g, eig, precond, score)
+
+
+def far_kernel(place, flat, turned, g, eig, done, precond, score):
+    outer_step(place, flat, turned, g, eig, precond, score)
+
+
 def outer_half(place, acts, grads, eigvals, done=None):
-    tokens, piece = acts[0].shape
     width = eigvals.shape[0]
-    cols = 256
+    tokens, cols = grads.shape[0], 256
     steps = grads.shape[1] // cols
     here = lambda i, place: (0, place[1] * steps + i)
-    whole = pl.BlockSpec((tokens, piece), lambda i, place: (0, 0))
-    in_specs = [whole] * 4 + [
+    fixed = lambda a: pl.BlockSpec(a.shape, lambda i, place: (0, 0))
+    in_specs = [fixed(a) for a in acts] + [
         pl.BlockSpec((tokens, cols), lambda i, place: (0, i)),
         pl.BlockSpec((width, cols), here),
     ]
+    out_shape = [
+        jax.ShapeDtypeStruct(eigvals.shape, jnp.float32),
+        jax.ShapeDtypeStruct((tokens, 128), jnp.float32),
+    ]
+    out_specs = [pl.BlockSpec((width, cols), here), fixed(out_shape[1])]
     args = [place, *acts, grads, eigvals]
     aliases = {}
-    if done is not None:
+    if done is None:
+        out_shape += [
+            jax.ShapeDtypeStruct((tokens, width), jnp.bfloat16),
+            jax.ShapeDtypeStruct((width, tokens), jnp.bfloat16),
+        ]
+        out_specs += [fixed(out_shape[2]), fixed(out_shape[3])]
+    else:
         in_specs.append(pl.BlockSpec(memory_space=pl.ANY))
         aliases = {len(args): 0}
         args.append(done)
     return pl.pallas_call(
-        outer_kernel,
-        out_shape=(
-            jax.ShapeDtypeStruct(eigvals.shape, jnp.float32),
-            jax.ShapeDtypeStruct((tokens, 128), jnp.float32),
-        ),
+        near_kernel if done is None else far_kernel,
+        out_shape=out_shape,
         grid_spec=pltpu.PrefetchScalarGridSpec(
-            num_scalar_prefetch=1,
-            grid=(steps,),
-            in_specs=in_specs,
-            out_specs=(
-                pl.BlockSpec((width, cols), here),
-                pl.BlockSpec((tokens, 128), lambda i, place: (0, 0)),
-            ),
+            num_scalar_prefetch=1, grid=(steps,), in_specs=in_specs, out_specs=out_specs
         ),
         input_output_aliases=aliases,
-        compiler_params=pltpu.CompilerParams(vmem_limit_bytes=24 * 2**20),
+        compiler_params=pltpu.CompilerParams(vmem_limit_bytes=VMEM),
         cost_estimate=pl.CostEstimate(
             flops=4 * tokens * width * grads.shape[1], bytes_accessed=8 * width * grads.shape[1], transcendentals=0
         ),
@@ -259,38 +253,40 @@
     width = block * rows * cols
     half, piece = block // 2, block // 4
 
-    def turned(x, flip):
+    def turned(x):
         pairs = []
         for b in range(seqs):
             for f in range(rows * cols):
-                pairs.append((b * rows * cols + f, ((f ^ flip) * rows + b % rows) * cols + b // rows))
+                pairs.append((b * rows * cols + f, (f * rows + b % rows) * cols + b // rows))
         return lax.ppermute(x, PLANE, pairs)
 
     def plane_gather(x):
         near = swap(x, "row")
         return [x, near, swap(x, "col"), swap(near, "col")]
 
-    grads_here = turned(grads, 0)
-    acts_here = turned(swap(acts, "row"), cols)
-
-    own = lax.dynamic_slice_in_dim(basis_in, k * half, half, axis=1)
-    other = swap(lax.dynamic_slice_in_dim(basis_in, (1 - k) * half, half, axis=1), "col")
-    both = jnp.stack([own, other])
-    mine = lax.dynamic_slice_in_dim(both, x * piece, piece, axis=2)
-    theirs = lax.dynamic_slice(both, (0, y * half, (1 - x) * piece), (2, half, piece))
-    first = swap(theirs, "row")
+    other = lax.dynamic_slice(basis_in, (y * half, (1 - x) * half), (half, half))
+    first = swap(other, "row")
     second = swap(first, "grp")
     upper = jnp.where(y == 0, first, second)
     lower = jnp.where(y == 0, second, first)
-    far = jnp.concatenate([upper, lower], axis=1)
-    tiles = jnp.concatenate([mine[0], mine[1], far[0], far[1]], axis=1)
+    columns = jnp.stack([lax.dynamic_slice_in_dim(basis_in, x * half, half, axis=1), jnp.concatenate([upper, lower])])
+    mine = lax.dynamic_slice_in_dim(columns, k * piece, piece, axis=2)
+    near = swap(lax.dynamic_slice_in_dim(columns, (1 - k) * piece, piece, axis=2), "col")
+    tiles = jnp.concatenate([mine[0], near[0], mine[1], near[1]], axis=1)
 
     ids = jnp.stack([source_ids] + [swap(source_ids, "seq", j) for j in range(1, seqs)])
+    grads_here = turned(grads)
+    grads_near, ids = lax.optimization_barrier((swap(grads_here, "col"), ids))
+    acts, grads_near = lax.optimization_barrier((acts, grads_near))
+    acts_here = turned(acts)
+    grads_far = swap(grads_here, "row")
+    grad_slots = [grads_here, grads_far, grads_near, swap(grads_far, "col")]
+
     slot_ids = jnp.stack([lax.dynamic_index_in_dim(ids, u ^ s ^ j, keepdims=False) for j in range(seqs)])
     onehot = (slot_ids.reshape(-1, 1) == jnp.arange(SOURCES, dtype=jnp.int32)[None, :]).astype(jnp.float32)
 
     order_g = jnp.stack([2 - 2 * low, 3 - 2 * low, 2 * low, 2 * low + 1]).astype(jnp.int32)
-    send_g, keep_g = rotate(plane_gather(grads_here), basis_out, order_g)
+    send_g, keep_g = rotate(grad_slots, basis_out, order_g)
     pair_g = added(keep_g, swap(send_g, "seq", 1)).astype(jnp.bfloat16)
     near_g = added(pair_g, swap(pair_g, "seq", 2)).astype(jnp.bfloat16)
     far_g = swap(near_g, "seq", 1)
@@ -302,8 +298,10 @@
     own_a = (added(keep_a[:, :piece], got_a[:, :piece]) + cross.astype(jnp.float32)).astype(jnp.bfloat16)
     quarters = plane_gather(own_a)
 
-    precond, near_value = outer_half(jnp.stack([u, low]).astype(jnp.int32), quarters, near_g, eigvals)
-    precond, far_value = outer_half(jnp.stack([u, 1 - low]).astype(jnp.int32), quarters, far_g, eigvals, precond)
+    precond, near_value, flat, across = outer_half(jnp.stack([c, low]).astype(jnp.int32), quarters, near_g, eigvals)
+    precond, far_value = outer_half(
+        jnp.stack([c, 1 - low]).astype(jnp.int32), (flat, across), far_g, eigvals, precond
+    )
     value = jnp.sum(near_value + far_value, axis=1)
     part = jnp.sum(onehot * value[:, None], axis=0)
     slots = value.reshape(seqs, tok)

time: 132 us -> 145 us (1.098)
  starting transfers between devices: 28 us -> 40.5 us
  waiting for transfers between devices: 64.1 us -> 65.7 us
    ppermute x21 -> x20, starting transfers between devices: 22 us -> 38.2 us  [swap(): lax.ppermute(x, axis, [(i, i ^ step) for i in range(lax.axis_size(axis))])]
    ppermute x2, starting transfers between devices: 6.02 us -> 2.28 us  [turned(): return lax.ppermute(x, PLANE, pairs)]
    ppermute x21 -> x20, waiting for transfers between devices: 62.7 us -> 65.7 us  [swap(): lax.ppermute(x, axis, [(i, i ^ step) for i in range(lax.axis_size(axis))])]
    dynamic_slice x1, local copies, waits for them, and re-layouts: 2.65 us -> 1.08 us  [local_pairs(): lax.dynamic_slice(basis_in, (y * half, (1 - x) * half), (half, half))]
  transfers between devices with their start and end apart: 23 -> 22, of which waited for: 10 -> 7; matrix products, arithmetic and copies ran while one was open for 4% -> 4% of each run, Pallas kernels for 9% -> 7%
where the time goes in v3:
time: 145 us; the launch traced here: 144 us
  waiting for transfers between devices  65.7 us (45%)
  starting transfers between devices  40.5 us (28%)
  Pallas kernels  16.9 us (12%)
  blocking collectives  9.07 us (6%)
  other arithmetic  5.98 us (4%)
  local copies, waits for them, and re-layouts  5.32 us (4%)
    ppermute x20, waiting for transfers between devices, swap(): lax.ppermute(x, axis, [(i, i ^ step) for i in range(lax.axis_size(axis))])  65.7 us
    ppermute x20, starting transfers between devices, swap(): lax.ppermute(x, axis, [(i, i ^ step) for i in range(lax.axis_size(axis))])  38.2 us
    pallas_call x2, Pallas kernels, outer_half(): pl.pallas_call(near_kernel if done is None else far_kernel, out_shape=out...  12.7 us
    all_to_all x1, blocking collectives, local_pairs(): lax.all_to_all(message, PLANE, split_axis=0, concat_axis=0, tiled=True)  9.07 us
    pallas_call x2, Pallas kernels, rotate(): pl.pallas_call(rotate_kernel, out_shape=(jax.ShapeDtypeStruct((rows, cols...  4.11 us
  transfers between devices with their start and end apart: 22, of which 7 were waited for; matrix products, arithmetic and copies ran while one was open for 4% of the time, Pallas kernels for 7%

profile of v3, /device:TPU:0, one launch (start us, length us, event | category | flops | bytes accessed | tf_op | source)
XLA Modules:
  0.0 144.4 jit_solution(11120419065667234591)
XLA Ops:
  0.6 1.1 dynamic_slice.39
  1.7 3.0 %collective-permute-start.9 = (bf16[512,512]{1,0:T(8,128)(2,1)S(1)}, bf16[512,512]{1,0:T(8,128)(2,1)S(1)}, u32[]{:S(2)}, u32[]{:S(2)}) collective-permute-start(bf16[512,512]{1,0:T(8,128)(2,1)S(1)} %dynamic_slice.39), channel_id=1, source_target_pairs={{0,2},{2,0},{1,3},{3,1},{4,6},{6,4},{5,7},{7,5},{8,10},{10,8},{9,1... | collective-permute-start | bytes 1572872 | tf_op jit(solution)/shard_map/ppermute | solution.py:110
  4.7 11.9 %collective-permute-done.9 = bf16[512,512]{1,0:T(8,128)(2,1)S(1)} collective-permute-done((bf16[512,512]{1,0:T(8,128)(2,1)S(1)}, bf16[512,512]{1,0:T(8,128)(2,1)S(1)}, u32[]{:S(2)}, u32[]{:S(2)}) %collective-permute-start.9) | collective-permute-done | bytes 524320 | tf_op jit(solution)/shard_map/ppermute | solution.py:110
  16.7 1.8 %collective-permute-start.10 = (bf16[512,512]{1,0:T(8,128)(2,1)S(1)}, bf16[512,512]{1,0:T(8,128)(2,1)S(1)}, u32[]{:S(2)}, u32[]{:S(2)}) collective-permute-start(bf16[512,512]{1,0:T(8,128)(2,1)S(1)} %collective-permute-done.9), channel_id=1, source_target_pairs={{0,16},{16,0},{1,17},{17,1},{2,18},{18,2},{3,19},{19,3},{4,20},{20... | collective-permute-start | bytes 1572872 | tf_op jit(solution)/shard_map/ppermute | solution.py:110
  18.4 1.6 %collective-permute-start = (bf16[128,1024]{1,0:T(8,128)(2,1)}, bf16[128,1024]{1,0:T(8,128)(2,1)S(1)}, u32[]{:S(2)}, u32[]{:S(2)}) collective-permute-start(bf16[128,1024]{1,0:T(8,128)(2,1)} %param.8), channel_id=1, source_target_pairs={{0,0},{1,4},{2,8},{3,12},{4,2},{5,6},{6,10},{7,14},{8,1},{9,5},{10... | collective-permute-start | bytes 786440 | tf_op jit(solution)/shard_map/ppermute | solution.py:261
  20.0 3.3 %collective-permute-start.2 = (s32[128]{0:T(128)}, s32[128]{0:T(128)S(1)}, u32[]{:S(2)}, u32[]{:S(2)}) collective-permute-start(s32[128]{0:T(128)} %param.9), channel_id=1, source_target_pairs={{0,4},{4,0},{8,12},{12,8},{1,5},{5,1},{9,13},{13,9},{2,6},{6,2},{1... | collective-permute-start | bytes 1544 | tf_op jit(solution)/shard_map/ppermute | solution.py:110
  23.3 1.2 collective-permute-start.3
  24.6 1.2 collective-permute-start.4
  25.8 1.3 dynamic-slice_bitcast_fusion
  27.1 6.8 %collective-permute-start.1 = (bf16[128,1024]{1,0:T(8,128)(2,1)S(1)}, bf16[128,1024]{1,0:T(8,128)(2,1)S(1)}, u32[]{:S(2)}, u32[]{:S(2)}) collective-permute-start(bf16[128,1024]{1,0:T(8,128)(2,1)S(1)} %collective-permute-done.x0), channel_id=1, source_target_pairs={{0,1},{1,0},{2,3},{3,2},{4,5},{5,4},{6,7},{7,6},{8,9},{9,8},{10,11... | collective-permute-start | bytes 786440 | tf_op jit(solution)/shard_map/ppermute | solution.py:110
  33.9 0.0 collective-permute-done.10
  33.9 0.1 broadcast_select_fusion.1
  34.0 0.1 maximum_bitcast_fusion
  34.1 0.0 copy-start.9
  34.1 0.0 copy-start.10
  34.1 0.0 copy-start.11
  34.1 0.0 copy-start
  34.1 1.5 %fusion.1 = (bf16[2,1024,256]{2,1,0:T(8,128)(2,1)}, bf16[2,1024,256]{2,1,0:T(8,128)(2,1)}) fusion(s32[]{:T(128)S(6)} %select_n.67, bf16[1,1024,512]{2,1,0:T(8,128)(2,1)S(1)} %dynamic-slice_bitcast_fusion, bf16[1,1024,512]{2,1,0:T(8,128)(2,1)S(1)} %maximum_bitcast_fusion, s32[]{:T(128)S(6)} %select_n.68), kind=kLoop, calls=%fused_computation.6 | loop fusion | flops 4194304 | bytes 4194312 | tf_op jit(solution)/shard_map/stack | solution.py:272
  35.6 0.0 collective-permute-start.11
  35.7 0.1 collective-permute-start.17
  35.7 0.0 collective-permute-done.1.x2
  35.8 0.7 collective-permute-start.5
  36.5 8.0 %collective-permute-done.17.x1 = bf16[128,1024]{1,0:T(8,128)(2,1)S(1)} collective-permute-done((bf16[128,1024]{1,0:T(8,128)(2,1)S(1)}, bf16[128,1024]{1,0:T(8,128)(2,1)S(1)}, u32[]{:S(2)}, u32[]{:S(2)}) %collective-permute-start.17) | collective-permute-done | bytes 262176 | tf_op jit(solution)/shard_map/ppermute | solution.py:110
  44.4 0.0 collective-permute-start.18
  44.4 0.0 collective-permute-done.5.x0
  44.4 6.4 %collective-permute-start.6 = (bf16[128,1024]{1,0:T(8,128)(2,1)S(1)}, bf16[128,1024]{1,0:T(8,128)(2,1)S(1)}, u32[]{:S(2)}, u32[]{:S(2)}) collective-permute-start(bf16[128,1024]{1,0:T(8,128)(2,1)S(1)} %collective-permute-done.5.x0), channel_id=1, source_target_pairs={{0,2},{2,0},{1,3},{3,1},{4,6},{6,4},{5,7},{7,5},{8,10},{10,8},{9,1... | collective-permute-start | bytes 786440 | tf_op jit(solution)/shard_map/ppermute | solution.py:110
  50.8 0.1 pad_add_fusion.3.order
  50.9 0.0 collective-permute-done.18.x3
  50.9 2.3 %rotate.3 = (bf16[512,512]{1,0:T(8,128)(2,1)S(1)}, f32[512,512]{1,0:T(8,128)S(1)}) custom-call(s32[4]{0:T(128)S(1)} %pad_add_fusion.3.order, bf16[128,1024]{1,0:T(8,128)(2,1)S(1)} %collective-permute-done.x0, bf16[128,1024]{1,0:T(8,128)(2,1)S(1)} %collective-permute-done.17.x1, bf16[128,1024]{1,0:T(8,128)(2,1)S(1)} %collective-permute-done.1.x2, ...), custom_call_target="tpu_custom_call" | custom-call | flops 1073741824 | bytes 2097152 | tf_op jit(solution)/shard_map/rotate/pallas_call | solution.py:135
  53.2 4.8 %collective-permute-start.19 = (bf16[512,512]{1,0:T(8,128)(2,1)S(1)}, bf16[512,512]{1,0:T(8,128)(2,1)S(1)}, u32[]{:S(2)}, u32[]{:S(2)}) collective-permute-start(bf16[512,512]{1,0:T(8,128)(2,1)S(1)} %get-tuple-element.23), channel_id=1, source_target_pairs={{0,4},{4,0},{8,12},{12,8},{1,5},{5,1},{9,13},{13,9},{2,6},{6,2},{1... | collective-permute-start | bytes 1572872 | tf_op jit(solution)/shard_map/ppermute | solution.py:110
  58.0 0.2 collective-permute-start.7
  58.2 0.0 collective-permute-done.6.x1
  58.2 2.2 %collective-permute-start.8 = (bf16[128,1024]{1,0:T(8,128)(2,1)S(1)}, bf16[128,1024]{1,0:T(8,128)(2,1)S(1)}, u32[]{:S(2)}, u32[]{:S(2)}) collective-permute-start(bf16[128,1024]{1,0:T(8,128)(2,1)S(1)} %collective-permute-done.6.x1), channel_id=1, source_target_pairs={{0,1},{1,0},{2,3},{3,2},{4,5},{5,4},{6,7},{7,6},{8,9},{9,8},{10,11... | collective-permute-start | bytes 786440 | tf_op jit(solution)/shard_map/ppermute | solution.py:110
  60.4 0.1 slice_bitcast_fusion.3
  60.5 1.3 slice_bitcast_fusion.2
  61.8 0.3 pad_maximum_fusion.basis
  62.1 0.0 collective-permute-done.7.x2
  62.1 1.8 %rotate.2 = (bf16[512,512]{1,0:T(8,128)(2,1)S(1)}, f32[512,512]{1,0:T(8,128)S(1)}) custom-call(s32[4]{0:T(128)S(1)} %broadcast_xor_fusion.order, bf16[128,1024]{1,0:T(8,128)(2,1)S(1)} %collective-permute-done.5.x0, bf16[128,1024]{1,0:T(8,128)(2,1)S(1)} %collective-permute-done.6.x1, bf16[128,1024]{1,0:T(8,128)(2,1)S(1)} %collective-permute-done.7.x2, ...), custom_call_target="tpu_custom_call" | custom-call | flops 1073741824 | bytes 2097152 | tf_op jit(solution)/shard_map/rotate/pallas_call | solution.py:135
  63.9 2.4 %collective-permute-start.12 = (bf16[512,512]{1,0:T(8,128)(2,1)S(1)}, bf16[512,512]{1,0:T(8,128)(2,1)S(1)}, u32[]{:S(2)}, u32[]{:S(2)}) collective-permute-start(bf16[512,512]{1,0:T(8,128)(2,1)S(1)} %get-tuple-element.20), channel_id=1, source_target_pairs={{0,4},{4,0},{8,12},{12,8},{1,5},{5,1},{9,13},{13,9},{2,6},{6,2},{1... | collective-permute-start | bytes 1572872 | tf_op jit(solution)/shard_map/ppermute | solution.py:110
  66.3 4.1 %collective-permute-done.19 = bf16[512,512]{1,0:T(8,128)(2,1)S(1)} collective-permute-done((bf16[512,512]{1,0:T(8,128)(2,1)S(1)}, bf16[512,512]{1,0:T(8,128)(2,1)S(1)}, u32[]{:S(2)}, u32[]{:S(2)}) %collective-permute-start.19) | collective-permute-done | bytes 524320 | tf_op jit(solution)/shard_map/ppermute | solution.py:110
  70.4 0.2 add_convert_fusion.1
  70.5 1.5 %collective-permute-start.20 = (bf16[512,512]{1,0:T(8,128)(2,1)S(1)}, bf16[512,512]{1,0:T(8,128)(2,1)S(1)}, u32[]{:S(2)}, u32[]{:S(2)}) collective-permute-start(bf16[512,512]{1,0:T(8,128)(2,1)S(1)} %add_convert_fusion.1), channel_id=1, source_target_pairs={{0,8},{4,12},{8,0},{12,4},{1,9},{5,13},{9,1},{13,5},{2,10},{6,14},... | collective-permute-start | bytes 1572872 | tf_op jit(solution)/shard_map/ppermute | solution.py:110
  72.0 15.7 %collective-permute-done.12 = bf16[512,512]{1,0:T(8,128)(2,1)S(1)} collective-permute-done((bf16[512,512]{1,0:T(8,128)(2,1)S(1)}, bf16[512,512]{1,0:T(8,128)(2,1)S(1)}, u32[]{:S(2)}, u32[]{:S(2)}) %collective-permute-start.12) | collective-permute-done | bytes 524320 | tf_op jit(solution)/shard_map/ppermute | solution.py:110
  87.7 0.1 add_convert_fusion.3
  87.8 3.1 %collective-permute-start.13 = (bf16[512,256]{1,0:T(8,128)(2,1)S(1)}, bf16[512,256]{1,0:T(8,128)(2,1)S(1)}, u32[]{:S(2)}, u32[]{:S(2)}) collective-permute-start(bf16[512,256]{1,0:T(8,128)(2,1)S(1)} %add_convert_fusion.3), channel_id=1, source_target_pairs={{0,8},{4,12},{8,0},{12,4},{1,9},{5,13},{9,1},{13,5},{2,10},{6,14},... | collective-permute-start | bytes 786440 | tf_op jit(solution)/shard_map/ppermute | solution.py:110
  90.9 17.8 %collective-permute-done.13 = bf16[512,256]{1,0:T(8,128)(2,1)S(1)} collective-permute-done((bf16[512,256]{1,0:T(8,128)(2,1)S(1)}, bf16[512,256]{1,0:T(8,128)(2,1)S(1)}, u32[]{:S(2)}, u32[]{:S(2)}) %collective-permute-start.13) | collective-permute-done | bytes 262176 | tf_op jit(solution)/shard_map/ppermute | solution.py:110
  108.7 0.1 add_convert_fusion.2.a0
  108.8 0.1 collective-permute-start.14
  108.9 0.1 add_convert_fusion.g
  109.1 0.1 collective-permute-start.21
  109.2 0.6 pad_add_fusion.2.place
  109.8 0.0 collective-permute-start.15
  109.8 7.3 %collective-permute-done.14.a1 = bf16[512,256]{1,0:T(8,128)(2,1)S(1)} collective-permute-done((bf16[512,256]{1,0:T(8,128)(2,1)S(1)}, bf16[512,256]{1,0:T(8,128)(2,1)S(1)}, u32[]{:S(2)}, u32[]{:S(2)}) %collective-permute-start.14) | collective-permute-done | bytes 262176 | tf_op jit(solution)/shard_map/ppermute | solution.py:110
  117.1 0.6 pad_add_fusion.1.place
  117.8 0.9 collective-permute-done.16.a3
  118.7 0.7 copy-done.7
  119.4 6.7 %outer_half.2 = (f32[1024,1024]{1,0:T(8,128)}, f32[512,128]{1,0:T(8,128)}, bf16[512,1024]{1,0:T(8,128)(2,1)}, bf16[1024,512]{1,0:T(8,128)(2,1)}) custom-call(s32[2]{0:T(128)} %pad_add_fusion.2.place, bf16[512,256]{1,0:T(8,128)(2,1)} %copy-done.3, bf16[512,256]{1,0:T(8,128)(2,1)} %copy-done.5, bf16[512,256]{1,0:T(8,128)(2,1)} %copy-done.6, ...), custom_call_target="tpu_custom_call" | custom-call | flops 1073741824 | bytes 4194304 | tf_op jit(solution)/shard_map/outer_half/pallas_call | solution.py:226
  126.1 0.8 copy-done.4
  126.9 6.1 %outer_half.3 = (f32[1024,1024]{1,0:T(8,128)}, f32[512,128]{1,0:T(8,128)}) custom-call(s32[2]{0:T(128)} %pad_add_fusion.1.place, bf16[512,1024]{1,0:T(8,128)(2,1)} %get-tuple-element.24.flat, bf16[1024,512]{1,0:T(8,128)(2,1)} %get-tuple-element.25.turned, bf16[512,512]{1,0:T(8,128)(2,1)} %copy-done.4, ...), custom_call_target="tpu_custom_call", output_to_operand_aliasing={{0}: (5, {})} | custom-call | flops 1073741824 | bytes 4194304 | tf_op jit(solution)/shard_map/outer_half/pallas_call | solution.py:226
  133.0 1.1 add_reduce_fusion
  134.1 0.1 select_reduce_fusion
  134.3 9.1 %all_to_all.9 = f32[16,1,136]{2,1,0:T(1,128)S(1)} all-to-all(f32[16,1,136]{2,1,0:T(1,128)S(1)} %all_to_all.6), channel_id=1, replica_groups=mesh['grp'=2,'seq'=4,'row'=2,'col'=2] {'seq','row','col'}, dimensions={0} | all-to-all | bytes 17408 | tf_op jit(solution)/shard_map/all_to_all | solution.py:312
  143.4 0.5 slice_multiply_fusion
  143.9 0.5 slice_multiply_fusion.1
  (38 shorter events, 0.2 us)
Async XLA Ops:
  1.7 14.9 %collective-permute-start.9 = (bf16[512,512]{1,0:T(8,128)(2,1)S(1)}, bf16[512,512]{1,0:T(8,128)(2,1)S(1)}, u32[]{:S(2)}, u32[]{:S(2)}) collective-permute-start(bf16[512,512]{1,0:T(8,128)(2,1)S(1)} %dynamic_slice.39), channel_id=1, source_target_pairs={{0,2},{2,0},{1,3},{3,1},{4,6},{6,4},{5,7},{7,5},{8,10},{10,8},{9,1... | collective-permute-start | bytes 1572872 | tf_op jit(solution)/shard_map/ppermute | solution.py:110
  16.7 17.3 %collective-permute-start.10 = (bf16[512,512]{1,0:T(8,128)(2,1)S(1)}, bf16[512,512]{1,0:T(8,128)(2,1)S(1)}, u32[]{:S(2)}, u32[]{:S(2)}) collective-permute-start(bf16[512,512]{1,0:T(8,128)(2,1)S(1)} %collective-permute-done.9), channel_id=1, source_target_pairs={{0,16},{16,0},{1,17},{17,1},{2,18},{18,2},{3,19},{19,3},{4,20},{20... | collective-permute-start | bytes 1572872 | tf_op jit(solution)/shard_map/ppermute | solution.py:110
  18.4 8.7 %collective-permute-start = (bf16[128,1024]{1,0:T(8,128)(2,1)}, bf16[128,1024]{1,0:T(8,128)(2,1)S(1)}, u32[]{:S(2)}, u32[]{:S(2)}) collective-permute-start(bf16[128,1024]{1,0:T(8,128)(2,1)} %param.8), channel_id=1, source_target_pairs={{0,0},{1,4},{2,8},{3,12},{4,2},{5,6},{6,10},{7,14},{8,1},{9,5},{10... | collective-permute-start | bytes 786440 | tf_op jit(solution)/shard_map/ppermute | solution.py:261
  20.0 15.6 %collective-permute-start.2 = (s32[128]{0:T(128)}, s32[128]{0:T(128)S(1)}, u32[]{:S(2)}, u32[]{:S(2)}) collective-permute-start(s32[128]{0:T(128)} %param.9), channel_id=1, source_target_pairs={{0,4},{4,0},{8,12},{12,8},{1,5},{5,1},{9,13},{13,9},{2,6},{6,2},{1... | collective-permute-start | bytes 1544 | tf_op jit(solution)/shard_map/ppermute | solution.py:110
  23.3 12.3 %collective-permute-start.3 = (s32[128]{0:T(128)}, s32[128]{0:T(128)S(1)}, u32[]{:S(2)}, u32[]{:S(2)}) collective-permute-start(s32[128]{0:T(128)} %param.9), channel_id=1, source_target_pairs={{0,8},{4,12},{8,0},{12,4},{1,9},{5,13},{9,1},{13,5},{2,10},{6,14},... | collective-permute-start | bytes 1544 | tf_op jit(solution)/shard_map/ppermute | solution.py:110
  24.6 11.1 %collective-permute-start.4 = (s32[128]{0:T(128)}, s32[128]{0:T(128)S(1)}, u32[]{:S(2)}, u32[]{:S(2)}) collective-permute-start(s32[128]{0:T(128)} %param.9), channel_id=1, source_target_pairs={{0,12},{4,8},{8,4},{12,0},{1,13},{5,9},{9,5},{13,1},{2,14},{6,10},... | collective-permute-start | bytes 1544 | tf_op jit(solution)/shard_map/ppermute | solution.py:110
  27.1 8.6 %collective-permute-start.1 = (bf16[128,1024]{1,0:T(8,128)(2,1)S(1)}, bf16[128,1024]{1,0:T(8,128)(2,1)S(1)}, u32[]{:S(2)}, u32[]{:S(2)}) collective-permute-start(bf16[128,1024]{1,0:T(8,128)(2,1)S(1)} %collective-permute-done.x0), channel_id=1, source_target_pairs={{0,1},{1,0},{2,3},{3,2},{4,5},{5,4},{6,7},{7,6},{8,9},{9,8},{10,11... | collective-permute-start | bytes 786440 | tf_op jit(solution)/shard_map/ppermute | solution.py:110
  34.1 1.5 %copy-start.9 = (s32[128]{0:T(128)S(1)}, s32[128]{0:T(128)}, u32[]{:S(2)}) copy-start(s32[128]{0:T(128)} %param.9) | copy-start | bytes 1540
  34.1 1.7 %copy-start.10 = (bf16[128,1024]{1,0:T(8,128)(2,1)S(1)}, bf16[128,1024]{1,0:T(8,128)(2,1)}, u32[]{:S(2)}) copy-start(bf16[128,1024]{1,0:T(8,128)(2,1)} %param.7) | copy-start | bytes 786436
  34.1 16.7 %copy-start.11 = (s32[4]{0:T(128)S(1)}, s32[4]{0:T(128)}, u32[]{:S(2)}) copy-start(s32[4]{0:T(128)} %constant.68.clone) | copy-start | bytes 52
  34.1 16.8 %copy-start = (bf16[1024,1024]{1,0:T(8,128)(2,1)S(1)}, bf16[1024,1024]{1,0:T(8,128)(2,1)}, u32[]{:S(2)}) copy-start(bf16[1024,1024]{1,0:T(8,128)(2,1)} %basis.1) | copy-start | bytes 6291460
  35.6 24.9 %collective-permute-start.11 = (bf16[2,1024,256]{2,1,0:T(8,128)(2,1)}, bf16[2,1024,256]{2,1,0:T(8,128)(2,1)}, u32[]{:S(2)}, u32[]{:S(2)}) collective-permute-start(bf16[2,1024,256]{2,1,0:T(8,128)(2,1)} %get-tuple-element.32), channel_id=1, source_target_pairs={{0,1},{1,0},{2,3},{3,2},{4,5},{5,4},{6,7},{7,6},{8,9},{9,8},{10,11... | collective-permute-start | bytes 3145736 | tf_op jit(solution)/shard_map/ppermute | solution.py:110
  35.7 8.8 %collective-permute-start.17 = (bf16[128,1024]{1,0:T(8,128)(2,1)S(1)}, bf16[128,1024]{1,0:T(8,128)(2,1)S(1)}, u32[]{:S(2)}, u32[]{:S(2)}) collective-permute-start(bf16[128,1024]{1,0:T(8,128)(2,1)S(1)} %collective-permute-done.x0), channel_id=1, source_target_pairs={{0,2},{2,0},{1,3},{3,1},{4,6},{6,4},{5,7},{7,5},{8,10},{10,8},{9,1... | collective-permute-start | bytes 786440 | tf_op jit(solution)/shard_map/ppermute | solution.py:110
  35.8 8.7 %collective-permute-start.5 = (bf16[128,1024]{1,0:T(8,128)(2,1)S(1)}, bf16[128,1024]{1,0:T(8,128)(2,1)S(1)}, u32[]{:S(2)}, u32[]{:S(2)}) collective-permute-start(bf16[128,1024]{1,0:T(8,128)(2,1)S(1)} %copy-done.10), channel_id=1, source_target_pairs={{0,0},{1,4},{2,8},{3,12},{4,2},{5,6},{6,10},{7,14},{8,1},{9,5},{10... | collective-permute-start | bytes 786440 | tf_op jit(solution)/shard_map/ppermute | solution.py:261
  44.4 6.5 %collective-permute-start.18 = (bf16[128,1024]{1,0:T(8,128)(2,1)S(1)}, bf16[128,1024]{1,0:T(8,128)(2,1)}, u32[]{:S(2)}, u32[]{:S(2)}) collective-permute-start(bf16[128,1024]{1,0:T(8,128)(2,1)S(1)} %collective-permute-done.17.x1), channel_id=1, source_target_pairs={{0,1},{1,0},{2,3},{3,2},{4,5},{5,4},{6,7},{7,6},{8,9},{9,8},{10,11... | collective-permute-start | bytes 786440 | tf_op jit(solution)/shard_map/ppermute | solution.py:110
  44.4 13.7 %collective-permute-start.6 = (bf16[128,1024]{1,0:T(8,128)(2,1)S(1)}, bf16[128,1024]{1,0:T(8,128)(2,1)S(1)}, u32[]{:S(2)}, u32[]{:S(2)}) collective-permute-start(bf16[128,1024]{1,0:T(8,128)(2,1)S(1)} %collective-permute-done.5.x0), channel_id=1, source_target_pairs={{0,2},{2,0},{1,3},{3,1},{4,6},{6,4},{5,7},{7,5},{8,10},{10,8},{9,1... | collective-permute-start | bytes 786440 | tf_op jit(solution)/shard_map/ppermute | solution.py:110
  50.8 9.6 %copy-start.1 = (bf16[2,1024,256]{2,1,0:T(8,128)(2,1)S(1)}, bf16[2,1024,256]{2,1,0:T(8,128)(2,1)}, u32[]{:S(2)}) copy-start(bf16[2,1024,256]{2,1,0:T(8,128)(2,1)} %get-tuple-element.31) | copy-start | bytes 3145732
  53.2 17.2 %collective-permute-start.19 = (bf16[512,512]{1,0:T(8,128)(2,1)S(1)}, bf16[512,512]{1,0:T(8,128)(2,1)S(1)}, u32[]{:S(2)}, u32[]{:S(2)}) collective-permute-start(bf16[512,512]{1,0:T(8,128)(2,1)S(1)} %get-tuple-element.23), channel_id=1, source_target_pairs={{0,4},{4,0},{8,12},{12,8},{1,5},{5,1},{9,13},{13,9},{2,6},{6,2},{1... | collective-permute-start | bytes 1572872 | tf_op jit(solution)/shard_map/ppermute | solution.py:110
  58.0 4.1 %collective-permute-start.7 = (bf16[128,1024]{1,0:T(8,128)(2,1)S(1)}, bf16[128,1024]{1,0:T(8,128)(2,1)S(1)}, u32[]{:S(2)}, u32[]{:S(2)}) collective-permute-start(bf16[128,1024]{1,0:T(8,128)(2,1)S(1)} %collective-permute-done.5.x0), channel_id=1, source_target_pairs={{0,1},{1,0},{2,3},{3,2},{4,5},{5,4},{6,7},{7,6},{8,9},{9,8},{10,11... | collective-permute-start | bytes 786440 | tf_op jit(solution)/shard_map/ppermute | solution.py:110
  58.2 3.9 %collective-permute-start.8 = (bf16[128,1024]{1,0:T(8,128)(2,1)S(1)}, bf16[128,1024]{1,0:T(8,128)(2,1)S(1)}, u32[]{:S(2)}, u32[]{:S(2)}) collective-permute-start(bf16[128,1024]{1,0:T(8,128)(2,1)S(1)} %collective-permute-done.6.x1), channel_id=1, source_target_pairs={{0,1},{1,0},{2,3},{3,2},{4,5},{5,4},{6,7},{7,6},{8,9},{9,8},{10,11... | collective-permute-start | bytes 786440 | tf_op jit(solution)/shard_map/ppermute | solution.py:110
  63.9 23.8 %collective-permute-start.12 = (bf16[512,512]{1,0:T(8,128)(2,1)S(1)}, bf16[512,512]{1,0:T(8,128)(2,1)S(1)}, u32[]{:S(2)}, u32[]{:S(2)}) collective-permute-start(bf16[512,512]{1,0:T(8,128)(2,1)S(1)} %get-tuple-element.20), channel_id=1, source_target_pairs={{0,4},{4,0},{8,12},{12,8},{1,5},{5,1},{9,13},{13,9},{2,6},{6,2},{1... | collective-permute-start | bytes 1572872 | tf_op jit(solution)/shard_map/ppermute | solution.py:110
  70.5 38.4 %collective-permute-start.20 = (bf16[512,512]{1,0:T(8,128)(2,1)S(1)}, bf16[512,512]{1,0:T(8,128)(2,1)S(1)}, u32[]{:S(2)}, u32[]{:S(2)}) collective-permute-start(bf16[512,512]{1,0:T(8,128)(2,1)S(1)} %add_convert_fusion.1), channel_id=1, source_target_pairs={{0,8},{4,12},{8,0},{12,4},{1,9},{5,13},{9,1},{13,5},{2,10},{6,14},... | collective-permute-start | bytes 1572872 | tf_op jit(solution)/shard_map/ppermute | solution.py:110
  87.8 20.9 %collective-permute-start.13 = (bf16[512,256]{1,0:T(8,128)(2,1)S(1)}, bf16[512,256]{1,0:T(8,128)(2,1)S(1)}, u32[]{:S(2)}, u32[]{:S(2)}) collective-permute-start(bf16[512,256]{1,0:T(8,128)(2,1)S(1)} %add_convert_fusion.3), channel_id=1, source_target_pairs={{0,8},{4,12},{8,0},{12,4},{1,9},{5,13},{9,1},{13,5},{2,10},{6,14},... | collective-permute-start | bytes 786440 | tf_op jit(solution)/shard_map/ppermute | solution.py:110
  108.8 9.8 %copy-start.3 = (bf16[512,256]{1,0:T(8,128)(2,1)}, bf16[512,256]{1,0:T(8,128)(2,1)S(1)}, u32[]{:S(2)}) copy-start(bf16[512,256]{1,0:T(8,128)(2,1)S(1)} %add_convert_fusion.2.a0) | copy-start | bytes 786436
  108.8 8.3 %collective-permute-start.14 = (bf16[512,256]{1,0:T(8,128)(2,1)S(1)}, bf16[512,256]{1,0:T(8,128)(2,1)S(1)}, u32[]{:S(2)}, u32[]{:S(2)}) collective-permute-start(bf16[512,256]{1,0:T(8,128)(2,1)S(1)} %add_convert_fusion.2.a0), channel_id=1, source_target_pairs={{0,2},{2,0},{1,3},{3,1},{4,6},{6,4},{5,7},{7,5},{8,10},{10,8},{9,1... | collective-permute-start | bytes 786440 | tf_op jit(solution)/shard_map/ppermute | solution.py:110
  109.1 9.6 %copy-start.2 = (bf16[512,512]{1,0:T(8,128)(2,1)}, bf16[512,512]{1,0:T(8,128)(2,1)S(1)}, u32[]{:S(2)}) copy-start(bf16[512,512]{1,0:T(8,128)(2,1)S(1)} %add_convert_fusion.g) | copy-start | bytes 1572868
  109.1 17.0 %collective-permute-start.21 = (bf16[512,512]{1,0:T(8,128)(2,1)S(1)}, bf16[512,512]{1,0:T(8,128)(2,1)S(1)}, u32[]{:S(2)}, u32[]{:S(2)}) collective-permute-start(bf16[512,512]{1,0:T(8,128)(2,1)S(1)} %add_convert_fusion.g), channel_id=1, source_target_pairs={{0,4},{4,0},{8,12},{12,8},{1,5},{5,1},{9,13},{13,9},{2,6},{6,2},{1... | collective-permute-start | bytes 1572872 | tf_op jit(solution)/shard_map/ppermute | solution.py:110
  109.8 8.0 %collective-permute-start.15 = (bf16[512,256]{1,0:T(8,128)(2,1)S(1)}, bf16[512,256]{1,0:T(8,128)(2,1)S(1)}, u32[]{:S(2)}, u32[]{:S(2)}) collective-permute-start(bf16[512,256]{1,0:T(8,128)(2,1)S(1)} %add_convert_fusion.2.a0), channel_id=1, source_target_pairs={{0,1},{1,0},{2,3},{3,2},{4,5},{5,4},{6,7},{7,6},{8,9},{9,8},{10,11... | collective-permute-start | bytes 786440 | tf_op jit(solution)/shard_map/ppermute | solution.py:110
  117.1 1.5 %copy-start.5 = (bf16[512,256]{1,0:T(8,128)(2,1)}, bf16[512,256]{1,0:T(8,128)(2,1)S(1)}, u32[]{:S(2)}) copy-start(bf16[512,256]{1,0:T(8,128)(2,1)S(1)} %collective-permute-done.14.a1) | copy-start | bytes 786436
  117.1 1.5 %collective-permute-start.16 = (bf16[512,256]{1,0:T(8,128)(2,1)S(1)}, bf16[512,256]{1,0:T(8,128)(2,1)S(1)}, u32[]{:S(2)}, u32[]{:S(2)}) collective-permute-start(bf16[512,256]{1,0:T(8,128)(2,1)S(1)} %collective-permute-done.14.a1), channel_id=1, source_target_pairs={{0,1},{1,0},{2,3},{3,2},{4,5},{5,4},{6,7},{7,6},{8,9},{9,8},{10,11... | collective-permute-start | bytes 786440 | tf_op jit(solution)/shard_map/ppermute | solution.py:110
  117.8 0.9 copy-start.6
  118.7 0.7 copy-start.7
  126.1 0.8 copy-start.4
  126.9 6.1 %copy-start.8 = (f32[512,128]{1,0:T(8,128)S(1)}, f32[512,128]{1,0:T(8,128)}, u32[]{:S(2)}) copy-start(f32[512,128]{1,0:T(8,128)} %get-tuple-element.28) | copy-start | bytes 786436

commit v4 on v1

--- a/solution.py
+++ b/solution.py
@@ -1,6 +1,10 @@
+import functools
+
 import jax
 import jax.numpy as jnp
 from jax import lax
+from jax.experimental import pallas as pl
+from jax.experimental.pallas import tpu as pltpu
 from jax.sharding import PartitionSpec as P
 
 SOURCES = 8
@@ -11,7 +15,7 @@
     return lax.ppermute(x, PLANE, pairs)
 
 
-def local(acts, grads, source_ids, basis_in, basis_out, eigvals):
+def local_any(acts, grads, source_ids, basis_in, basis_out, eigvals):
     seqs, rows, cols = (lax.axis_size(name) for name in PLANE)
     s = lax.axis_index("seq")
     tok = acts.shape[0]
@@ -101,6 +105,320 @@
     return (precond, scores, influence)
 
 
+VMEM = 16 * 2**20
+ROTATE_VMEM = 10 * 2**20
+LANES = 128
+STAND = 2 * 10**10
+BLOCKS = 4
+
+
+def swap(x, axis, step=1):
+    return lax.ppermute(x, axis, [(i, i ^ step) for i in range(lax.axis_size(axis))])
+
+
+def stand_kernel(x, out):
+    out[...] = x[...]
+
+
+def stand(token, *values):
+    token, *values = lax.optimization_barrier((token, *values))
+    vmem = pl.BlockSpec(memory_space=pltpu.VMEM)
+    token = pl.pallas_call(
+        stand_kernel,
+        out_shape=jax.ShapeDtypeStruct(token.shape, token.dtype),
+        in_specs=[vmem],
+        out_specs=vmem,
+        compiler_params=pltpu.CompilerParams(vmem_limit_bytes=2**20),
+        cost_estimate=pl.CostEstimate(flops=STAND, bytes_accessed=0, transcendentals=0),
+        name="stand",
+    )(token)
+    return token, *values
+
+
+def added(a, b):
+    return a.astype(jnp.float32) + b.astype(jnp.float32)
+
+
+def rotate_kernel(x0, x1, x2, x3, basis, *refs, notes, flips):
+    note, (*sends, keep, rows) = refs[:notes], refs[notes:]
+    tok = x0.shape[0]
+    for j, x in enumerate((x0, x1, x2, x3)):
+        rows[pl.ds(j * tok, tok), :] = x[...]
+    at = 0
+    for i, out in enumerate((*sends, keep)):
+        cut = out.shape[1]
+        block = jnp.dot(rows[...], basis[:, at : at + cut], preferred_element_type=jnp.float32)
+        for j in range(4):
+            k = j ^ (i in flips)
+            out[j * tok : (j + 1) * tok, :] = block[k * tok : (k + 1) * tok, :].astype(out.dtype)
+        at += cut
+    if note:
+        sends[0][rows.shape[0] :, :] = note[0][...]
+
+
+def rotate(slots, basis, messages, *note, flips=()):
+    tok, depth = slots[0].shape
+    rows, cols = tok * len(slots), basis.shape[1]
+    cut = cols // (messages + 1)
+    vmem = pl.BlockSpec(memory_space=pltpu.VMEM)
+    return pl.pallas_call(
+        functools.partial(rotate_kernel, notes=len(note), flips=flips),
+        out_shape=[jax.ShapeDtypeStruct((rows + sum(n.shape[0] for n in note), cut), jnp.bfloat16)] * messages
+        + [jax.ShapeDtypeStruct((rows, cut), jnp.float32)],
+        in_specs=[vmem] * (5 + len(note)),
+        out_specs=[vmem] * (messages + 1),
+        scratch_shapes=[pltpu.VMEM((rows, depth), jnp.bfloat16)],
+        compiler_params=pltpu.CompilerParams(vmem_limit_bytes=ROTATE_VMEM),
+        cost_estimate=pl.CostEstimate(flops=2 * rows * depth * cols, bytes_accessed=2 * depth * cols, transcendentals=0),
+        name="rotate",
+    )(*slots, basis, *note)
+
+
+def pair_kernel(keep, got, note, out):
+    count = keep.shape[0]
+    out[:count, :] = (keep[...] + got[:count, :].astype(jnp.float32)).astype(jnp.bfloat16)
+    row = lax.broadcasted_iota(jnp.int32, note.shape, 0)
+    theirs = jnp.broadcast_to(got[count : count + 1, :].astype(jnp.float32), note.shape)
+    out[count:, :] = jnp.where(row == 1, theirs, note[...].astype(jnp.float32)).astype(jnp.bfloat16)
+
+
+def sum_kernel(pair, across, out):
+    count = out.shape[0]
+    out[...] = added(pair[:count, :], across[:count, :]).astype(jnp.bfloat16)
+
+
+def small_call(kernel, rows, *args):
+    vmem = pl.BlockSpec(memory_space=pltpu.VMEM)
+    shape = (rows, args[0].shape[1])
+    return pl.pallas_call(
+        kernel,
+        out_shape=jax.ShapeDtypeStruct(shape, jnp.bfloat16),
+        in_specs=[vmem] * len(args),
+        out_specs=vmem,
+        compiler_params=pltpu.CompilerParams(vmem_limit_bytes=ROTATE_VMEM),
+        cost_estimate=pl.CostEstimate(flops=rows * shape[1], bytes_accessed=8 * rows * shape[1], transcendentals=0),
+    )(*args)
+
+
+def outer_columns(first, flat, turned, g, eig, precond, score, ratio, outs):
+    rows = ratio.shape[0] // outs.shape[0]
+    where = pl.ds(pl.multiple_of(first, ratio.shape[1]), ratio.shape[1])
+    stores = []
+    for i in range(outs.shape[0]):
+        block = slice(i * rows, (i + 1) * rows)
+        outer = jnp.dot(turned[block, :], g[...], preferred_element_type=jnp.float32)
+        ratio[block, :] = outer / eig[block, :]
+        stores.append(pltpu.make_async_copy(ratio.at[block, :], precond.at[block, where], outs.at[i]))
+        stores[-1].start()
+    mapped = jnp.dot(flat[...], ratio[...].astype(jnp.bfloat16), preferred_element_type=jnp.float32)
+    part = mapped * g[...].astype(jnp.float32)
+    folded = score[...]
+    for lane in range(0, part.shape[1], score.shape[1]):
+        folded = folded + part[:, lane : lane + score.shape[1]]
+    score[...] = folded
+    for store in stores:
+        store.wait()
+
+
+def near_kernel(
+    place, a0, a1, a2, a3, g, eig, precond, score, flat, turned, later, parts, grads, tile, ratio, outs, loads
+):
+    half = grads.shape[1]
+    copies = [pltpu.make_async_copy(a, parts.at[m], loads.at[m]) for m, a in enumerate((a0, a1, a2, a3))]
+    copies.append(pltpu.make_async_copy(g, grads, loads.at[4]))
+    for i, kept in ((0, tile), (1, later)):
+        where = pl.ds(pl.multiple_of(place[1 + i] * half, half), half)
+        copies.append(pltpu.make_async_copy(eig.at[:, where], kept, loads.at[5 + i]))
+    for copy in copies:
+        copy.start()
+    tok = parts.shape[1] // 4
+    piece = parts.shape[2]
+    for m in range(4):
+        copies[m].wait()
+        where = pl.ds(pl.multiple_of((place[0] ^ m) * piece, piece), piece)
+        rows = jnp.concatenate([parts[m, (j ^ m) * tok : ((j ^ m) + 1) * tok, :] for j in range(4)])
+        flat[:, where] = rows
+        turned[where, :] = rows.T
+    score[...] = jnp.zeros_like(score)
+    copies[4].wait()
+    copies[5].wait()
+    outer_columns(
+        place[1] * half, flat, turned, grads, tile, precond, score, ratio, outs
+    )
+    copies[6].wait()
+
+
+def far_kernel(place, flat, turned, g, eig, done, before, token, precond, value, score, ratio, outs):
+    score[...] = before[...]
+    outer_columns(
+        place[2] * g.shape[1], flat, turned, g, eig, precond, score, ratio, outs
+    )
+    tok = score.shape[0] // 4
+    for j in range(4):
+        value[j : j + 1, :] = jnp.sum(score[j * tok : (j + 1) * tok, :].T, axis=0, keepdims=True)
+
+
+def outer_near(place, acts, grads, eigvals):
+    width = eigvals.shape[0]
+    tokens, cols = grads.shape
+    vmem, hbm = pl.BlockSpec(memory_space=pltpu.VMEM), pl.BlockSpec(memory_space=pltpu.HBM)
+    anywhere = pl.BlockSpec(memory_space=pl.ANY)
+    return pl.pallas_call(
+        near_kernel,
+        out_shape=(
+            jax.ShapeDtypeStruct(eigvals.shape, jnp.float32),
+            jax.ShapeDtypeStruct((tokens, LANES), jnp.float32),
+            jax.ShapeDtypeStruct((tokens, width), jnp.bfloat16),
+            jax.ShapeDtypeStruct((width, tokens), jnp.bfloat16),
+            jax.ShapeDtypeStruct((width, cols), jnp.float32),
+        ),
+        in_specs=[pl.BlockSpec(memory_space=pltpu.SMEM)] + [anywhere] * 5 + [hbm],
+        out_specs=(hbm, vmem, vmem, vmem, vmem),
+        scratch_shapes=[
+            pltpu.VMEM((4, tokens, width // 4), jnp.bfloat16),
+            pltpu.VMEM((tokens, cols), jnp.bfloat16),
+            pltpu.VMEM((width, cols), jnp.float32),
+            pltpu.VMEM((width, cols), jnp.float32),
+            pltpu.SemaphoreType.DMA((BLOCKS,)),
+            pltpu.SemaphoreType.DMA((7,)),
+        ],
+        compiler_params=pltpu.CompilerParams(vmem_limit_bytes=VMEM),
+        cost_estimate=pl.CostEstimate(
+            flops=4 * tokens * width * cols, bytes_accessed=12 * width * cols, transcendentals=0
+        ),
+        name="outer_near",
+    )(place, *acts, grads, eigvals)
+
+
+def outer_far(place, flat, turned, grads, eigvals, done, before, token):
+    tokens, cols = grads.shape
+    width = done.shape[0]
+    vmem, hbm = pl.BlockSpec(memory_space=pltpu.VMEM), pl.BlockSpec(memory_space=pltpu.HBM)
+    return pl.pallas_call(
+        far_kernel,
+        out_shape=(
+            jax.ShapeDtypeStruct(done.shape, jnp.float32),
+            jax.ShapeDtypeStruct((4, tokens // 4), jnp.float32),
+        ),
+        in_specs=[pl.BlockSpec(memory_space=pltpu.SMEM), vmem, vmem, vmem, vmem, hbm, vmem, vmem],
+        out_specs=(hbm, vmem),
+        scratch_shapes=[
+            pltpu.VMEM((tokens, LANES), jnp.float32),
+            pltpu.VMEM((width, cols), jnp.float32),
+            pltpu.SemaphoreType.DMA((BLOCKS,)),
+        ],
+        input_output_aliases={5: 0},
+        compiler_params=pltpu.CompilerParams(vmem_limit_bytes=VMEM),
+        cost_estimate=pl.CostEstimate(
+            flops=4 * tokens * width * cols, bytes_accessed=4 * width * cols, transcendentals=0
+        ),
+        name="outer_far",
+    )(place, flat, turned, grads, eigvals, done, before, token)
+
+
+def local_pairs(acts, grads, source_ids, basis_in, basis_out, eigvals):
+    seqs, rows, cols = (lax.axis_size(name) for name in PLANE)
+    s = lax.axis_index("seq")
+    x = lax.axis_index("row")
+    k = lax.axis_index("col")
+    u = k * rows + x
+    low, high = s % 2, s // 2
+    tok = acts.shape[0]
+    total_tokens = tok * seqs
+    block = acts.shape[1]
+    width = block * rows * cols
+    half, piece = block // 2, block // 4
+
+    def turned(x, flip):
+        pairs = []
+        for b in range(seqs):
+            for f in range(rows * cols):
+                pairs.append((b * rows * cols + f, ((f ^ flip) * rows + b % rows) * cols + b // rows))
+        return lax.ppermute(x, PLANE, pairs)
+
+    def plane_gather(x):
+        near = swap(x, "row")
+        return [x, near, swap(x, "col"), swap(near, "col")]
+
+    tie = lambda *values: lax.optimization_barrier(values)
+    token = jnp.zeros((8, LANES), jnp.float32)
+    acts_there = swap(acts, "row")
+    grads_here = turned(grads, 0)
+    theirs = swap(lax.dynamic_slice_in_dim(basis_in, (1 - k) * half, half, axis=1), "col")
+    basis_out = jnp.concatenate(
+        [lax.dynamic_slice_in_dim(basis_out, at * half, half, axis=1) for at in (1 - low, low)], axis=1
+    )
+    note = lambda *ids: jnp.concatenate([jnp.pad(jnp.stack(ids), ((0, 16 - len(ids)), (0, half - tok)))])
+    source_ids = source_ids.astype(jnp.bfloat16)
+    (token,) = stand(token)
+    token, acts_there = tie(token, acts_there)
+    acts_here = turned(acts_there, cols)
+    (token,) = stand(token)
+    token, grads_here, basis_in, basis_out = tie(token, grads_here, basis_in, basis_out)
+    grads_far = swap(grads_here, "row")
+    mine = lax.dynamic_slice_in_dim(basis_in, k * half, half, axis=1)
+    first, second = jnp.where(k == low, mine, theirs), jnp.where(k == low, theirs, mine)
+    first, second = (jnp.roll(t, -(1 - x) * piece, axis=1) for t in (first, second))
+    tiles = jnp.concatenate([first[:, :piece], second[:, piece:], second[:, :piece], first[:, piece:]], axis=1)
+    (token,) = stand(token)
+    token, grads_far, tiles, grads_here = tie(token, grads_far, tiles, grads_here)
+    grads_both = swap(grads_far, "col")
+    grads_near = swap(grads_here, "col")
+    token, acts_here = tie(token, acts_here)
+    send_g, keep_g = rotate([grads_here, grads_far, grads_near, grads_both], basis_out, 1, note(source_ids))
+    got_g = swap(send_g, "seq", 1)
+    acts_here, keep_g = tie(acts_here, keep_g)
+    acts_far = swap(acts_here, "row")
+    token, keep_g = stand(token, keep_g)
+    token, acts_far, acts_here = tie(token, acts_far, acts_here)
+    acts_both = swap(acts_far, "col")
+    acts_near = swap(acts_here, "col")
+    to_x, to_pair, to_both, keep_a = rotate([acts_here, acts_far, acts_near, acts_both], tiles, 3, flips=(0, 2))
+    from_both = lax.ppermute(
+        to_both,
+        ("seq", "row"),
+        [(i * rows + j, (i ^ 1) * rows + (j ^ 1)) for i in range(seqs) for j in range(rows)],
+    )
+    from_pair = swap(to_pair, "seq", 1)
+    from_x = swap(to_x, "row")
+    token, keep_a = tie(token, keep_a)
+    token, got_g = tie(token, got_g)
+    count = seqs * tok
+    pair_g = small_call(pair_kernel, count + 16, keep_g, got_g, note(source_ids))
+    token, pair_g = tie(token, pair_g)
+    across_g = swap(pair_g, "seq", 2)
+    (token,) = stand(token)
+    token, from_x, from_pair, from_both = tie(token, from_x, from_pair, from_both)
+    same, swapped = added(keep_a, from_pair), added(from_x, from_both)
+    stay = jnp.where(x == high, same, swapped)
+    cross = swap(jnp.where(x == high, swapped, same).astype(jnp.bfloat16), "seq", 2)
+    token, across_g = tie(token, across_g)
+    near_g = small_call(sum_kernel, count, pair_g, across_g)
+    token, near_g = tie(token, near_g)
+    far_g = swap(near_g, "seq", 1)
+    (token,) = stand(token)
+    token, cross = tie(token, cross)
+    own_a = (stay + cross.astype(jnp.float32)).astype(jnp.bfloat16)
+    quarters = plane_gather(own_a)
+
+    ids = jnp.stack([source_ids, got_g[count, :tok], across_g[count, :tok], across_g[count + 1, :tok]])
+    slot_ids = jnp.stack([lax.dynamic_index_in_dim(ids, u ^ s ^ j, keepdims=False) for j in range(seqs)])
+    place = jnp.stack([u, low, 1 - low]).astype(jnp.int32)
+    precond, value, flat, across, later = outer_near(place, quarters, near_g, eigvals)
+    precond, slots = outer_far(place, flat, across, far_g, later, precond, value, token)
+    chosen = slot_ids[None] == jnp.arange(SOURCES, dtype=jnp.bfloat16)[:, None, None]
+    part = jnp.sum(jnp.where(chosen, slots[None], 0.0), axis=(1, 2))
+    blocks = jnp.stack([lax.dynamic_index_in_dim(slots, u ^ j, keepdims=False) for j in range(seqs)])
+    message = jnp.concatenate([blocks, jnp.broadcast_to(part[None, :], (seqs, SOURCES))], axis=1)
+    message = jnp.broadcast_to(message[:, None, :], (seqs, rows * cols, tok + SOURCES))
+    message = message.reshape(seqs * rows * cols, tok + SOURCES)
+    summed = jnp.sum(lax.all_to_all(message, PLANE, split_axis=0, concat_axis=0, tiled=True), axis=0)
+    scale_score = float(total_tokens) / float(width * width)
+    scores = summed[:tok] * scale_score
+    influence = summed[tok:] * (scale_score * (float(SOURCES) / float(total_tokens)))
+    return (precond, scores, influence)
+
+
 def solution(mesh):
     in_specs = (
         P(("grp", "seq"), ("row", "col")),
@@ -111,4 +429,6 @@
         P("seq", ("row", "col")),
     )
     out_specs = (P(("grp", "seq"), ("row", "col")), P(("grp", "seq")), P("grp"))
+    fits = (mesh.shape["seq"], mesh.shape["row"], mesh.shape["col"]) == (4, 2, 2)
+    local = local_pairs if fits else local_any
     return jax.shard_map(local, mesh=mesh, in_specs=in_specs, out_specs=out_specs, check_vma=False)

time: 158 us -> 121 us (0.77)
  starting transfers between devices: 107 us -> 35.7 us
  waiting for transfers between devices: 38 us -> 51 us
  Pallas kernels: 0 us -> 11.5 us
  blocking collectives: 0 us -> 10.9 us
  matrix products: 8.46 us -> 0 us
  local copies, waits for them, and re-layouts: 0.73 us -> 7.03 us
    ppermute x29 -> x20, starting transfers between devices: 107 us -> 35.7 us  [the longest x17 27.1 us: swap(): lax.ppermute(x, axis, [(i, i ^ step) for i in range(lax.axis_size(axis))])]
    ppermute x29 -> x20, waiting for transfers between devices: 38 us -> 51 us  [the longest x17 42.7 us: swap(): lax.ppermute(x, axis, [(i, i ^ step) for i in range(lax.axis_size(axis))])]
    pallas_call x0 -> x12, Pallas kernels: none -> 11.5 us  [the longest x2 4.31 us: rotate(): pl.pallas_call(functools.partial(rotate_kernel, notes=len(note), flips=fl...]
    all_to_all x0 -> x1, blocking collectives: none -> 10.9 us  [local_pairs(): lax.all_to_all(message, PLANE, split_axis=0, concat_axis=0, tiled=True)]
    dot_general x13 -> x0, matrix products: 8.46 us -> none  [the longest x8 3.56 us: rotate(): jnp.dot(x, basis, preferred_element_type=jnp.float32).astype(jnp.bfloat16)]
    dynamic_slice x0 -> x4, local copies, waits for them, and re-layouts: none -> 3.96 us  [the longest x1 2.26 us: local_pairs(): lax.dynamic_slice_in_dim(basis_in, (1 - k) * half, half, axis=1)]
  transfers between devices with their start and end apart: 29 -> 20, of which waited for: 9 -> 11; matrix products, arithmetic and copies ran while one was open for 4% -> 6% of each run, Pallas kernels for 0% -> 6%
where the time goes in v4:
time: 121 us; the launch traced here: 120 us
  waiting for transfers between devices  51 us (42%)
  starting transfers between devices  35.7 us (30%)
  Pallas kernels  11.5 us (10%)
  blocking collectives  10.9 us (9%)
  local copies, waits for them, and re-layouts  7.03 us (6%)
  other arithmetic  3.45 us (3%)
    ppermute x17, waiting for transfers between devices, swap(): lax.ppermute(x, axis, [(i, i ^ step) for i in range(lax.axis_size(axis))])  42.7 us
    ppermute x17, starting transfers between devices, swap(): lax.ppermute(x, axis, [(i, i ^ step) for i in range(lax.axis_size(axis))])  27.1 us
    all_to_all x1, blocking collectives, local_pairs(): lax.all_to_all(message, PLANE, split_axis=0, concat_axis=0, tiled=True)  10.9 us
    ppermute x2, starting transfers between devices, turned(): return lax.ppermute(x, PLANE, pairs)  7.21 us
    ppermute x1, waiting for transfers between devices, local_pairs(): lax.ppermute(to_both, ('seq', 'row'), [(i * rows + j, (i ^ 1) * rows + (j...  6.09 us
    pallas_call x2, Pallas kernels, rotate(): pl.pallas_call(functools.partial(rotate_kernel, notes=len(note), flips=fl...  4.31 us
    pallas_call x1, Pallas kernels, outer_near(): pl.pallas_call(near_kernel, out_shape=(jax.ShapeDtypeStruct(eigvals.shape...  3.61 us
  transfers between devices with their start and end apart: 20, of which 11 were waited for; matrix products, arithmetic and copies ran while one was open for 6% of the time, Pallas kernels for 6%

profile of v4, /device:TPU:0, one launch (start us, length us, event | category | flops | bytes accessed | tf_op | source)
XLA Modules:
  0.0 120.4 jit_solution(7716309404531030848)
XLA Ops:
  0.6 3.0 %collective-permute-start = (bf16[128,1024]{1,0:T(8,128)(2,1)}, bf16[128,1024]{1,0:T(8,128)(2,1)}, u32[]{:S(2)}, u32[]{:S(2)}) collective-permute-start(bf16[128,1024]{1,0:T(8,128)(2,1)} %param.8), channel_id=1, source_target_pairs={{0,2},{2,0},{1,3},{3,1},{4,6},{6,4},{5,7},{7,5},{8,10},{10,8},{9,1... | collective-permute-start | bytes 786440 | tf_op jit(solution)/shard_map/ppermute | solution.py:116
  3.6 1.6 %collective-permute-start.1 = (bf16[128,1024]{1,0:T(8,128)(2,1)}, bf16[128,1024]{1,0:T(8,128)(2,1)S(1)}, u32[]{:S(2)}, u32[]{:S(2)}) collective-permute-start(bf16[128,1024]{1,0:T(8,128)(2,1)} %param.9), channel_id=1, source_target_pairs={{0,0},{1,4},{2,8},{3,12},{4,2},{5,6},{6,10},{7,14},{8,1},{9,5},{10... | collective-permute-start | bytes 786440 | tf_op jit(solution)/shard_map/ppermute | solution.py:337
  5.2 2.3 %constant_dynamic-slice_fusion.8 = bf16[1024,512]{1,0:T(8,128)(2,1)} fusion(bf16[1024,1024]{1,0:T(8,128)(2,1)} %param.11, s32[]{:T(128)S(6)} %select_n.93), kind=kLoop, calls=%fused_computation.24 | loop fusion | bytes 2097156 | tf_op jit(solution)/shard_map/dynamic_slice | solution.py:347
  7.5 2.0 %collective-permute-start.3 = (bf16[1024,512]{1,0:T(8,128)(2,1)}, bf16[1024,512]{1,0:T(8,128)(2,1)S(1)}, u32[]{:S(2)}, u32[]{:S(2)}) collective-permute-start(bf16[1024,512]{1,0:T(8,128)(2,1)} %constant_dynamic-slice_fusion.8), channel_id=1, source_target_pairs={{0,1},{1,0},{2,3},{3,2},{4,5},{5,4},{6,7},{7,6},{8,9},{9,8},{10,11... | collective-permute-start | bytes 3145736 | tf_op jit(solution)/shard_map/ppermute | solution.py:116
  9.5 1.7 %constant_dynamic-slice_fusion.10 = (bf16[1024,512]{1,0:T(8,128)(2,1)S(1)}, bf16[1024,512]{1,0:T(8,128)(2,1)S(1)}) fusion(bf16[1024,1024]{1,0:T(8,128)(2,1)} %param.12, s32[]{:T(128)S(6)} %select_n.89, s32[]{:T(128)S(6)} %select_n.90), kind=kLoop, calls=%fused_computation.26 | loop fusion | bytes 4194312 | tf_op jit(solution)/shard_map/dynamic_slice | solution.py:349
  11.2 0.3 pad_maximum_fusion.basis
  11.4 3.7 %collective-permute-done = bf16[128,1024]{1,0:T(8,128)(2,1)} collective-permute-done((bf16[128,1024]{1,0:T(8,128)(2,1)}, bf16[128,1024]{1,0:T(8,128)(2,1)}, u32[]{:S(2)}, u32[]{:S(2)}) %collective-permute-start) | collective-permute-done | bytes 262176 | tf_op jit(solution)/shard_map/ppermute | solution.py:116
  15.2 0.0 collective-permute-done.1.x0
  15.2 2.5 %collective-permute-start.2 = (bf16[128,1024]{1,0:T(8,128)(2,1)S(1)}, bf16[128,1024]{1,0:T(8,128)(2,1)S(1)}, u32[]{:S(2)}, u32[]{:S(2)}) collective-permute-start(bf16[128,1024]{1,0:T(8,128)(2,1)S(1)} %collective-permute-done.1.x0), channel_id=1, source_target_pairs={{0,2},{2,0},{1,3},{3,1},{4,6},{6,4},{5,7},{7,5},{8,10},{10,8},{9,1... | collective-permute-start | bytes 786440 | tf_op jit(solution)/shard_map/ppermute | solution.py:116
  17.7 5.6 %collective-permute-start.4 = (bf16[128,1024]{1,0:T(8,128)(2,1)}, bf16[128,1024]{1,0:T(8,128)(2,1)}, u32[]{:S(2)}, u32[]{:S(2)}) collective-permute-start(bf16[128,1024]{1,0:T(8,128)(2,1)} %collective-permute-done), channel_id=1, source_target_pairs={{0,8},{1,12},{2,0},{3,4},{4,10},{5,14},{6,2},{7,6},{8,9},{9,13},{1... | collective-permute-start | bytes 786440 | tf_op jit(solution)/shard_map/ppermute | solution.py:337
  23.3 0.0 collective-permute-done.3
  23.3 0.5 broadcast_select_fusion
  23.8 0.8 fusion
  24.6 0.1 fusion.2
  24.7 0.1 fusion.3
  24.8 0.0 copy-start.2
  24.8 0.3 pad_maximum_fusion.1.basis
  25.1 0.0 collective-permute-done.2.x1
  25.1 2.4 %collective-permute-start.5 = (bf16[128,1024]{1,0:T(8,128)(2,1)S(1)}, bf16[128,1024]{1,0:T(8,128)(2,1)S(1)}, u32[]{:S(2)}, u32[]{:S(2)}) collective-permute-start(bf16[128,1024]{1,0:T(8,128)(2,1)S(1)} %collective-permute-done.1.x0), channel_id=1, source_target_pairs={{0,1},{1,0},{2,3},{3,2},{4,5},{5,4},{6,7},{7,6},{8,9},{9,8},{10,11... | collective-permute-start | bytes 786440 | tf_op jit(solution)/shard_map/ppermute | solution.py:116
  27.5 0.0 collective-permute-start.6
  27.5 2.2 %collective-permute-done.4.x0 = bf16[128,1024]{1,0:T(8,128)(2,1)} collective-permute-done((bf16[128,1024]{1,0:T(8,128)(2,1)}, bf16[128,1024]{1,0:T(8,128)(2,1)}, u32[]{:S(2)}, u32[]{:S(2)}) %collective-permute-start.4) | collective-permute-done | bytes 262176 | tf_op jit(solution)/shard_map/ppermute | solution.py:337
  29.7 0.0 collective-permute-done.5.x2
  29.7 0.0 collective-permute-done.6.x3
  29.7 2.0 %rotate.2 = (bf16[528,512]{1,0:T(8,128)(2,1)}, f32[512,512]{1,0:T(8,128)S(1)}) custom-call(bf16[128,1024]{1,0:T(8,128)(2,1)S(1)} %collective-permute-done.1.x0, bf16[128,1024]{1,0:T(8,128)(2,1)S(1)} %collective-permute-done.2.x1, bf16[128,1024]{1,0:T(8,128)(2,1)S(1)} %collective-permute-done.5.x2, bf16[128,1024]{1,0:T(8,128)(2,1)S(1)} %collective-permute-done.6.x3, ...), custom_call_target="tpu_custom_call" | custom-call | flops 1073741824 | bytes 2097152 | tf_op jit(solution)/shard_map/rotate/pallas_call | solution.py:164
  31.7 0.0 collective-permute-start.7
  31.7 5.6 %collective-permute-start.10 = (bf16[528,512]{1,0:T(8,128)(2,1)}, bf16[528,512]{1,0:T(8,128)(2,1)}, u32[]{:S(2)}, u32[]{:S(2)}) collective-permute-start(bf16[528,512]{1,0:T(8,128)(2,1)} %get-tuple-element.74), channel_id=1, source_target_pairs={{0,4},{4,0},{8,12},{12,8},{1,5},{5,1},{9,13},{13,9},{2,6},{6,2},{1... | collective-permute-start | bytes 1622024 | tf_op jit(solution)/shard_map/ppermute | solution.py:116
  37.3 1.2 collective-permute-done.7.x1
  38.4 5.2 %collective-permute-start.8 = (bf16[128,1024]{1,0:T(8,128)(2,1)}, bf16[128,1024]{1,0:T(8,128)(2,1)}, u32[]{:S(2)}, u32[]{:S(2)}) collective-permute-start(bf16[128,1024]{1,0:T(8,128)(2,1)} %collective-permute-done.4.x0), channel_id=1, source_target_pairs={{0,1},{1,0},{2,3},{3,2},{4,5},{5,4},{6,7},{7,6},{8,9},{9,8},{10,11... | collective-permute-start | bytes 786440 | tf_op jit(solution)/shard_map/ppermute | solution.py:116
  43.6 0.0 collective-permute-start.9
  43.6 1.8 %collective-permute-done.8.x2 = bf16[128,1024]{1,0:T(8,128)(2,1)} collective-permute-done((bf16[128,1024]{1,0:T(8,128)(2,1)}, bf16[128,1024]{1,0:T(8,128)(2,1)}, u32[]{:S(2)}, u32[]{:S(2)}) %collective-permute-start.8) | collective-permute-done | bytes 262176 | tf_op jit(solution)/shard_map/ppermute | solution.py:116
  45.4 0.0 collective-permute-done.9.x3
  45.4 2.4 %rotate.3 = (bf16[512,256]{1,0:T(8,128)(2,1)S(1)}, bf16[512,256]{1,0:T(8,128)(2,1)S(1)}, bf16[512,256]{1,0:T(8,128)(2,1)S(1)}, f32[512,256]{1,0:T(8,128)S(1)}) custom-call(bf16[128,1024]{1,0:T(8,128)(2,1)} %collective-permute-done.4.x0, bf16[128,1024]{1,0:T(8,128)(2,1)S(1)} %collective-permute-done.7.x1, bf16[128,1024]{1,0:T(8,128)(2,1)} %collective-permute-done.8.x2, ...), custom_call_target="tpu_custom_call" | custom-call | flops 1073741824 | bytes 2097152 | tf_op jit(solution)/shard_map/rotate/pallas_call | solution.py:164
  47.8 0.4 collective-permute-start.11
  48.2 3.0 %collective-permute-start.12 = (bf16[512,256]{1,0:T(8,128)(2,1)S(1)}, bf16[512,256]{1,0:T(8,128)(2,1)S(1)}, u32[]{:S(2)}, u32[]{:S(2)}) collective-permute-start(bf16[512,256]{1,0:T(8,128)(2,1)S(1)} %get-tuple-element.80), channel_id=1, source_target_pairs={{0,4},{4,0},{8,12},{12,8},{1,5},{5,1},{9,13},{13,9},{2,6},{6,2},{1... | collective-permute-start | bytes 786440 | tf_op jit(solution)/shard_map/ppermute | solution.py:116
  51.2 1.4 %collective-permute-start.13 = (bf16[512,256]{1,0:T(8,128)(2,1)S(1)}, bf16[512,256]{1,0:T(8,128)(2,1)S(1)}, u32[]{:S(2)}, u32[]{:S(2)}) collective-permute-start(bf16[512,256]{1,0:T(8,128)(2,1)S(1)} %get-tuple-element.81), channel_id=1, source_target_pairs={{0,6},{2,4},{4,2},{6,0},{8,14},{10,12},{12,10},{14,8},{1,7},{3,5},... | collective-permute-start | bytes 786440 | tf_op jit(solution)/shard_map/ppermute | solution.py:377
  52.5 0.0 collective-permute-done.10.got
  52.6 1.1 shard_map.85.pair
  53.7 1.6 %collective-permute-start.14 = (bf16[528,512]{1,0:T(8,128)(2,1)S(1)}, bf16[528,512]{1,0:T(8,128)(2,1)S(1)}, u32[]{:S(2)}, u32[]{:S(2)}) collective-permute-start(bf16[528,512]{1,0:T(8,128)(2,1)S(1)} %shard_map.85.pair), channel_id=1, source_target_pairs={{0,8},{4,12},{8,0},{12,4},{1,9},{5,13},{9,1},{13,5},{2,10},{6,14},... | collective-permute-start | bytes 1622024 | tf_op jit(solution)/shard_map/ppermute | solution.py:116
  55.3 1.2 collective-permute-done.11
  56.4 10.4 %collective-permute-done.12 = bf16[512,256]{1,0:T(8,128)(2,1)S(1)} collective-permute-done((bf16[512,256]{1,0:T(8,128)(2,1)S(1)}, bf16[512,256]{1,0:T(8,128)(2,1)S(1)}, u32[]{:S(2)}, u32[]{:S(2)}) %collective-permute-start.12) | collective-permute-done | bytes 262176 | tf_op jit(solution)/shard_map/ppermute | solution.py:116
  66.9 6.1 %collective-permute-done.13 = bf16[512,256]{1,0:T(8,128)(2,1)S(1)} collective-permute-done((bf16[512,256]{1,0:T(8,128)(2,1)S(1)}, bf16[512,256]{1,0:T(8,128)(2,1)S(1)}, u32[]{:S(2)}, u32[]{:S(2)}) %collective-permute-start.13) | collective-permute-done | bytes 262176 | tf_op jit(solution)/shard_map/ppermute | solution.py:377
  73.0 0.1 select_convert_fusion
  73.1 0.1 collective-permute-start.15
  73.2 13.9 %collective-permute-done.14.across = bf16[528,512]{1,0:T(8,128)(2,1)S(1)} collective-permute-done((bf16[528,512]{1,0:T(8,128)(2,1)S(1)}, bf16[528,512]{1,0:T(8,128)(2,1)S(1)}, u32[]{:S(2)}, u32[]{:S(2)}) %collective-permute-start.14) | collective-permute-done | bytes 540704 | tf_op jit(solution)/shard_map/ppermute | solution.py:116
  87.1 0.1 shard_map.86.g
  87.2 4.1 %collective-permute-done.15 = bf16[512,256]{1,0:T(8,128)(2,1)S(1)} collective-permute-done((bf16[512,256]{1,0:T(8,128)(2,1)S(1)}, bf16[512,256]{1,0:T(8,128)(2,1)S(1)}, u32[]{:S(2)}, u32[]{:S(2)}) %collective-permute-start.15) | collective-permute-done | bytes 262176 | tf_op jit(solution)/shard_map/ppermute | solution.py:116
  91.3 0.2 add_convert_fusion.a0
  91.5 0.6 collective-permute-start.16
  92.1 0.7 collective-permute-start.19
  92.9 0.1 pad_add_fusion.place
  93.0 0.7 slice.30
  93.6 0.0 collective-permute-start.17
  93.6 4.9 %collective-permute-done.16.a1 = bf16[512,256]{1,0:T(8,128)(2,1)S(1)} collective-permute-done((bf16[512,256]{1,0:T(8,128)(2,1)S(1)}, bf16[512,256]{1,0:T(8,128)(2,1)S(1)}, u32[]{:S(2)}, u32[]{:S(2)}) %collective-permute-start.16) | collective-permute-done | bytes 262176 | tf_op jit(solution)/shard_map/ppermute | solution.py:116
  98.5 0.0 collective-permute-start.18
  98.6 0.0 collective-permute-done.17.a2
  98.6 1.5 %collective-permute-done.18.a3 = bf16[512,256]{1,0:T(8,128)(2,1)S(1)} collective-permute-done((bf16[512,256]{1,0:T(8,128)(2,1)S(1)}, bf16[512,256]{1,0:T(8,128)(2,1)S(1)}, u32[]{:S(2)}, u32[]{:S(2)}) %collective-permute-start.18) | collective-permute-done | bytes 262176 | tf_op jit(solution)/shard_map/ppermute | solution.py:116
  100.1 2.2 %copy-done = f32[1024,1024]{1,0:T(8,128)S(1)} copy-done((f32[1024,1024]{1,0:T(8,128)S(1)}, f32[1024,1024]{1,0:T(8,128)}, u32[]{:S(2)}) %copy-start) | copy-done | bytes 4194328
  102.3 3.6 %outer_near.1 = (f32[1024,1024]{1,0:T(8,128)}, f32[512,128]{1,0:T(8,128)S(1)}, bf16[512,1024]{1,0:T(8,128)(2,1)S(1)}, bf16[1024,512]{1,0:T(8,128)(2,1)S(1)}, f32[1024,512]{1,0:T(8,128)S(1)}) custom-call(s32[3]{0:T(128)S(1)} %pad_add_fusion.place, bf16[512,256]{1,0:T(8,128)(2,1)S(1)} %add_convert_fusion.a0, bf16[512,256]{1,0:T(8,128)(2,1)S(1)} %collective-permute-done.16.a1, ...), custom_call_target="tpu_custom_call" | custom-call | flops 1073741824 | bytes 6291456 | tf_op jit(solution)/shard_map/outer_near/pallas_call | solution.py:266
  105.9 0.0 collective-permute-done.19.g
  105.9 2.3 %outer_far.1 = (f32[1024,1024]{1,0:T(8,128)}, f32[4,128]{1,0:T(4,128)S(1)}) custom-call(s32[3]{0:T(128)S(1)} %pad_add_fusion.place, bf16[512,1024]{1,0:T(8,128)(2,1)S(1)} %get-tuple-element.92.flat, bf16[1024,512]{1,0:T(8,128)(2,1)S(1)} %get-tuple-element.93.turned, bf16[512,512]{1,0:T(8,128)(2,1)S(1)} %collective-permute-done.19.g, ...), custom_call_target="tpu_custom_call", output_to_operand_aliasing={{0}: (5, {})} | custom-call | flops 1073741824 | bytes 2097152 | tf_op jit(solution)/shard_map/outer_far/pallas_call | solution.py:297
  108.2 0.1 select_reduce_fusion
  108.5 10.9 %all_to_all.9 = f32[16,1,136]{2,1,0:T(1,128)S(1)} all-to-all(f32[16,1,136]{2,1,0:T(1,128)S(1)} %all_to_all.6), channel_id=1, replica_groups=mesh['grp'=2,'seq'=4,'row'=2,'col'=2] {'seq','row','col'}, dimensions={0} | all-to-all | bytes 17408 | tf_op jit(solution)/shard_map/all_to_all | solution.py:415
  119.4 0.5 slice_multiply_fusion
  119.9 0.5 slice_multiply_fusion.1
  (23 shorter events, 0.2 us)
Async XLA Ops:
  0.6 14.5 %collective-permute-start = (bf16[128,1024]{1,0:T(8,128)(2,1)}, bf16[128,1024]{1,0:T(8,128)(2,1)}, u32[]{:S(2)}, u32[]{:S(2)}) collective-permute-start(bf16[128,1024]{1,0:T(8,128)(2,1)} %param.8), channel_id=1, source_target_pairs={{0,2},{2,0},{1,3},{3,1},{4,6},{6,4},{5,7},{7,5},{8,10},{10,8},{9,1... | collective-permute-start | bytes 786440 | tf_op jit(solution)/shard_map/ppermute | solution.py:116
  3.6 11.5 %collective-permute-start.1 = (bf16[128,1024]{1,0:T(8,128)(2,1)}, bf16[128,1024]{1,0:T(8,128)(2,1)S(1)}, u32[]{:S(2)}, u32[]{:S(2)}) collective-permute-start(bf16[128,1024]{1,0:T(8,128)(2,1)} %param.9), channel_id=1, source_target_pairs={{0,0},{1,4},{2,8},{3,12},{4,2},{5,6},{6,10},{7,14},{8,1},{9,5},{10... | collective-permute-start | bytes 786440 | tf_op jit(solution)/shard_map/ppermute | solution.py:337
  7.5 15.8 %collective-permute-start.3 = (bf16[1024,512]{1,0:T(8,128)(2,1)}, bf16[1024,512]{1,0:T(8,128)(2,1)S(1)}, u32[]{:S(2)}, u32[]{:S(2)}) collective-permute-start(bf16[1024,512]{1,0:T(8,128)(2,1)} %constant_dynamic-slice_fusion.8), channel_id=1, source_target_pairs={{0,1},{1,0},{2,3},{3,2},{4,5},{5,4},{6,7},{7,6},{8,9},{9,8},{10,11... | collective-permute-start | bytes 3145736 | tf_op jit(solution)/shard_map/ppermute | solution.py:116
  15.2 8.1 %copy-start.1 = (bf16[1024,1024]{1,0:T(8,128)(2,1)S(1)}, bf16[1024,1024]{1,0:T(8,128)(2,1)}, u32[]{:S(2)}) copy-start(bf16[1024,1024]{1,0:T(8,128)(2,1)} %param.11) | copy-start | bytes 6291460
  15.2 9.9 %collective-permute-start.2 = (bf16[128,1024]{1,0:T(8,128)(2,1)S(1)}, bf16[128,1024]{1,0:T(8,128)(2,1)S(1)}, u32[]{:S(2)}, u32[]{:S(2)}) collective-permute-start(bf16[128,1024]{1,0:T(8,128)(2,1)S(1)} %collective-permute-done.1.x0), channel_id=1, source_target_pairs={{0,2},{2,0},{1,3},{3,1},{4,6},{6,4},{5,7},{7,5},{8,10},{10,8},{9,1... | collective-permute-start | bytes 786440 | tf_op jit(solution)/shard_map/ppermute | solution.py:116
  17.7 12.0 %collective-permute-start.4 = (bf16[128,1024]{1,0:T(8,128)(2,1)}, bf16[128,1024]{1,0:T(8,128)(2,1)}, u32[]{:S(2)}, u32[]{:S(2)}) collective-permute-start(bf16[128,1024]{1,0:T(8,128)(2,1)} %collective-permute-done), channel_id=1, source_target_pairs={{0,8},{1,12},{2,0},{3,4},{4,10},{5,14},{6,2},{7,6},{8,9},{9,13},{1... | collective-permute-start | bytes 786440 | tf_op jit(solution)/shard_map/ppermute | solution.py:337
  24.8 2.7 %copy-start.2 = (s32[128]{0:T(128)S(1)}, s32[128]{0:T(128)}, u32[]{:S(2)}) copy-start(s32[128]{0:T(128)} %param.10) | copy-start | bytes 1540
  25.1 4.6 %collective-permute-start.5 = (bf16[128,1024]{1,0:T(8,128)(2,1)S(1)}, bf16[128,1024]{1,0:T(8,128)(2,1)S(1)}, u32[]{:S(2)}, u32[]{:S(2)}) collective-permute-start(bf16[128,1024]{1,0:T(8,128)(2,1)S(1)} %collective-permute-done.1.x0), channel_id=1, source_target_pairs={{0,1},{1,0},{2,3},{3,2},{4,5},{5,4},{6,7},{7,6},{8,9},{9,8},{10,11... | collective-permute-start | bytes 786440 | tf_op jit(solution)/shard_map/ppermute | solution.py:116
  27.5 2.2 %collective-permute-start.6 = (bf16[128,1024]{1,0:T(8,128)(2,1)S(1)}, bf16[128,1024]{1,0:T(8,128)(2,1)S(1)}, u32[]{:S(2)}, u32[]{:S(2)}) collective-permute-start(bf16[128,1024]{1,0:T(8,128)(2,1)S(1)} %collective-permute-done.2.x1), channel_id=1, source_target_pairs={{0,1},{1,0},{2,3},{3,2},{4,5},{5,4},{6,7},{7,6},{8,9},{9,8},{10,11... | collective-permute-start | bytes 786440 | tf_op jit(solution)/shard_map/ppermute | solution.py:116
  31.7 6.8 %collective-permute-start.7 = (bf16[128,1024]{1,0:T(8,128)(2,1)}, bf16[128,1024]{1,0:T(8,128)(2,1)S(1)}, u32[]{:S(2)}, u32[]{:S(2)}) collective-permute-start(bf16[128,1024]{1,0:T(8,128)(2,1)} %collective-permute-done.4.x0), channel_id=1, source_target_pairs={{0,2},{2,0},{1,3},{3,1},{4,6},{6,4},{5,7},{7,5},{8,10},{10,8},{9,1... | collective-permute-start | bytes 786440 | tf_op jit(solution)/shard_map/ppermute | solution.py:116
  31.7 20.9 %collective-permute-start.10 = (bf16[528,512]{1,0:T(8,128)(2,1)}, bf16[528,512]{1,0:T(8,128)(2,1)}, u32[]{:S(2)}, u32[]{:S(2)}) collective-permute-start(bf16[528,512]{1,0:T(8,128)(2,1)} %get-tuple-element.74), channel_id=1, source_target_pairs={{0,4},{4,0},{8,12},{12,8},{1,5},{5,1},{9,13},{13,9},{2,6},{6,2},{1... | collective-permute-start | bytes 1622024 | tf_op jit(solution)/shard_map/ppermute | solution.py:116
  38.4 7.0 %collective-permute-start.8 = (bf16[128,1024]{1,0:T(8,128)(2,1)}, bf16[128,1024]{1,0:T(8,128)(2,1)}, u32[]{:S(2)}, u32[]{:S(2)}) collective-permute-start(bf16[128,1024]{1,0:T(8,128)(2,1)} %collective-permute-done.4.x0), channel_id=1, source_target_pairs={{0,1},{1,0},{2,3},{3,2},{4,5},{5,4},{6,7},{7,6},{8,9},{9,8},{10,11... | collective-permute-start | bytes 786440 | tf_op jit(solution)/shard_map/ppermute | solution.py:116
  43.6 1.8 %collective-permute-start.9 = (bf16[128,1024]{1,0:T(8,128)(2,1)S(1)}, bf16[128,1024]{1,0:T(8,128)(2,1)}, u32[]{:S(2)}, u32[]{:S(2)}) collective-permute-start(bf16[128,1024]{1,0:T(8,128)(2,1)S(1)} %collective-permute-done.7.x1), channel_id=1, source_target_pairs={{0,1},{1,0},{2,3},{3,2},{4,5},{5,4},{6,7},{7,6},{8,9},{9,8},{10,11... | collective-permute-start | bytes 786440 | tf_op jit(solution)/shard_map/ppermute | solution.py:116
  47.8 8.7 %collective-permute-start.11 = (bf16[512,256]{1,0:T(8,128)(2,1)S(1)}, bf16[512,256]{1,0:T(8,128)(2,1)S(1)}, u32[]{:S(2)}, u32[]{:S(2)}) collective-permute-start(bf16[512,256]{1,0:T(8,128)(2,1)S(1)} %get-tuple-element.79), channel_id=1, source_target_pairs={{0,2},{2,0},{1,3},{3,1},{4,6},{6,4},{5,7},{7,5},{8,10},{10,8},{9,1... | collective-permute-start | bytes 786440 | tf_op jit(solution)/shard_map/ppermute | solution.py:116
  48.2 18.7 %collective-permute-start.12 = (bf16[512,256]{1,0:T(8,128)(2,1)S(1)}, bf16[512,256]{1,0:T(8,128)(2,1)S(1)}, u32[]{:S(2)}, u32[]{:S(2)}) collective-permute-start(bf16[512,256]{1,0:T(8,128)(2,1)S(1)} %get-tuple-element.80), channel_id=1, source_target_pairs={{0,4},{4,0},{8,12},{12,8},{1,5},{5,1},{9,13},{13,9},{2,6},{6,2},{1... | collective-permute-start | bytes 786440 | tf_op jit(solution)/shard_map/ppermute | solution.py:116
  51.2 21.8 %collective-permute-start.13 = (bf16[512,256]{1,0:T(8,128)(2,1)S(1)}, bf16[512,256]{1,0:T(8,128)(2,1)S(1)}, u32[]{:S(2)}, u32[]{:S(2)}) collective-permute-start(bf16[512,256]{1,0:T(8,128)(2,1)S(1)} %get-tuple-element.81), channel_id=1, source_target_pairs={{0,6},{2,4},{4,2},{6,0},{8,14},{10,12},{12,10},{14,8},{1,7},{3,5},... | collective-permute-start | bytes 786440 | tf_op jit(solution)/shard_map/ppermute | solution.py:377
  53.7 33.4 %collective-permute-start.14 = (bf16[528,512]{1,0:T(8,128)(2,1)S(1)}, bf16[528,512]{1,0:T(8,128)(2,1)S(1)}, u32[]{:S(2)}, u32[]{:S(2)}) collective-permute-start(bf16[528,512]{1,0:T(8,128)(2,1)S(1)} %shard_map.85.pair), channel_id=1, source_target_pairs={{0,8},{4,12},{8,0},{12,4},{1,9},{5,13},{9,1},{13,5},{2,10},{6,14},... | collective-permute-start | bytes 1622024 | tf_op jit(solution)/shard_map/ppermute | solution.py:116
  73.1 18.2 %collective-permute-start.15 = (bf16[512,256]{1,0:T(8,128)(2,1)S(1)}, bf16[512,256]{1,0:T(8,128)(2,1)S(1)}, u32[]{:S(2)}, u32[]{:S(2)}) collective-permute-start(bf16[512,256]{1,0:T(8,128)(2,1)S(1)} %select_convert_fusion), channel_id=1, source_target_pairs={{0,8},{4,12},{8,0},{12,4},{1,9},{5,13},{9,1},{13,5},{2,10},{6,14},... | collective-permute-start | bytes 786440 | tf_op jit(solution)/shard_map/ppermute | solution.py:116
  91.5 7.0 %collective-permute-start.16 = (bf16[512,256]{1,0:T(8,128)(2,1)S(1)}, bf16[512,256]{1,0:T(8,128)(2,1)S(1)}, u32[]{:S(2)}, u32[]{:S(2)}) collective-permute-start(bf16[512,256]{1,0:T(8,128)(2,1)S(1)} %add_convert_fusion.a0), channel_id=1, source_target_pairs={{0,2},{2,0},{1,3},{3,1},{4,6},{6,4},{5,7},{7,5},{8,10},{10,8},{9,1... | collective-permute-start | bytes 786440 | tf_op jit(solution)/shard_map/ppermute | solution.py:116
  92.1 13.8 %collective-permute-start.19 = (bf16[512,512]{1,0:T(8,128)(2,1)S(1)}, bf16[512,512]{1,0:T(8,128)(2,1)S(1)}, u32[]{:S(2)}, u32[]{:S(2)}) collective-permute-start(bf16[512,512]{1,0:T(8,128)(2,1)S(1)} %shard_map.86.g), channel_id=1, source_target_pairs={{0,4},{4,0},{8,12},{12,8},{1,5},{5,1},{9,13},{13,9},{2,6},{6,2},{1... | collective-permute-start | bytes 1572872 | tf_op jit(solution)/shard_map/ppermute | solution.py:116
  93.6 5.0 %collective-permute-start.17 = (bf16[512,256]{1,0:T(8,128)(2,1)S(1)}, bf16[512,256]{1,0:T(8,128)(2,1)S(1)}, u32[]{:S(2)}, u32[]{:S(2)}) collective-permute-start(bf16[512,256]{1,0:T(8,128)(2,1)S(1)} %add_convert_fusion.a0), channel_id=1, source_target_pairs={{0,1},{1,0},{2,3},{3,2},{4,5},{5,4},{6,7},{7,6},{8,9},{9,8},{10,11... | collective-permute-start | bytes 786440 | tf_op jit(solution)/shard_map/ppermute | solution.py:116
  98.5 1.5 %collective-permute-start.18 = (bf16[512,256]{1,0:T(8,128)(2,1)S(1)}, bf16[512,256]{1,0:T(8,128)(2,1)S(1)}, u32[]{:S(2)}, u32[]{:S(2)}) collective-permute-start(bf16[512,256]{1,0:T(8,128)(2,1)S(1)} %collective-permute-done.16.a1), channel_id=1, source_target_pairs={{0,1},{1,0},{2,3},{3,2},{4,5},{5,4},{6,7},{7,6},{8,9},{9,8},{10,11... | collective-permute-start | bytes 786440 | tf_op jit(solution)/shard_map/ppermute | solution.py:116
  100.1 2.2 %copy-start = (f32[1024,1024]{1,0:T(8,128)S(1)}, f32[1024,1024]{1,0:T(8,128)}, u32[]{:S(2)}) copy-start(f32[1024,1024]{1,0:T(8,128)} %eig.1) | copy-start | bytes 12582916

commit v5 on v4

--- a/solution.py
+++ b/solution.py
@@ -106,6 +106,7 @@
 
 
 VMEM = 16 * 2**20
+NEAR_VMEM = 48 * 2**20
 ROTATE_VMEM = 10 * 2**20
 LANES = 128
 STAND = 2 * 10**10
@@ -282,7 +283,7 @@
             pltpu.SemaphoreType.DMA((BLOCKS,)),
             pltpu.SemaphoreType.DMA((7,)),
         ],
-        compiler_params=pltpu.CompilerParams(vmem_limit_bytes=VMEM),
+        compiler_params=pltpu.CompilerParams(vmem_limit_bytes=NEAR_VMEM),
         cost_estimate=pl.CostEstimate(
             flops=4 * tokens * width * cols, bytes_accessed=12 * width * cols, transcendentals=0
         ),
@@ -329,11 +330,11 @@
     width = block * rows * cols
     half, piece = block // 2, block // 4
 
-    def turned(x, flip):
+    def turned(x):
         pairs = []
         for b in range(seqs):
             for f in range(rows * cols):
-                pairs.append((b * rows * cols + f, ((f ^ flip) * rows + b % rows) * cols + b // rows))
+                pairs.append((b * rows * cols + f, (f * rows + b % rows) * cols + b // rows))
         return lax.ppermute(x, PLANE, pairs)
 
     def plane_gather(x):
@@ -342,8 +343,7 @@
 
     tie = lambda *values: lax.optimization_barrier(values)
     token = jnp.zeros((8, LANES), jnp.float32)
-    acts_there = swap(acts, "row")
-    grads_here = turned(grads, 0)
+    grads_here = turned(grads)
     theirs = swap(lax.dynamic_slice_in_dim(basis_in, (1 - k) * half, half, axis=1), "col")
     basis_out = jnp.concatenate(
         [lax.dynamic_slice_in_dim(basis_out, at * half, half, axis=1) for at in (1 - low, low)], axis=1
@@ -351,10 +351,8 @@
     note = lambda *ids: jnp.concatenate([jnp.pad(jnp.stack(ids), ((0, 16 - len(ids)), (0, half - tok)))])
     source_ids = source_ids.astype(jnp.bfloat16)
     (token,) = stand(token)
-    token, acts_there = tie(token, acts_there)
-    acts_here = turned(acts_there, cols)
-    (token,) = stand(token)
-    token, grads_here, basis_in, basis_out = tie(token, grads_here, basis_in, basis_out)
+    token, grads_here, basis_in, basis_out, acts = tie(token, grads_here, basis_in, basis_out, acts)
+    acts_here = turned(acts)
     grads_far = swap(grads_here, "row")
     mine = lax.dynamic_slice_in_dim(basis_in, k * half, half, axis=1)
     first, second = jnp.where(k == low, mine, theirs), jnp.where(k == low, theirs, mine)

time: 121 us -> 120 us (level)
  starting transfers between devices: 35.7 us -> 42.5 us
  waiting for transfers between devices: 51 us -> 45.5 us
  local copies, waits for them, and re-layouts: 7.03 us -> 4.84 us
    ppermute x17 -> x16, starting transfers between devices: 27.1 us -> 39.5 us  [swap(): lax.ppermute(x, axis, [(i, i ^ step) for i in range(lax.axis_size(axis))])]
    ppermute x2, starting transfers between devices: 7.21 us -> 2.97 us  [turned(): return lax.ppermute(x, PLANE, pairs)]
    ppermute x1, waiting for transfers between devices: 6.09 us -> 3.56 us  [local_pairs(): lax.ppermute(to_both, ('seq', 'row'), [(i * rows + j, (i ^ 1) * rows + (j...]
    ppermute x2, waiting for transfers between devices: 2.19 us -> 0.01 us  [turned(): return lax.ppermute(x, PLANE, pairs)]
    unnamed x6, local copies, waits for them, and re-layouts: 2.2 us -> 0.02 us
    ppermute x1, starting transfers between devices: 1.39 us -> 0.01 us  [local_pairs(): lax.ppermute(to_both, ('seq', 'row'), [(i * rows + j, (i ^ 1) * rows + (j...]
    ppermute x17 -> x16, waiting for transfers between devices: 42.7 us -> 41.9 us  [swap(): lax.ppermute(x, axis, [(i, i ^ step) for i in range(lax.axis_size(axis))])]
  transfers between devices with their start and end apart: 20 -> 19, of which waited for: 11 -> 12; matrix products, arithmetic and copies ran while one was open for 6% -> 6% of each run, Pallas kernels for 6% -> 6%
where the time goes in v5:
time: 120 us; the launch traced here: 119 us
  waiting for transfers between devices  45.5 us (38%)
  starting transfers between devices  42.5 us (35%)
  Pallas kernels  11.9 us (10%)
  blocking collectives  10.2 us (8%)
  local copies, waits for them, and re-layouts  4.84 us (4%)
  other arithmetic  3.5 us (3%)
    ppermute x16, waiting for transfers between devices, swap(): lax.ppermute(x, axis, [(i, i ^ step) for i in range(lax.axis_size(axis))])  41.9 us
    ppermute x16, starting transfers between devices, swap(): lax.ppermute(x, axis, [(i, i ^ step) for i in range(lax.axis_size(axis))])  39.5 us
    all_to_all x1, blocking collectives, local_pairs(): lax.all_to_all(message, PLANE, split_axis=0, concat_axis=0, tiled=True)  10.2 us
    pallas_call x2, Pallas kernels, rotate(): pl.pallas_call(functools.partial(rotate_kernel, notes=len(note), flips=fl...  4.31 us
    pallas_call x1, Pallas kernels, outer_near(): pl.pallas_call(near_kernel, out_shape=(jax.ShapeDtypeStruct(eigvals.shape...  3.96 us
    ppermute x1, waiting for transfers between devices, local_pairs(): lax.ppermute(to_both, ('seq', 'row'), [(i * rows + j, (i ^ 1) * rows + (j...  3.56 us
    ppermute x2, starting transfers between devices, turned(): return lax.ppermute(x, PLANE, pairs)  2.97 us
  transfers between devices with their start and end apart: 19, of which 12 were waited for; matrix products, arithmetic and copies ran while one was open for 6% of the time, Pallas kernels for 6%

profile of v5, /device:TPU:0, one launch (start us, length us, event | category | flops | bytes accessed | tf_op | source)
XLA Modules:
  0.0 119.1 jit_solution(1525448739856065744)
XLA Ops:
  0.6 1.6 %collective-permute-start = (bf16[128,1024]{1,0:T(8,128)(2,1)}, bf16[128,1024]{1,0:T(8,128)(2,1)S(1)}, u32[]{:S(2)}, u32[]{:S(2)}) collective-permute-start(bf16[128,1024]{1,0:T(8,128)(2,1)} %param.9), channel_id=1, source_target_pairs={{0,0},{1,4},{2,8},{3,12},{4,2},{5,6},{6,10},{7,14},{8,1},{9,5},{10... | collective-permute-start | bytes 786440 | tf_op jit(solution)/shard_map/ppermute | solution.py:338
  2.2 2.3 %constant_dynamic-slice_fusion.8 = bf16[1024,512]{1,0:T(8,128)(2,1)} fusion(bf16[1024,1024]{1,0:T(8,128)(2,1)} %param.11, s32[]{:T(128)S(6)} %select_n.93), kind=kLoop, calls=%fused_computation.24 | loop fusion | bytes 2097156 | tf_op jit(solution)/shard_map/dynamic_slice | solution.py:347
  4.5 3.5 %collective-permute-start.2 = (bf16[1024,512]{1,0:T(8,128)(2,1)}, bf16[1024,512]{1,0:T(8,128)(2,1)S(1)}, u32[]{:S(2)}, u32[]{:S(2)}) collective-permute-start(bf16[1024,512]{1,0:T(8,128)(2,1)} %constant_dynamic-slice_fusion.8), channel_id=1, source_target_pairs={{0,1},{1,0},{2,3},{3,2},{4,5},{5,4},{6,7},{7,6},{8,9},{9,8},{10,11... | collective-permute-start | bytes 3145736 | tf_op jit(solution)/shard_map/ppermute | solution.py:117
  8.0 1.7 %constant_dynamic-slice_fusion.10 = (bf16[1024,512]{1,0:T(8,128)(2,1)S(1)}, bf16[1024,512]{1,0:T(8,128)(2,1)S(1)}) fusion(bf16[1024,1024]{1,0:T(8,128)(2,1)} %param.12, s32[]{:T(128)S(6)} %select_n.89, s32[]{:T(128)S(6)} %select_n.90), kind=kLoop, calls=%fused_computation.26 | loop fusion | bytes 4194312 | tf_op jit(solution)/shard_map/dynamic_slice | solution.py:349
  9.6 0.0 copy-start.1
  9.7 0.3 pad_maximum_fusion.basis
  9.9 0.0 copy-start
  9.9 0.0 collective-permute-done.x0
  9.9 5.4 %collective-permute-start.1 = (bf16[128,1024]{1,0:T(8,128)(2,1)S(1)}, bf16[128,1024]{1,0:T(8,128)(2,1)S(1)}, u32[]{:S(2)}, u32[]{:S(2)}) collective-permute-start(bf16[128,1024]{1,0:T(8,128)(2,1)S(1)} %collective-permute-done.x0), channel_id=1, source_target_pairs={{0,2},{2,0},{1,3},{3,1},{4,6},{6,4},{5,7},{7,5},{8,10},{10,8},{9,1... | collective-permute-start | bytes 786440 | tf_op jit(solution)/shard_map/ppermute | solution.py:117
  15.4 1.4 %collective-permute-start.3 = (bf16[128,1024]{1,0:T(8,128)(2,1)S(1)}, bf16[128,1024]{1,0:T(8,128)(2,1)}, u32[]{:S(2)}, u32[]{:S(2)}) collective-permute-start(bf16[128,1024]{1,0:T(8,128)(2,1)S(1)} %copy-done.1), channel_id=1, source_target_pairs={{0,0},{1,4},{2,8},{3,12},{4,2},{5,6},{6,10},{7,14},{8,1},{9,5},{10... | collective-permute-start | bytes 786440 | tf_op jit(solution)/shard_map/ppermute | solution.py:338
  16.7 0.0 collective-permute-done.2
  16.7 0.0 copy-done
  16.7 0.5 broadcast_select_fusion
  17.3 0.8 fusion
  18.1 0.1 fusion.2
  18.2 0.1 fusion.3
  18.3 0.0 copy-start.2
  18.3 0.3 pad_maximum_fusion.1.basis
  18.6 1.1 collective-permute-done.1.x1
  19.7 5.1 %collective-permute-start.4 = (bf16[128,1024]{1,0:T(8,128)(2,1)S(1)}, bf16[128,1024]{1,0:T(8,128)(2,1)S(1)}, u32[]{:S(2)}, u32[]{:S(2)}) collective-permute-start(bf16[128,1024]{1,0:T(8,128)(2,1)S(1)} %collective-permute-done.x0), channel_id=1, source_target_pairs={{0,1},{1,0},{2,3},{3,2},{4,5},{5,4},{6,7},{7,6},{8,9},{9,8},{10,11... | collective-permute-start | bytes 786440 | tf_op jit(solution)/shard_map/ppermute | solution.py:117
  24.8 0.1 collective-permute-start.5
  24.9 0.0 collective-permute-done.3.x0
  24.9 1.1 collective-permute-done.4.x2
  26.0 0.4 collective-permute-done.5.x3
  26.4 2.0 %rotate.2 = (bf16[528,512]{1,0:T(8,128)(2,1)}, f32[512,512]{1,0:T(8,128)S(1)}) custom-call(bf16[128,1024]{1,0:T(8,128)(2,1)S(1)} %collective-permute-done.x0, bf16[128,1024]{1,0:T(8,128)(2,1)S(1)} %collective-permute-done.1.x1, bf16[128,1024]{1,0:T(8,128)(2,1)S(1)} %collective-permute-done.4.x2, bf16[128,1024]{1,0:T(8,128)(2,1)S(1)} %collective-permute-done.5.x3, ...), custom_call_target="tpu_custom_call" | custom-call | flops 1073741824 | bytes 2097152 | tf_op jit(solution)/shard_map/rotate/pallas_call | solution.py:165
  28.3 5.8 %collective-permute-start.6 = (bf16[128,1024]{1,0:T(8,128)(2,1)}, bf16[128,1024]{1,0:T(8,128)(2,1)S(1)}, u32[]{:S(2)}, u32[]{:S(2)}) collective-permute-start(bf16[128,1024]{1,0:T(8,128)(2,1)} %collective-permute-done.3.x0), channel_id=1, source_target_pairs={{0,2},{2,0},{1,3},{3,1},{4,6},{6,4},{5,7},{7,5},{8,10},{10,8},{9,1... | collective-permute-start | bytes 786440 | tf_op jit(solution)/shard_map/ppermute | solution.py:117
  34.1 4.7 %collective-permute-start.9 = (bf16[528,512]{1,0:T(8,128)(2,1)}, bf16[528,512]{1,0:T(8,128)(2,1)}, u32[]{:S(2)}, u32[]{:S(2)}) collective-permute-start(bf16[528,512]{1,0:T(8,128)(2,1)} %get-tuple-element.72), channel_id=1, source_target_pairs={{0,4},{4,0},{8,12},{12,8},{1,5},{5,1},{9,13},{13,9},{2,6},{6,2},{1... | collective-permute-start | bytes 1622024 | tf_op jit(solution)/shard_map/ppermute | solution.py:117
  38.8 0.0 collective-permute-done.6.x1
  38.8 5.2 %collective-permute-start.7 = (bf16[128,1024]{1,0:T(8,128)(2,1)}, bf16[128,1024]{1,0:T(8,128)(2,1)}, u32[]{:S(2)}, u32[]{:S(2)}) collective-permute-start(bf16[128,1024]{1,0:T(8,128)(2,1)} %collective-permute-done.3.x0), channel_id=1, source_target_pairs={{0,1},{1,0},{2,3},{3,2},{4,5},{5,4},{6,7},{7,6},{8,9},{9,8},{10,11... | collective-permute-start | bytes 786440 | tf_op jit(solution)/shard_map/ppermute | solution.py:117
  44.0 0.0 collective-permute-start.8
  44.0 1.8 %collective-permute-done.7.x2 = bf16[128,1024]{1,0:T(8,128)(2,1)} collective-permute-done((bf16[128,1024]{1,0:T(8,128)(2,1)}, bf16[128,1024]{1,0:T(8,128)(2,1)}, u32[]{:S(2)}, u32[]{:S(2)}) %collective-permute-start.7) | collective-permute-done | bytes 262176 | tf_op jit(solution)/shard_map/ppermute | solution.py:117
  45.8 0.0 collective-permute-done.8.x3
  45.8 2.4 %rotate.3 = (bf16[512,256]{1,0:T(8,128)(2,1)S(1)}, bf16[512,256]{1,0:T(8,128)(2,1)S(1)}, bf16[512,256]{1,0:T(8,128)(2,1)S(1)}, f32[512,256]{1,0:T(8,128)S(1)}) custom-call(bf16[128,1024]{1,0:T(8,128)(2,1)} %collective-permute-done.3.x0, bf16[128,1024]{1,0:T(8,128)(2,1)S(1)} %collective-permute-done.6.x1, bf16[128,1024]{1,0:T(8,128)(2,1)} %collective-permute-done.7.x2, ...), custom_call_target="tpu_custom_call" | custom-call | flops 1073741824 | bytes 2097152 | tf_op jit(solution)/shard_map/rotate/pallas_call | solution.py:165
  48.2 0.4 collective-permute-start.10
  48.5 4.1 %collective-permute-start.11 = (bf16[512,256]{1,0:T(8,128)(2,1)S(1)}, bf16[512,256]{1,0:T(8,128)(2,1)S(1)}, u32[]{:S(2)}, u32[]{:S(2)}) collective-permute-start(bf16[512,256]{1,0:T(8,128)(2,1)S(1)} %get-tuple-element.78), channel_id=1, source_target_pairs={{0,4},{4,0},{8,12},{12,8},{1,5},{5,1},{9,13},{13,9},{2,6},{6,2},{1... | collective-permute-start | bytes 786440 | tf_op jit(solution)/shard_map/ppermute | solution.py:117
  52.6 0.0 collective-permute-start.12
  52.6 0.0 collective-permute-done.9.got
  52.6 1.1 shard_map.85.pair
  53.8 1.6 %collective-permute-start.13 = (bf16[528,512]{1,0:T(8,128)(2,1)S(1)}, bf16[528,512]{1,0:T(8,128)(2,1)S(1)}, u32[]{:S(2)}, u32[]{:S(2)}) collective-permute-start(bf16[528,512]{1,0:T(8,128)(2,1)S(1)} %shard_map.85.pair), channel_id=1, source_target_pairs={{0,8},{4,12},{8,0},{12,4},{1,9},{5,13},{9,1},{13,5},{2,10},{6,14},... | collective-permute-start | bytes 1622024 | tf_op jit(solution)/shard_map/ppermute | solution.py:117
  55.4 1.4 %collective-permute-done.10 = bf16[512,256]{1,0:T(8,128)(2,1)S(1)} collective-permute-done((bf16[512,256]{1,0:T(8,128)(2,1)S(1)}, bf16[512,256]{1,0:T(8,128)(2,1)S(1)}, u32[]{:S(2)}, u32[]{:S(2)}) %collective-permute-start.10) | collective-permute-done | bytes 262176 | tf_op jit(solution)/shard_map/ppermute | solution.py:117
  56.8 11.6 %collective-permute-done.11 = bf16[512,256]{1,0:T(8,128)(2,1)S(1)} collective-permute-done((bf16[512,256]{1,0:T(8,128)(2,1)S(1)}, bf16[512,256]{1,0:T(8,128)(2,1)S(1)}, u32[]{:S(2)}, u32[]{:S(2)}) %collective-permute-start.11) | collective-permute-done | bytes 262176 | tf_op jit(solution)/shard_map/ppermute | solution.py:117
  68.4 3.6 %collective-permute-done.12 = bf16[512,256]{1,0:T(8,128)(2,1)S(1)} collective-permute-done((bf16[512,256]{1,0:T(8,128)(2,1)S(1)}, bf16[512,256]{1,0:T(8,128)(2,1)S(1)}, u32[]{:S(2)}, u32[]{:S(2)}) %collective-permute-start.12) | collective-permute-done | bytes 262176 | tf_op jit(solution)/shard_map/ppermute | solution.py:375
  71.9 0.1 select_convert_fusion
  72.1 2.2 %collective-permute-start.14 = (bf16[512,256]{1,0:T(8,128)(2,1)S(1)}, bf16[512,256]{1,0:T(8,128)(2,1)S(1)}, u32[]{:S(2)}, u32[]{:S(2)}) collective-permute-start(bf16[512,256]{1,0:T(8,128)(2,1)S(1)} %select_convert_fusion), channel_id=1, source_target_pairs={{0,8},{4,12},{8,0},{12,4},{1,9},{5,13},{9,1},{13,5},{2,10},{6,14},... | collective-permute-start | bytes 786440 | tf_op jit(solution)/shard_map/ppermute | solution.py:117
  74.3 12.8 %collective-permute-done.13.across = bf16[528,512]{1,0:T(8,128)(2,1)S(1)} collective-permute-done((bf16[528,512]{1,0:T(8,128)(2,1)S(1)}, bf16[528,512]{1,0:T(8,128)(2,1)S(1)}, u32[]{:S(2)}, u32[]{:S(2)}) %collective-permute-start.13) | collective-permute-done | bytes 540704 | tf_op jit(solution)/shard_map/ppermute | solution.py:117
  87.1 0.1 shard_map.86.g
  87.3 4.1 %collective-permute-done.14 = bf16[512,256]{1,0:T(8,128)(2,1)S(1)} collective-permute-done((bf16[512,256]{1,0:T(8,128)(2,1)S(1)}, bf16[512,256]{1,0:T(8,128)(2,1)S(1)}, u32[]{:S(2)}, u32[]{:S(2)}) %collective-permute-start.14) | collective-permute-done | bytes 262176 | tf_op jit(solution)/shard_map/ppermute | solution.py:117
  91.4 0.2 add_convert_fusion.a0
  91.6 1.5 %collective-permute-start.15 = (bf16[512,256]{1,0:T(8,128)(2,1)S(1)}, bf16[512,256]{1,0:T(8,128)(2,1)S(1)}, u32[]{:S(2)}, u32[]{:S(2)}) collective-permute-start(bf16[512,256]{1,0:T(8,128)(2,1)S(1)} %add_convert_fusion.a0), channel_id=1, source_target_pairs={{0,2},{2,0},{1,3},{3,1},{4,6},{6,4},{5,7},{7,5},{8,10},{10,8},{9,1... | collective-permute-start | bytes 786440 | tf_op jit(solution)/shard_map/ppermute | solution.py:117
  93.1 0.0 collective-permute-start.18
  93.1 0.1 pad_add_fusion.place
  93.1 0.7 slice.30
  93.8 0.0 collective-permute-start.16
  93.8 4.8 %collective-permute-done.15.a1 = bf16[512,256]{1,0:T(8,128)(2,1)S(1)} collective-permute-done((bf16[512,256]{1,0:T(8,128)(2,1)S(1)}, bf16[512,256]{1,0:T(8,128)(2,1)S(1)}, u32[]{:S(2)}, u32[]{:S(2)}) %collective-permute-start.15) | collective-permute-done | bytes 262176 | tf_op jit(solution)/shard_map/ppermute | solution.py:117
  98.6 0.0 collective-permute-start.17
  98.7 0.0 collective-permute-done.16.a2
  98.7 1.5 %collective-permute-done.17.a3 = bf16[512,256]{1,0:T(8,128)(2,1)S(1)} collective-permute-done((bf16[512,256]{1,0:T(8,128)(2,1)S(1)}, bf16[512,256]{1,0:T(8,128)(2,1)S(1)}, u32[]{:S(2)}, u32[]{:S(2)}) %collective-permute-start.17) | collective-permute-done | bytes 262176 | tf_op jit(solution)/shard_map/ppermute | solution.py:117
  100.2 4.0 %outer_near.1 = (f32[1024,1024]{1,0:T(8,128)}, f32[512,128]{1,0:T(8,128)S(1)}, bf16[512,1024]{1,0:T(8,128)(2,1)S(1)}, bf16[1024,512]{1,0:T(8,128)(2,1)S(1)}, f32[1024,512]{1,0:T(8,128)S(1)}) custom-call(s32[3]{0:T(128)S(1)} %pad_add_fusion.place, bf16[512,256]{1,0:T(8,128)(2,1)S(1)} %add_convert_fusion.a0, bf16[512,256]{1,0:T(8,128)(2,1)S(1)} %collective-permute-done.15.a1, ...), custom_call_target="tpu_custom_call" | custom-call | flops 1073741824 | bytes 6291456 | tf_op jit(solution)/shard_map/outer_near/pallas_call | solution.py:267
  104.1 1.2 %collective-permute-done.18.g = bf16[512,512]{1,0:T(8,128)(2,1)S(1)} collective-permute-done((bf16[512,512]{1,0:T(8,128)(2,1)S(1)}, bf16[512,512]{1,0:T(8,128)(2,1)S(1)}, u32[]{:S(2)}, u32[]{:S(2)}) %collective-permute-start.18) | collective-permute-done | bytes 524320 | tf_op jit(solution)/shard_map/ppermute | solution.py:117
  105.3 2.3 %outer_far.1 = (f32[1024,1024]{1,0:T(8,128)}, f32[4,128]{1,0:T(4,128)S(1)}) custom-call(s32[3]{0:T(128)S(1)} %pad_add_fusion.place, bf16[512,1024]{1,0:T(8,128)(2,1)S(1)} %get-tuple-element.90.flat, bf16[1024,512]{1,0:T(8,128)(2,1)S(1)} %get-tuple-element.91.turned, bf16[512,512]{1,0:T(8,128)(2,1)S(1)} %collective-permute-done.18.g, ...), custom_call_target="tpu_custom_call", output_to_operand_aliasing={{0}: (5, {})} | custom-call | flops 1073741824 | bytes 2097152 | tf_op jit(solution)/shard_map/outer_far/pallas_call | solution.py:298
  107.7 0.1 select_reduce_fusion
  107.9 10.2 %all_to_all.9 = f32[16,1,136]{2,1,0:T(1,128)S(1)} all-to-all(f32[16,1,136]{2,1,0:T(1,128)S(1)} %all_to_all.6), channel_id=1, replica_groups=mesh['grp'=2,'seq'=4,'row'=2,'col'=2] {'seq','row','col'}, dimensions={0} | all-to-all | bytes 17408 | tf_op jit(solution)/shard_map/all_to_all | solution.py:413
  118.1 0.5 slice_multiply_fusion
  118.6 0.5 slice_multiply_fusion.1
  (20 shorter events, 0.2 us)
Async XLA Ops:
  0.6 9.3 %collective-permute-start = (bf16[128,1024]{1,0:T(8,128)(2,1)}, bf16[128,1024]{1,0:T(8,128)(2,1)S(1)}, u32[]{:S(2)}, u32[]{:S(2)}) collective-permute-start(bf16[128,1024]{1,0:T(8,128)(2,1)} %param.9), channel_id=1, source_target_pairs={{0,0},{1,4},{2,8},{3,12},{4,2},{5,6},{6,10},{7,14},{8,1},{9,5},{10... | collective-permute-start | bytes 786440 | tf_op jit(solution)/shard_map/ppermute | solution.py:338
  4.5 12.2 %collective-permute-start.2 = (bf16[1024,512]{1,0:T(8,128)(2,1)}, bf16[1024,512]{1,0:T(8,128)(2,1)S(1)}, u32[]{:S(2)}, u32[]{:S(2)}) collective-permute-start(bf16[1024,512]{1,0:T(8,128)(2,1)} %constant_dynamic-slice_fusion.8), channel_id=1, source_target_pairs={{0,1},{1,0},{2,3},{3,2},{4,5},{5,4},{6,7},{7,6},{8,9},{9,8},{10,11... | collective-permute-start | bytes 3145736 | tf_op jit(solution)/shard_map/ppermute | solution.py:117
  9.6 5.7 %copy-start.1 = (bf16[128,1024]{1,0:T(8,128)(2,1)S(1)}, bf16[128,1024]{1,0:T(8,128)(2,1)}, u32[]{:S(2)}) copy-start(bf16[128,1024]{1,0:T(8,128)(2,1)} %param.8) | copy-start | bytes 786436
  9.9 6.8 %copy-start = (bf16[1024,1024]{1,0:T(8,128)(2,1)S(1)}, bf16[1024,1024]{1,0:T(8,128)(2,1)}, u32[]{:S(2)}) copy-start(bf16[1024,1024]{1,0:T(8,128)(2,1)} %param.11) | copy-start | bytes 6291460
  9.9 9.8 %collective-permute-start.1 = (bf16[128,1024]{1,0:T(8,128)(2,1)S(1)}, bf16[128,1024]{1,0:T(8,128)(2,1)S(1)}, u32[]{:S(2)}, u32[]{:S(2)}) collective-permute-start(bf16[128,1024]{1,0:T(8,128)(2,1)S(1)} %collective-permute-done.x0), channel_id=1, source_target_pairs={{0,2},{2,0},{1,3},{3,1},{4,6},{6,4},{5,7},{7,5},{8,10},{10,8},{9,1... | collective-permute-start | bytes 786440 | tf_op jit(solution)/shard_map/ppermute | solution.py:117
  15.4 9.6 %collective-permute-start.3 = (bf16[128,1024]{1,0:T(8,128)(2,1)S(1)}, bf16[128,1024]{1,0:T(8,128)(2,1)}, u32[]{:S(2)}, u32[]{:S(2)}) collective-permute-start(bf16[128,1024]{1,0:T(8,128)(2,1)S(1)} %copy-done.1), channel_id=1, source_target_pairs={{0,0},{1,4},{2,8},{3,12},{4,2},{5,6},{6,10},{7,14},{8,1},{9,5},{10... | collective-permute-start | bytes 786440 | tf_op jit(solution)/shard_map/ppermute | solution.py:338
  18.3 6.7 %copy-start.2 = (s32[128]{0:T(128)S(1)}, s32[128]{0:T(128)}, u32[]{:S(2)}) copy-start(s32[128]{0:T(128)} %param.10) | copy-start | bytes 1540
  19.7 6.3 %collective-permute-start.4 = (bf16[128,1024]{1,0:T(8,128)(2,1)S(1)}, bf16[128,1024]{1,0:T(8,128)(2,1)S(1)}, u32[]{:S(2)}, u32[]{:S(2)}) collective-permute-start(bf16[128,1024]{1,0:T(8,128)(2,1)S(1)} %collective-permute-done.x0), channel_id=1, source_target_pairs={{0,1},{1,0},{2,3},{3,2},{4,5},{5,4},{6,7},{7,6},{8,9},{9,8},{10,11... | collective-permute-start | bytes 786440 | tf_op jit(solution)/shard_map/ppermute | solution.py:117
  24.8 1.5 %collective-permute-start.5 = (bf16[128,1024]{1,0:T(8,128)(2,1)S(1)}, bf16[128,1024]{1,0:T(8,128)(2,1)S(1)}, u32[]{:S(2)}, u32[]{:S(2)}) collective-permute-start(bf16[128,1024]{1,0:T(8,128)(2,1)S(1)} %collective-permute-done.1.x1), channel_id=1, source_target_pairs={{0,1},{1,0},{2,3},{3,2},{4,5},{5,4},{6,7},{7,6},{8,9},{9,8},{10,11... | collective-permute-start | bytes 786440 | tf_op jit(solution)/shard_map/ppermute | solution.py:117
  28.3 10.5 %collective-permute-start.6 = (bf16[128,1024]{1,0:T(8,128)(2,1)}, bf16[128,1024]{1,0:T(8,128)(2,1)S(1)}, u32[]{:S(2)}, u32[]{:S(2)}) collective-permute-start(bf16[128,1024]{1,0:T(8,128)(2,1)} %collective-permute-done.3.x0), channel_id=1, source_target_pairs={{0,2},{2,0},{1,3},{3,1},{4,6},{6,4},{5,7},{7,5},{8,10},{10,8},{9,1... | collective-permute-start | bytes 786440 | tf_op jit(solution)/shard_map/ppermute | solution.py:117
  34.1 18.5 %collective-permute-start.9 = (bf16[528,512]{1,0:T(8,128)(2,1)}, bf16[528,512]{1,0:T(8,128)(2,1)}, u32[]{:S(2)}, u32[]{:S(2)}) collective-permute-start(bf16[528,512]{1,0:T(8,128)(2,1)} %get-tuple-element.72), channel_id=1, source_target_pairs={{0,4},{4,0},{8,12},{12,8},{1,5},{5,1},{9,13},{13,9},{2,6},{6,2},{1... | collective-permute-start | bytes 1622024 | tf_op jit(solution)/shard_map/ppermute | solution.py:117
  38.8 7.0 %collective-permute-start.7 = (bf16[128,1024]{1,0:T(8,128)(2,1)}, bf16[128,1024]{1,0:T(8,128)(2,1)}, u32[]{:S(2)}, u32[]{:S(2)}) collective-permute-start(bf16[128,1024]{1,0:T(8,128)(2,1)} %collective-permute-done.3.x0), channel_id=1, source_target_pairs={{0,1},{1,0},{2,3},{3,2},{4,5},{5,4},{6,7},{7,6},{8,9},{9,8},{10,11... | collective-permute-start | bytes 786440 | tf_op jit(solution)/shard_map/ppermute | solution.py:117
  44.0 1.8 %collective-permute-start.8 = (bf16[128,1024]{1,0:T(8,128)(2,1)S(1)}, bf16[128,1024]{1,0:T(8,128)(2,1)}, u32[]{:S(2)}, u32[]{:S(2)}) collective-permute-start(bf16[128,1024]{1,0:T(8,128)(2,1)S(1)} %collective-permute-done.6.x1), channel_id=1, source_target_pairs={{0,1},{1,0},{2,3},{3,2},{4,5},{5,4},{6,7},{7,6},{8,9},{9,8},{10,11... | collective-permute-start | bytes 786440 | tf_op jit(solution)/shard_map/ppermute | solution.py:117
  48.2 8.7 %collective-permute-start.10 = (bf16[512,256]{1,0:T(8,128)(2,1)S(1)}, bf16[512,256]{1,0:T(8,128)(2,1)S(1)}, u32[]{:S(2)}, u32[]{:S(2)}) collective-permute-start(bf16[512,256]{1,0:T(8,128)(2,1)S(1)} %get-tuple-element.77), channel_id=1, source_target_pairs={{0,2},{2,0},{1,3},{3,1},{4,6},{6,4},{5,7},{7,5},{8,10},{10,8},{9,1... | collective-permute-start | bytes 786440 | tf_op jit(solution)/shard_map/ppermute | solution.py:117
  48.5 19.9 %collective-permute-start.11 = (bf16[512,256]{1,0:T(8,128)(2,1)S(1)}, bf16[512,256]{1,0:T(8,128)(2,1)S(1)}, u32[]{:S(2)}, u32[]{:S(2)}) collective-permute-start(bf16[512,256]{1,0:T(8,128)(2,1)S(1)} %get-tuple-element.78), channel_id=1, source_target_pairs={{0,4},{4,0},{8,12},{12,8},{1,5},{5,1},{9,13},{13,9},{2,6},{6,2},{1... | collective-permute-start | bytes 786440 | tf_op jit(solution)/shard_map/ppermute | solution.py:117
  52.6 19.3 %collective-permute-start.12 = (bf16[512,256]{1,0:T(8,128)(2,1)S(1)}, bf16[512,256]{1,0:T(8,128)(2,1)S(1)}, u32[]{:S(2)}, u32[]{:S(2)}) collective-permute-start(bf16[512,256]{1,0:T(8,128)(2,1)S(1)} %get-tuple-element.79), channel_id=1, source_target_pairs={{0,6},{2,4},{4,2},{6,0},{8,14},{10,12},{12,10},{14,8},{1,7},{3,5},... | collective-permute-start | bytes 786440 | tf_op jit(solution)/shard_map/ppermute | solution.py:375
  53.8 33.4 %collective-permute-start.13 = (bf16[528,512]{1,0:T(8,128)(2,1)S(1)}, bf16[528,512]{1,0:T(8,128)(2,1)S(1)}, u32[]{:S(2)}, u32[]{:S(2)}) collective-permute-start(bf16[528,512]{1,0:T(8,128)(2,1)S(1)} %shard_map.85.pair), channel_id=1, source_target_pairs={{0,8},{4,12},{8,0},{12,4},{1,9},{5,13},{9,1},{13,5},{2,10},{6,14},... | collective-permute-start | bytes 1622024 | tf_op jit(solution)/shard_map/ppermute | solution.py:117
  72.1 19.3 %collective-permute-start.14 = (bf16[512,256]{1,0:T(8,128)(2,1)S(1)}, bf16[512,256]{1,0:T(8,128)(2,1)S(1)}, u32[]{:S(2)}, u32[]{:S(2)}) collective-permute-start(bf16[512,256]{1,0:T(8,128)(2,1)S(1)} %select_convert_fusion), channel_id=1, source_target_pairs={{0,8},{4,12},{8,0},{12,4},{1,9},{5,13},{9,1},{13,5},{2,10},{6,14},... | collective-permute-start | bytes 786440 | tf_op jit(solution)/shard_map/ppermute | solution.py:117
  91.6 7.0 %collective-permute-start.15 = (bf16[512,256]{1,0:T(8,128)(2,1)S(1)}, bf16[512,256]{1,0:T(8,128)(2,1)S(1)}, u32[]{:S(2)}, u32[]{:S(2)}) collective-permute-start(bf16[512,256]{1,0:T(8,128)(2,1)S(1)} %add_convert_fusion.a0), channel_id=1, source_target_pairs={{0,2},{2,0},{1,3},{3,1},{4,6},{6,4},{5,7},{7,5},{8,10},{10,8},{9,1... | collective-permute-start | bytes 786440 | tf_op jit(solution)/shard_map/ppermute | solution.py:117
  93.1 12.3 %collective-permute-start.18 = (bf16[512,512]{1,0:T(8,128)(2,1)S(1)}, bf16[512,512]{1,0:T(8,128)(2,1)S(1)}, u32[]{:S(2)}, u32[]{:S(2)}) collective-permute-start(bf16[512,512]{1,0:T(8,128)(2,1)S(1)} %shard_map.86.g), channel_id=1, source_target_pairs={{0,4},{4,0},{8,12},{12,8},{1,5},{5,1},{9,13},{13,9},{2,6},{6,2},{1... | collective-permute-start | bytes 1572872 | tf_op jit(solution)/shard_map/ppermute | solution.py:117
  93.8 4.9 %collective-permute-start.16 = (bf16[512,256]{1,0:T(8,128)(2,1)S(1)}, bf16[512,256]{1,0:T(8,128)(2,1)S(1)}, u32[]{:S(2)}, u32[]{:S(2)}) collective-permute-start(bf16[512,256]{1,0:T(8,128)(2,1)S(1)} %add_convert_fusion.a0), channel_id=1, source_target_pairs={{0,1},{1,0},{2,3},{3,2},{4,5},{5,4},{6,7},{7,6},{8,9},{9,8},{10,11... | collective-permute-start | bytes 786440 | tf_op jit(solution)/shard_map/ppermute | solution.py:117
  98.6 1.5 %collective-permute-start.17 = (bf16[512,256]{1,0:T(8,128)(2,1)S(1)}, bf16[512,256]{1,0:T(8,128)(2,1)S(1)}, u32[]{:S(2)}, u32[]{:S(2)}) collective-permute-start(bf16[512,256]{1,0:T(8,128)(2,1)S(1)} %collective-permute-done.15.a1), channel_id=1, source_target_pairs={{0,1},{1,0},{2,3},{3,2},{4,5},{5,4},{6,7},{7,6},{8,9},{9,8},{10,11... | collective-permute-start | bytes 786440 | tf_op jit(solution)/shard_map/ppermute | solution.py:117

commit v6 on v4

--- a/solution.py
+++ b/solution.py
@@ -106,6 +106,7 @@
 
 
 VMEM = 16 * 2**20
+NEAR_VMEM = 48 * 2**20
 ROTATE_VMEM = 10 * 2**20
 LANES = 128
 STAND = 2 * 10**10
@@ -258,6 +259,12 @@
         value[j : j + 1, :] = jnp.sum(score[j * tok : (j + 1) * tok, :].T, axis=0, keepdims=True)
 
 
+def finish_kernel(scale_score, scale_influence, parts, scores, influence):
+    tok = scores.shape[0]
+    scores[...] = jnp.sum(parts[:, :tok], axis=0) * scale_score
+    influence[...] = jnp.sum(parts[:, tok:], axis=0) * scale_influence
+
+
 def outer_near(place, acts, grads, eigvals):
     width = eigvals.shape[0]
     tokens, cols = grads.shape
@@ -282,7 +289,7 @@
             pltpu.SemaphoreType.DMA((BLOCKS,)),
             pltpu.SemaphoreType.DMA((7,)),
         ],
-        compiler_params=pltpu.CompilerParams(vmem_limit_bytes=VMEM),
+        compiler_params=pltpu.CompilerParams(vmem_limit_bytes=NEAR_VMEM),
         cost_estimate=pl.CostEstimate(
             flops=4 * tokens * width * cols, bytes_accessed=12 * width * cols, transcendentals=0
         ),
@@ -350,8 +357,6 @@
     )
     note = lambda *ids: jnp.concatenate([jnp.pad(jnp.stack(ids), ((0, 16 - len(ids)), (0, half - tok)))])
     source_ids = source_ids.astype(jnp.bfloat16)
-    (token,) = stand(token)
-    token, acts_there = tie(token, acts_there)
     acts_here = turned(acts_there, cols)
     (token,) = stand(token)
     token, grads_here, basis_in, basis_out = tie(token, grads_here, basis_in, basis_out)
@@ -359,7 +364,7 @@
     mine = lax.dynamic_slice_in_dim(basis_in, k * half, half, axis=1)
     first, second = jnp.where(k == low, mine, theirs), jnp.where(k == low, theirs, mine)
     first, second = (jnp.roll(t, -(1 - x) * piece, axis=1) for t in (first, second))
-    tiles = jnp.concatenate([first[:, :piece], second[:, piece:], second[:, :piece], first[:, piece:]], axis=1)
+    tiles = jnp.concatenate([second[:, piece:], second[:, :piece], first[:, :piece], first[:, piece:]], axis=1)
     (token,) = stand(token)
     token, grads_far, tiles, grads_here = tie(token, grads_far, tiles, grads_here)
     grads_both = swap(grads_far, "col")
@@ -373,7 +378,7 @@
     token, acts_far, acts_here = tie(token, acts_far, acts_here)
     acts_both = swap(acts_far, "col")
     acts_near = swap(acts_here, "col")
-    to_x, to_pair, to_both, keep_a = rotate([acts_here, acts_far, acts_near, acts_both], tiles, 3, flips=(0, 2))
+    to_pair, to_both, to_x, keep_a = rotate([acts_here, acts_far, acts_near, acts_both], tiles, 3, flips=(1, 2))
     from_both = lax.ppermute(
         to_both,
         ("seq", "row"),
@@ -412,10 +417,17 @@
     message = jnp.concatenate([blocks, jnp.broadcast_to(part[None, :], (seqs, SOURCES))], axis=1)
     message = jnp.broadcast_to(message[:, None, :], (seqs, rows * cols, tok + SOURCES))
     message = message.reshape(seqs * rows * cols, tok + SOURCES)
-    summed = jnp.sum(lax.all_to_all(message, PLANE, split_axis=0, concat_axis=0, tiled=True), axis=0)
+    parts = lax.all_to_all(message, PLANE, split_axis=0, concat_axis=0, tiled=True)
     scale_score = float(total_tokens) / float(width * width)
-    scores = summed[:tok] * scale_score
-    influence = summed[tok:] * (scale_score * (float(SOURCES) / float(total_tokens)))
+    vmem = pl.BlockSpec(memory_space=pltpu.VMEM)
+    scores, influence = pl.pallas_call(
+        functools.partial(finish_kernel, scale_score, scale_score * (float(SOURCES) / float(total_tokens))),
+        out_shape=(jax.ShapeDtypeStruct((tok,), jnp.float32), jax.ShapeDtypeStruct((SOURCES,), jnp.float32)),
+        in_specs=[vmem],
+        out_specs=(vmem, vmem),
+        compiler_params=pltpu.CompilerParams(vmem_limit_bytes=2**20),
+        name="finish",
+    )(parts)
     return (precond, scores, influence)
 
 

time: 121 us -> 118 us (0.975)
  starting transfers between devices: 35.7 us -> 31.4 us
  waiting for transfers between devices: 51 us -> 55.1 us
  local copies, waits for them, and re-layouts: 7.03 us -> 4.77 us
    ppermute x17, waiting for transfers between devices: 42.7 us -> 45.9 us  [swap(): lax.ppermute(x, axis, [(i, i ^ step) for i in range(lax.axis_size(axis))])]
    ppermute x2, starting transfers between devices: 7.21 us -> 4.8 us  [turned(): return lax.ppermute(x, PLANE, pairs)]
    unnamed x6 -> x5, local copies, waits for them, and re-layouts: 2.2 us -> 0.01 us
    ppermute x17, starting transfers between devices: 27.1 us -> 25.3 us  [swap(): lax.ppermute(x, axis, [(i, i ^ step) for i in range(lax.axis_size(axis))])]
  transfers between devices with their start and end apart: 20 -> 20, of which waited for: 11 -> 13; matrix products, arithmetic and copies ran while one was open for 6% -> 6% of each run, Pallas kernels for 6% -> 6%
where the time goes in v6:
time: 118 us
  waiting for transfers between devices  55.1 us (47%)
  starting transfers between devices  31.4 us (27%)
  Pallas kernels  12.4 us (11%)
  blocking collectives  10.9 us (9%)
  local copies, waits for them, and re-layouts  4.77 us (4%)
  other arithmetic  2.5 us (2%)
    ppermute x17, waiting for transfers between devices, swap(): lax.ppermute(x, axis, [(i, i ^ step) for i in range(lax.axis_size(axis))])  45.9 us
    ppermute x17, starting transfers between devices, swap(): lax.ppermute(x, axis, [(i, i ^ step) for i in range(lax.axis_size(axis))])  25.3 us
    all_to_all x1, blocking collectives, local_pairs(): lax.all_to_all(message, PLANE, split_axis=0, concat_axis=0, tiled=True)  10.9 us
    ppermute x1, waiting for transfers between devices, local_pairs(): lax.ppermute(to_both, ('seq', 'row'), [(i * rows + j, (i ^ 1) * rows + (j...  6.12 us
    ppermute x2, starting transfers between devices, turned(): return lax.ppermute(x, PLANE, pairs)  4.8 us
    pallas_call x2, Pallas kernels, rotate(): pl.pallas_call(functools.partial(rotate_kernel, notes=len(note), flips=fl...  4.32 us
    pallas_call x1, Pallas kernels, outer_near(): pl.pallas_call(near_kernel, out_shape=(jax.ShapeDtypeStruct(eigvals.shape...  3.96 us
    ppermute x2, waiting for transfers between devices, turned(): return lax.ppermute(x, PLANE, pairs)  3.13 us
  transfers between devices with their start and end apart: 20, of which 13 were waited for; matrix products, arithmetic and copies ran while one was open for 6% of the time, Pallas kernels for 6%

profile of v6, /device:TPU:0, one launch (start us, length us, event | category | flops | bytes accessed | tf_op | source)
XLA Modules:
  0.0 117.9 jit_solution(4996248102150081641)
XLA Ops:
  0.6 1.6 %collective-permute-start = (bf16[128,1024]{1,0:T(8,128)(2,1)}, bf16[128,1024]{1,0:T(8,128)(2,1)S(1)}, u32[]{:S(2)}, u32[]{:S(2)}) collective-permute-start(bf16[128,1024]{1,0:T(8,128)(2,1)} %param.9), channel_id=1, source_target_pairs={{0,0},{1,4},{2,8},{3,12},{4,2},{5,6},{6,10},{7,14},{8,1},{9,5},{10... | collective-permute-start | bytes 786440 | tf_op jit(solution)/shard_map/ppermute | solution.py:344
  2.2 2.3 %constant_dynamic-slice_fusion.8 = bf16[1024,512]{1,0:T(8,128)(2,1)} fusion(bf16[1024,1024]{1,0:T(8,128)(2,1)} %param.11, s32[]{:T(128)S(6)} %select_n.92), kind=kLoop, calls=%fused_computation.25 | loop fusion | bytes 2097156 | tf_op jit(solution)/shard_map/dynamic_slice | solution.py:354
  4.5 3.5 %collective-permute-start.2 = (bf16[1024,512]{1,0:T(8,128)(2,1)}, bf16[1024,512]{1,0:T(8,128)(2,1)S(1)}, u32[]{:S(2)}, u32[]{:S(2)}) collective-permute-start(bf16[1024,512]{1,0:T(8,128)(2,1)} %constant_dynamic-slice_fusion.8), channel_id=1, source_target_pairs={{0,1},{1,0},{2,3},{3,2},{4,5},{5,4},{6,7},{7,6},{8,9},{9,8},{10,11... | collective-permute-start | bytes 3145736 | tf_op jit(solution)/shard_map/ppermute | solution.py:117
  8.0 3.5 %collective-permute-start.3 = (bf16[128,1024]{1,0:T(8,128)(2,1)}, bf16[128,1024]{1,0:T(8,128)(2,1)}, u32[]{:S(2)}, u32[]{:S(2)}) collective-permute-start(bf16[128,1024]{1,0:T(8,128)(2,1)} %param.8), channel_id=1, source_target_pairs={{0,2},{2,0},{1,3},{3,1},{4,6},{6,4},{5,7},{7,5},{8,10},{10,8},{9,1... | collective-permute-start | bytes 786440 | tf_op jit(solution)/shard_map/ppermute | solution.py:117
  11.5 1.7 %constant_dynamic-slice_fusion.10 = (bf16[1024,512]{1,0:T(8,128)(2,1)S(1)}, bf16[1024,512]{1,0:T(8,128)(2,1)S(1)}) fusion(bf16[1024,1024]{1,0:T(8,128)(2,1)} %param.12, s32[]{:T(128)S(6)} %select_n.89, s32[]{:T(128)S(6)} %select_n.90), kind=kLoop, calls=%fused_computation.27 | loop fusion | bytes 4194312 | tf_op jit(solution)/shard_map/dynamic_slice | solution.py:356
  13.1 0.3 pad_maximum_fusion.basis
  13.4 0.0 copy-start
  13.5 0.0 collective-permute-done.x0
  13.5 2.0 %collective-permute-start.1 = (bf16[128,1024]{1,0:T(8,128)(2,1)S(1)}, bf16[128,1024]{1,0:T(8,128)(2,1)S(1)}, u32[]{:S(2)}, u32[]{:S(2)}) collective-permute-start(bf16[128,1024]{1,0:T(8,128)(2,1)S(1)} %collective-permute-done.x0), channel_id=1, source_target_pairs={{0,2},{2,0},{1,3},{3,1},{4,6},{6,4},{5,7},{7,5},{8,10},{10,8},{9,1... | collective-permute-start | bytes 786440 | tf_op jit(solution)/shard_map/ppermute | solution.py:117
  15.5 4.1 %collective-permute-done.3 = bf16[128,1024]{1,0:T(8,128)(2,1)} collective-permute-done((bf16[128,1024]{1,0:T(8,128)(2,1)}, bf16[128,1024]{1,0:T(8,128)(2,1)}, u32[]{:S(2)}, u32[]{:S(2)}) %collective-permute-start.3) | collective-permute-done | bytes 262176 | tf_op jit(solution)/shard_map/ppermute | solution.py:117
  19.5 3.2 %collective-permute-start.4 = (bf16[128,1024]{1,0:T(8,128)(2,1)}, bf16[128,1024]{1,0:T(8,128)(2,1)}, u32[]{:S(2)}, u32[]{:S(2)}) collective-permute-start(bf16[128,1024]{1,0:T(8,128)(2,1)} %collective-permute-done.3), channel_id=1, source_target_pairs={{0,8},{1,12},{2,0},{3,4},{4,10},{5,14},{6,2},{7,6},{8,9},{9,13},{1... | collective-permute-start | bytes 786440 | tf_op jit(solution)/shard_map/ppermute | solution.py:344
  22.7 0.0 collective-permute-done.2
  22.7 0.0 copy-done
  22.7 0.5 broadcast_select_fusion.1
  23.3 0.4 fusion.1
  23.7 0.1 fusion.2
  23.7 0.4 fusion
  24.2 0.0 copy-start.1
  24.2 0.3 pad_maximum_fusion.1.basis
  24.5 0.5 collective-permute-done.1.x1
  24.9 1.0 collective-permute-start.5
  25.9 0.1 collective-permute-start.6
  26.0 3.1 %collective-permute-done.4.x0 = bf16[128,1024]{1,0:T(8,128)(2,1)} collective-permute-done((bf16[128,1024]{1,0:T(8,128)(2,1)}, bf16[128,1024]{1,0:T(8,128)(2,1)}, u32[]{:S(2)}, u32[]{:S(2)}) %collective-permute-start.4) | collective-permute-done | bytes 262176 | tf_op jit(solution)/shard_map/ppermute | solution.py:344
  29.1 0.0 collective-permute-done.5.x2
  29.1 0.0 collective-permute-done.6.x3
  29.1 2.0 %rotate.2 = (bf16[528,512]{1,0:T(8,128)(2,1)}, f32[512,512]{1,0:T(8,128)S(1)}) custom-call(bf16[128,1024]{1,0:T(8,128)(2,1)S(1)} %collective-permute-done.x0, bf16[128,1024]{1,0:T(8,128)(2,1)S(1)} %collective-permute-done.1.x1, bf16[128,1024]{1,0:T(8,128)(2,1)S(1)} %collective-permute-done.5.x2, bf16[128,1024]{1,0:T(8,128)(2,1)S(1)} %collective-permute-done.6.x3, ...), custom_call_target="tpu_custom_call" | custom-call | flops 1073741824 | bytes 2097152 | tf_op jit(solution)/shard_map/rotate/pallas_call | solution.py:165
  31.1 3.5 %collective-permute-start.7 = (bf16[128,1024]{1,0:T(8,128)(2,1)}, bf16[128,1024]{1,0:T(8,128)(2,1)S(1)}, u32[]{:S(2)}, u32[]{:S(2)}) collective-permute-start(bf16[128,1024]{1,0:T(8,128)(2,1)} %collective-permute-done.4.x0), channel_id=1, source_target_pairs={{0,2},{2,0},{1,3},{3,1},{4,6},{6,4},{5,7},{7,5},{8,10},{10,8},{9,1... | collective-permute-start | bytes 786440 | tf_op jit(solution)/shard_map/ppermute | solution.py:117
  34.6 2.1 %collective-permute-start.10 = (bf16[528,512]{1,0:T(8,128)(2,1)}, bf16[528,512]{1,0:T(8,128)(2,1)}, u32[]{:S(2)}, u32[]{:S(2)}) collective-permute-start(bf16[528,512]{1,0:T(8,128)(2,1)} %get-tuple-element.72), channel_id=1, source_target_pairs={{0,4},{4,0},{8,12},{12,8},{1,5},{5,1},{9,13},{13,9},{2,6},{6,2},{1... | collective-permute-start | bytes 1622024 | tf_op jit(solution)/shard_map/ppermute | solution.py:117
  36.7 3.0 %collective-permute-done.7.x1 = bf16[128,1024]{1,0:T(8,128)(2,1)S(1)} collective-permute-done((bf16[128,1024]{1,0:T(8,128)(2,1)}, bf16[128,1024]{1,0:T(8,128)(2,1)S(1)}, u32[]{:S(2)}, u32[]{:S(2)}) %collective-permute-start.7) | collective-permute-done | bytes 262176 | tf_op jit(solution)/shard_map/ppermute | solution.py:117
  39.7 3.2 %collective-permute-start.8 = (bf16[128,1024]{1,0:T(8,128)(2,1)}, bf16[128,1024]{1,0:T(8,128)(2,1)}, u32[]{:S(2)}, u32[]{:S(2)}) collective-permute-start(bf16[128,1024]{1,0:T(8,128)(2,1)} %collective-permute-done.4.x0), channel_id=1, source_target_pairs={{0,1},{1,0},{2,3},{3,2},{4,5},{5,4},{6,7},{7,6},{8,9},{9,8},{10,11... | collective-permute-start | bytes 786440 | tf_op jit(solution)/shard_map/ppermute | solution.py:117
  43.0 0.0 collective-permute-start.9
  43.0 1.8 %collective-permute-done.8.x2 = bf16[128,1024]{1,0:T(8,128)(2,1)} collective-permute-done((bf16[128,1024]{1,0:T(8,128)(2,1)}, bf16[128,1024]{1,0:T(8,128)(2,1)}, u32[]{:S(2)}, u32[]{:S(2)}) %collective-permute-start.8) | collective-permute-done | bytes 262176 | tf_op jit(solution)/shard_map/ppermute | solution.py:117
  44.8 0.0 collective-permute-done.9.x3
  44.8 2.4 %rotate.3 = (bf16[512,256]{1,0:T(8,128)(2,1)S(1)}, bf16[512,256]{1,0:T(8,128)(2,1)S(1)}, bf16[512,256]{1,0:T(8,128)(2,1)S(1)}, f32[512,256]{1,0:T(8,128)S(1)}) custom-call(bf16[128,1024]{1,0:T(8,128)(2,1)} %collective-permute-done.4.x0, bf16[128,1024]{1,0:T(8,128)(2,1)S(1)} %collective-permute-done.7.x1, bf16[128,1024]{1,0:T(8,128)(2,1)} %collective-permute-done.8.x2, ...), custom_call_target="tpu_custom_call" | custom-call | flops 1073741824 | bytes 2097152 | tf_op jit(solution)/shard_map/rotate/pallas_call | solution.py:165
  47.2 1.3 %collective-permute-start.11 = (bf16[512,256]{1,0:T(8,128)(2,1)S(1)}, bf16[512,256]{1,0:T(8,128)(2,1)S(1)}, u32[]{:S(2)}, u32[]{:S(2)}) collective-permute-start(bf16[512,256]{1,0:T(8,128)(2,1)S(1)} %get-tuple-element.77), channel_id=1, source_target_pairs={{0,2},{2,0},{1,3},{3,1},{4,6},{6,4},{5,7},{7,5},{8,10},{10,8},{9,1... | collective-permute-start | bytes 786440 | tf_op jit(solution)/shard_map/ppermute | solution.py:117
  48.5 2.1 %collective-permute-start.12 = (bf16[512,256]{1,0:T(8,128)(2,1)S(1)}, bf16[512,256]{1,0:T(8,128)(2,1)S(1)}, u32[]{:S(2)}, u32[]{:S(2)}) collective-permute-start(bf16[512,256]{1,0:T(8,128)(2,1)S(1)} %get-tuple-element.78), channel_id=1, source_target_pairs={{0,4},{4,0},{8,12},{12,8},{1,5},{5,1},{9,13},{13,9},{2,6},{6,2},{1... | collective-permute-start | bytes 786440 | tf_op jit(solution)/shard_map/ppermute | solution.py:117
  50.6 1.4 %collective-permute-start.13 = (bf16[512,256]{1,0:T(8,128)(2,1)S(1)}, bf16[512,256]{1,0:T(8,128)(2,1)S(1)}, u32[]{:S(2)}, u32[]{:S(2)}) collective-permute-start(bf16[512,256]{1,0:T(8,128)(2,1)S(1)} %get-tuple-element.79), channel_id=1, source_target_pairs={{0,6},{2,4},{4,2},{6,0},{8,14},{10,12},{12,10},{14,8},{1,7},{3,5},... | collective-permute-start | bytes 786440 | tf_op jit(solution)/shard_map/ppermute | solution.py:382
  52.0 0.0 collective-permute-done.10.got
  52.0 1.1 shard_map.85.pair
  53.1 1.6 %collective-permute-start.14 = (bf16[528,512]{1,0:T(8,128)(2,1)S(1)}, bf16[528,512]{1,0:T(8,128)(2,1)S(1)}, u32[]{:S(2)}, u32[]{:S(2)}) collective-permute-start(bf16[528,512]{1,0:T(8,128)(2,1)S(1)} %shard_map.85.pair), channel_id=1, source_target_pairs={{0,8},{4,12},{8,0},{12,4},{1,9},{5,13},{9,1},{13,5},{2,10},{6,14},... | collective-permute-start | bytes 1622024 | tf_op jit(solution)/shard_map/ppermute | solution.py:117
  54.7 1.1 collective-permute-done.11
  55.8 10.4 %collective-permute-done.12 = bf16[512,256]{1,0:T(8,128)(2,1)S(1)} collective-permute-done((bf16[512,256]{1,0:T(8,128)(2,1)S(1)}, bf16[512,256]{1,0:T(8,128)(2,1)S(1)}, u32[]{:S(2)}, u32[]{:S(2)}) %collective-permute-start.12) | collective-permute-done | bytes 262176 | tf_op jit(solution)/shard_map/ppermute | solution.py:117
  66.3 6.1 %collective-permute-done.13 = bf16[512,256]{1,0:T(8,128)(2,1)S(1)} collective-permute-done((bf16[512,256]{1,0:T(8,128)(2,1)S(1)}, bf16[512,256]{1,0:T(8,128)(2,1)S(1)}, u32[]{:S(2)}, u32[]{:S(2)}) %collective-permute-start.13) | collective-permute-done | bytes 262176 | tf_op jit(solution)/shard_map/ppermute | solution.py:382
  72.4 0.1 select_convert_fusion
  72.5 0.1 collective-permute-start.15
  72.7 13.9 %collective-permute-done.14.across = bf16[528,512]{1,0:T(8,128)(2,1)S(1)} collective-permute-done((bf16[528,512]{1,0:T(8,128)(2,1)S(1)}, bf16[528,512]{1,0:T(8,128)(2,1)S(1)}, u32[]{:S(2)}, u32[]{:S(2)}) %collective-permute-start.14) | collective-permute-done | bytes 540704 | tf_op jit(solution)/shard_map/ppermute | solution.py:117
  86.5 0.1 shard_map.86.g
  86.6 4.2 %collective-permute-done.15 = bf16[512,256]{1,0:T(8,128)(2,1)S(1)} collective-permute-done((bf16[512,256]{1,0:T(8,128)(2,1)S(1)}, bf16[512,256]{1,0:T(8,128)(2,1)S(1)}, u32[]{:S(2)}, u32[]{:S(2)}) %collective-permute-start.15) | collective-permute-done | bytes 262176 | tf_op jit(solution)/shard_map/ppermute | solution.py:117
  90.8 0.2 add_convert_fusion.a0
  91.0 0.6 collective-permute-start.16
  91.6 0.7 collective-permute-start.19
  92.3 0.1 pad_add_fusion.place
  92.4 0.7 slice.19
  93.0 0.0 collective-permute-start.17
  93.1 5.0 %collective-permute-done.16.a1 = bf16[512,256]{1,0:T(8,128)(2,1)S(1)} collective-permute-done((bf16[512,256]{1,0:T(8,128)(2,1)S(1)}, bf16[512,256]{1,0:T(8,128)(2,1)S(1)}, u32[]{:S(2)}, u32[]{:S(2)}) %collective-permute-start.16) | collective-permute-done | bytes 262176 | tf_op jit(solution)/shard_map/ppermute | solution.py:117
  98.1 0.0 collective-permute-start.18
  98.1 0.0 collective-permute-done.17.a2
  98.1 1.5 %collective-permute-done.18.a3 = bf16[512,256]{1,0:T(8,128)(2,1)S(1)} collective-permute-done((bf16[512,256]{1,0:T(8,128)(2,1)S(1)}, bf16[512,256]{1,0:T(8,128)(2,1)S(1)}, u32[]{:S(2)}, u32[]{:S(2)}) %collective-permute-start.18) | collective-permute-done | bytes 262176 | tf_op jit(solution)/shard_map/ppermute | solution.py:117
  99.6 4.0 %outer_near.1 = (f32[1024,1024]{1,0:T(8,128)}, f32[512,128]{1,0:T(8,128)S(1)}, bf16[512,1024]{1,0:T(8,128)(2,1)S(1)}, bf16[1024,512]{1,0:T(8,128)(2,1)S(1)}, f32[1024,512]{1,0:T(8,128)S(1)}) custom-call(s32[3]{0:T(128)S(1)} %pad_add_fusion.place, bf16[512,256]{1,0:T(8,128)(2,1)S(1)} %add_convert_fusion.a0, bf16[512,256]{1,0:T(8,128)(2,1)S(1)} %collective-permute-done.16.a1, ...), custom_call_target="tpu_custom_call" | custom-call | flops 1073741824 | bytes 6291456 | tf_op jit(solution)/shard_map/outer_near/pallas_call | solution.py:273
  103.6 0.4 collective-permute-done.19.g
  104.0 2.3 %outer_far.1 = (f32[1024,1024]{1,0:T(8,128)}, f32[4,128]{1,0:T(4,128)S(1)}) custom-call(s32[3]{0:T(128)S(1)} %pad_add_fusion.place, bf16[512,1024]{1,0:T(8,128)(2,1)S(1)} %get-tuple-element.90.flat, bf16[1024,512]{1,0:T(8,128)(2,1)S(1)} %get-tuple-element.91.turned, bf16[512,512]{1,0:T(8,128)(2,1)S(1)} %collective-permute-done.19.g, ...), custom_call_target="tpu_custom_call", output_to_operand_aliasing={{0}: (5, {})} | custom-call | flops 1073741824 | bytes 2097152 | tf_op jit(solution)/shard_map/outer_far/pallas_call | solution.py:304
  106.3 0.1 select_reduce_fusion
  106.5 10.9 %all_to_all.11 = f32[16,1,136]{2,1,0:T(1,128)S(1)} all-to-all(f32[16,1,136]{2,1,0:T(1,128)S(1)} %all_to_all.7), channel_id=1, replica_groups=mesh['grp'=2,'seq'=4,'row'=2,'col'=2] {'seq','row','col'}, dimensions={0} | all-to-all | bytes 17408 | tf_op jit(solution)/shard_map/all_to_all | solution.py:420
  117.4 0.5 finish.1
  (19 shorter events, 0.1 us)
Async XLA Ops:
  0.6 12.8 %collective-permute-start = (bf16[128,1024]{1,0:T(8,128)(2,1)}, bf16[128,1024]{1,0:T(8,128)(2,1)S(1)}, u32[]{:S(2)}, u32[]{:S(2)}) collective-permute-start(bf16[128,1024]{1,0:T(8,128)(2,1)} %param.9), channel_id=1, source_target_pairs={{0,0},{1,4},{2,8},{3,12},{4,2},{5,6},{6,10},{7,14},{8,1},{9,5},{10... | collective-permute-start | bytes 786440 | tf_op jit(solution)/shard_map/ppermute | solution.py:344
  4.5 18.2 %collective-permute-start.2 = (bf16[1024,512]{1,0:T(8,128)(2,1)}, bf16[1024,512]{1,0:T(8,128)(2,1)S(1)}, u32[]{:S(2)}, u32[]{:S(2)}) collective-permute-start(bf16[1024,512]{1,0:T(8,128)(2,1)} %constant_dynamic-slice_fusion.8), channel_id=1, source_target_pairs={{0,1},{1,0},{2,3},{3,2},{4,5},{5,4},{6,7},{7,6},{8,9},{9,8},{10,11... | collective-permute-start | bytes 3145736 | tf_op jit(solution)/shard_map/ppermute | solution.py:117
  8.0 11.6 %collective-permute-start.3 = (bf16[128,1024]{1,0:T(8,128)(2,1)}, bf16[128,1024]{1,0:T(8,128)(2,1)}, u32[]{:S(2)}, u32[]{:S(2)}) collective-permute-start(bf16[128,1024]{1,0:T(8,128)(2,1)} %param.8), channel_id=1, source_target_pairs={{0,2},{2,0},{1,3},{3,1},{4,6},{6,4},{5,7},{7,5},{8,10},{10,8},{9,1... | collective-permute-start | bytes 786440 | tf_op jit(solution)/shard_map/ppermute | solution.py:117
  13.4 9.3 %copy-start = (bf16[1024,1024]{1,0:T(8,128)(2,1)S(1)}, bf16[1024,1024]{1,0:T(8,128)(2,1)}, u32[]{:S(2)}) copy-start(bf16[1024,1024]{1,0:T(8,128)(2,1)} %param.11) | copy-start | bytes 6291460
  13.5 11.5 %collective-permute-start.1 = (bf16[128,1024]{1,0:T(8,128)(2,1)S(1)}, bf16[128,1024]{1,0:T(8,128)(2,1)S(1)}, u32[]{:S(2)}, u32[]{:S(2)}) collective-permute-start(bf16[128,1024]{1,0:T(8,128)(2,1)S(1)} %collective-permute-done.x0), channel_id=1, source_target_pairs={{0,2},{2,0},{1,3},{3,1},{4,6},{6,4},{5,7},{7,5},{8,10},{10,8},{9,1... | collective-permute-start | bytes 786440 | tf_op jit(solution)/shard_map/ppermute | solution.py:117
  19.5 9.6 %collective-permute-start.4 = (bf16[128,1024]{1,0:T(8,128)(2,1)}, bf16[128,1024]{1,0:T(8,128)(2,1)}, u32[]{:S(2)}, u32[]{:S(2)}) collective-permute-start(bf16[128,1024]{1,0:T(8,128)(2,1)} %collective-permute-done.3), channel_id=1, source_target_pairs={{0,8},{1,12},{2,0},{3,4},{4,10},{5,14},{6,2},{7,6},{8,9},{9,13},{1... | collective-permute-start | bytes 786440 | tf_op jit(solution)/shard_map/ppermute | solution.py:344
  24.2 1.8 %copy-start.1 = (s32[128]{0:T(128)S(1)}, s32[128]{0:T(128)}, u32[]{:S(2)}) copy-start(s32[128]{0:T(128)} %param.10) | copy-start | bytes 1540
  24.9 4.2 %collective-permute-start.5 = (bf16[128,1024]{1,0:T(8,128)(2,1)S(1)}, bf16[128,1024]{1,0:T(8,128)(2,1)S(1)}, u32[]{:S(2)}, u32[]{:S(2)}) collective-permute-start(bf16[128,1024]{1,0:T(8,128)(2,1)S(1)} %collective-permute-done.x0), channel_id=1, source_target_pairs={{0,1},{1,0},{2,3},{3,2},{4,5},{5,4},{6,7},{7,6},{8,9},{9,8},{10,11... | collective-permute-start | bytes 786440 | tf_op jit(solution)/shard_map/ppermute | solution.py:117
  25.9 3.2 %collective-permute-start.6 = (bf16[128,1024]{1,0:T(8,128)(2,1)S(1)}, bf16[128,1024]{1,0:T(8,128)(2,1)S(1)}, u32[]{:S(2)}, u32[]{:S(2)}) collective-permute-start(bf16[128,1024]{1,0:T(8,128)(2,1)S(1)} %collective-permute-done.1.x1), channel_id=1, source_target_pairs={{0,1},{1,0},{2,3},{3,2},{4,5},{5,4},{6,7},{7,6},{8,9},{9,8},{10,11... | collective-permute-start | bytes 786440 | tf_op jit(solution)/shard_map/ppermute | solution.py:117
  31.1 8.6 %collective-permute-start.7 = (bf16[128,1024]{1,0:T(8,128)(2,1)}, bf16[128,1024]{1,0:T(8,128)(2,1)S(1)}, u32[]{:S(2)}, u32[]{:S(2)}) collective-permute-start(bf16[128,1024]{1,0:T(8,128)(2,1)} %collective-permute-done.4.x0), channel_id=1, source_target_pairs={{0,2},{2,0},{1,3},{3,1},{4,6},{6,4},{5,7},{7,5},{8,10},{10,8},{9,1... | collective-permute-start | bytes 786440 | tf_op jit(solution)/shard_map/ppermute | solution.py:117
  34.6 17.4 %collective-permute-start.10 = (bf16[528,512]{1,0:T(8,128)(2,1)}, bf16[528,512]{1,0:T(8,128)(2,1)}, u32[]{:S(2)}, u32[]{:S(2)}) collective-permute-start(bf16[528,512]{1,0:T(8,128)(2,1)} %get-tuple-element.72), channel_id=1, source_target_pairs={{0,4},{4,0},{8,12},{12,8},{1,5},{5,1},{9,13},{13,9},{2,6},{6,2},{1... | collective-permute-start | bytes 1622024 | tf_op jit(solution)/shard_map/ppermute | solution.py:117
  39.7 5.1 %collective-permute-start.8 = (bf16[128,1024]{1,0:T(8,128)(2,1)}, bf16[128,1024]{1,0:T(8,128)(2,1)}, u32[]{:S(2)}, u32[]{:S(2)}) collective-permute-start(bf16[128,1024]{1,0:T(8,128)(2,1)} %collective-permute-done.4.x0), channel_id=1, source_target_pairs={{0,1},{1,0},{2,3},{3,2},{4,5},{5,4},{6,7},{7,6},{8,9},{9,8},{10,11... | collective-permute-start | bytes 786440 | tf_op jit(solution)/shard_map/ppermute | solution.py:117
  43.0 1.8 %collective-permute-start.9 = (bf16[128,1024]{1,0:T(8,128)(2,1)S(1)}, bf16[128,1024]{1,0:T(8,128)(2,1)}, u32[]{:S(2)}, u32[]{:S(2)}) collective-permute-start(bf16[128,1024]{1,0:T(8,128)(2,1)S(1)} %collective-permute-done.7.x1), channel_id=1, source_target_pairs={{0,1},{1,0},{2,3},{3,2},{4,5},{5,4},{6,7},{7,6},{8,9},{9,8},{10,11... | collective-permute-start | bytes 786440 | tf_op jit(solution)/shard_map/ppermute | solution.py:117
  47.2 8.7 %collective-permute-start.11 = (bf16[512,256]{1,0:T(8,128)(2,1)S(1)}, bf16[512,256]{1,0:T(8,128)(2,1)S(1)}, u32[]{:S(2)}, u32[]{:S(2)}) collective-permute-start(bf16[512,256]{1,0:T(8,128)(2,1)S(1)} %get-tuple-element.77), channel_id=1, source_target_pairs={{0,2},{2,0},{1,3},{3,1},{4,6},{6,4},{5,7},{7,5},{8,10},{10,8},{9,1... | collective-permute-start | bytes 786440 | tf_op jit(solution)/shard_map/ppermute | solution.py:117
  48.5 17.8 %collective-permute-start.12 = (bf16[512,256]{1,0:T(8,128)(2,1)S(1)}, bf16[512,256]{1,0:T(8,128)(2,1)S(1)}, u32[]{:S(2)}, u32[]{:S(2)}) collective-permute-start(bf16[512,256]{1,0:T(8,128)(2,1)S(1)} %get-tuple-element.78), channel_id=1, source_target_pairs={{0,4},{4,0},{8,12},{12,8},{1,5},{5,1},{9,13},{13,9},{2,6},{6,2},{1... | collective-permute-start | bytes 786440 | tf_op jit(solution)/shard_map/ppermute | solution.py:117
  50.6 21.8 %collective-permute-start.13 = (bf16[512,256]{1,0:T(8,128)(2,1)S(1)}, bf16[512,256]{1,0:T(8,128)(2,1)S(1)}, u32[]{:S(2)}, u32[]{:S(2)}) collective-permute-start(bf16[512,256]{1,0:T(8,128)(2,1)S(1)} %get-tuple-element.79), channel_id=1, source_target_pairs={{0,6},{2,4},{4,2},{6,0},{8,14},{10,12},{12,10},{14,8},{1,7},{3,5},... | collective-permute-start | bytes 786440 | tf_op jit(solution)/shard_map/ppermute | solution.py:382
  53.1 33.4 %collective-permute-start.14 = (bf16[528,512]{1,0:T(8,128)(2,1)S(1)}, bf16[528,512]{1,0:T(8,128)(2,1)S(1)}, u32[]{:S(2)}, u32[]{:S(2)}) collective-permute-start(bf16[528,512]{1,0:T(8,128)(2,1)S(1)} %shard_map.85.pair), channel_id=1, source_target_pairs={{0,8},{4,12},{8,0},{12,4},{1,9},{5,13},{9,1},{13,5},{2,10},{6,14},... | collective-permute-start | bytes 1622024 | tf_op jit(solution)/shard_map/ppermute | solution.py:117
  72.5 18.3 %collective-permute-start.15 = (bf16[512,256]{1,0:T(8,128)(2,1)S(1)}, bf16[512,256]{1,0:T(8,128)(2,1)S(1)}, u32[]{:S(2)}, u32[]{:S(2)}) collective-permute-start(bf16[512,256]{1,0:T(8,128)(2,1)S(1)} %select_convert_fusion), channel_id=1, source_target_pairs={{0,8},{4,12},{8,0},{12,4},{1,9},{5,13},{9,1},{13,5},{2,10},{6,14},... | collective-permute-start | bytes 786440 | tf_op jit(solution)/shard_map/ppermute | solution.py:117
  91.0 7.1 %collective-permute-start.16 = (bf16[512,256]{1,0:T(8,128)(2,1)S(1)}, bf16[512,256]{1,0:T(8,128)(2,1)S(1)}, u32[]{:S(2)}, u32[]{:S(2)}) collective-permute-start(bf16[512,256]{1,0:T(8,128)(2,1)S(1)} %add_convert_fusion.a0), channel_id=1, source_target_pairs={{0,2},{2,0},{1,3},{3,1},{4,6},{6,4},{5,7},{7,5},{8,10},{10,8},{9,1... | collective-permute-start | bytes 786440 | tf_op jit(solution)/shard_map/ppermute | solution.py:117
  91.6 12.3 %collective-permute-start.19 = (bf16[512,512]{1,0:T(8,128)(2,1)S(1)}, bf16[512,512]{1,0:T(8,128)(2,1)S(1)}, u32[]{:S(2)}, u32[]{:S(2)}) collective-permute-start(bf16[512,512]{1,0:T(8,128)(2,1)S(1)} %shard_map.86.g), channel_id=1, source_target_pairs={{0,4},{4,0},{8,12},{12,8},{1,5},{5,1},{9,13},{13,9},{2,6},{6,2},{1... | collective-permute-start | bytes 1572872 | tf_op jit(solution)/shard_map/ppermute | solution.py:117
  93.0 5.1 %collective-permute-start.17 = (bf16[512,256]{1,0:T(8,128)(2,1)S(1)}, bf16[512,256]{1,0:T(8,128)(2,1)S(1)}, u32[]{:S(2)}, u32[]{:S(2)}) collective-permute-start(bf16[512,256]{1,0:T(8,128)(2,1)S(1)} %add_convert_fusion.a0), channel_id=1, source_target_pairs={{0,1},{1,0},{2,3},{3,2},{4,5},{5,4},{6,7},{7,6},{8,9},{9,8},{10,11... | collective-permute-start | bytes 786440 | tf_op jit(solution)/shard_map/ppermute | solution.py:117
  98.1 1.5 %collective-permute-start.18 = (bf16[512,256]{1,0:T(8,128)(2,1)S(1)}, bf16[512,256]{1,0:T(8,128)(2,1)S(1)}, u32[]{:S(2)}, u32[]{:S(2)}) collective-permute-start(bf16[512,256]{1,0:T(8,128)(2,1)S(1)} %collective-permute-done.16.a1), channel_id=1, source_target_pairs={{0,1},{1,0},{2,3},{3,2},{4,5},{5,4},{6,7},{7,6},{8,9},{9,8},{10,11... | collective-permute-start | bytes 786440 | tf_op jit(solution)/shard_map/ppermute | solution.py:117

commit v7 on v6

--- a/solution.py
+++ b/solution.py
@@ -179,7 +179,7 @@
     count = keep.shape[0]
     out[:count, :] = (keep[...] + got[:count, :].astype(jnp.float32)).astype(jnp.bfloat16)
     row = lax.broadcasted_iota(jnp.int32, note.shape, 0)
-    theirs = jnp.broadcast_to(got[count : count + 1, :].astype(jnp.float32), note.shape)
+    theirs = jnp.broadcast_to(got[count:, :].astype(jnp.float32)[:1], note.shape)
     out[count:, :] = jnp.where(row == 1, theirs, note[...].astype(jnp.float32)).astype(jnp.bfloat16)
 
 
@@ -351,7 +351,7 @@
     token = jnp.zeros((8, LANES), jnp.float32)
     acts_there = swap(acts, "row")
     grads_here = turned(grads, 0)
-    theirs = swap(lax.dynamic_slice_in_dim(basis_in, (1 - k) * half, half, axis=1), "col")
+    theirs = swap(jnp.where(k == 0, basis_in[:, half:], basis_in[:, :half]), "col")
     basis_out = jnp.concatenate(
         [lax.dynamic_slice_in_dim(basis_out, at * half, half, axis=1) for at in (1 - low, low)], axis=1
     )

time: 118 us -> 118 us (level)
  other arithmetic: 2.5 us -> 5.32 us
  local copies, waits for them, and re-layouts: 4.77 us -> 2.51 us
  waiting for transfers between devices: 55.1 us -> 53.3 us
  starting transfers between devices: 31.4 us -> 32.8 us
    dynamic_slice x1 -> x0, local copies, waits for them, and re-layouts: 2.26 us -> none  [local_pairs(): lax.dynamic_slice_in_dim(basis_in, (1 - k) * half, half, axis=1)]
    select_n x0 -> x1, other arithmetic: none -> 1.65 us  [local_pairs(): jnp.where(k == 0, basis_in[:, half:], basis_in[:, :half])]
    ppermute x17, starting transfers between devices: 25.3 us -> 26.6 us  [swap(): lax.ppermute(x, axis, [(i, i ^ step) for i in range(lax.axis_size(axis))])]
    ppermute x2, waiting for transfers between devices: 3.13 us -> 1.95 us  [turned(): return lax.ppermute(x, PLANE, pairs)]
  transfers between devices with their start and end apart: 20 -> 20, of which waited for: 13 -> 12; matrix products, arithmetic and copies ran while one was open for 6% -> 6% of each run, Pallas kernels for 6% -> 6%
where the time goes in v7:
time: 118 us
  waiting for transfers between devices  53.3 us (45%)
  starting transfers between devices  32.8 us (28%)
  Pallas kernels  12.4 us (11%)
  blocking collectives  10.8 us (9%)
  other arithmetic  5.32 us (5%)
  local copies, waits for them, and re-layouts  2.51 us (2%)
    ppermute x17, waiting for transfers between devices, swap(): lax.ppermute(x, axis, [(i, i ^ step) for i in range(lax.axis_size(axis))])  45.2 us
    ppermute x17, starting transfers between devices, swap(): lax.ppermute(x, axis, [(i, i ^ step) for i in range(lax.axis_size(axis))])  26.6 us
    all_to_all x1, blocking collectives, local_pairs(): lax.all_to_all(message, PLANE, split_axis=0, concat_axis=0, tiled=True)  10.8 us
    ppermute x1, waiting for transfers between devices, local_pairs(): lax.ppermute(to_both, ('seq', 'row'), [(i * rows + j, (i ^ 1) * rows + (j...  6.21 us
    ppermute x2, starting transfers between devices, turned(): return lax.ppermute(x, PLANE, pairs)  4.8 us
    pallas_call x2, Pallas kernels, rotate(): pl.pallas_call(functools.partial(rotate_kernel, notes=len(note), flips=fl...  4.32 us
    pallas_call x1, Pallas kernels, outer_near(): pl.pallas_call(near_kernel, out_shape=(jax.ShapeDtypeStruct(eigvals.shape...  3.96 us
  transfers between devices with their start and end apart: 20, of which 12 were waited for; matrix products, arithmetic and copies ran while one was open for 6% of the time, Pallas kernels for 6%

profile of v7, /device:TPU:0, one launch (start us, length us, event | category | flops | bytes accessed | tf_op | source)
XLA Modules:
  0.0 117.9 jit_solution(7715377547604090379)
XLA Ops:
  0.6 1.6 %collective-permute-start = (bf16[128,1024]{1,0:T(8,128)(2,1)}, bf16[128,1024]{1,0:T(8,128)(2,1)S(1)}, u32[]{:S(2)}, u32[]{:S(2)}) collective-permute-start(bf16[128,1024]{1,0:T(8,128)(2,1)} %param.9), channel_id=1, source_target_pairs={{0,0},{1,4},{2,8},{3,12},{4,2},{5,6},{6,10},{7,14},{8,1},{9,5},{10... | collective-permute-start | bytes 786440 | tf_op jit(solution)/shard_map/ppermute | solution.py:344
  2.2 1.7 %slice_select_fusion = bf16[1024,512]{1,0:T(8,128)(2,1)S(1)} fusion(bf16[1024,1024]{1,0:T(8,128)(2,1)} %param.11, pred[]{:T(512)S(6)} %eq.30), kind=kLoop, calls=%fused_computation.8 | loop fusion | flops 524288 | bytes 3145729 | tf_op jit(solution)/shard_map/jit(_where)/select_n | solution.py:354
  3.9 3.5 %collective-permute-start.2 = (bf16[1024,512]{1,0:T(8,128)(2,1)S(1)}, bf16[1024,512]{1,0:T(8,128)(2,1)}, u32[]{:S(2)}, u32[]{:S(2)}) collective-permute-start(bf16[1024,512]{1,0:T(8,128)(2,1)S(1)} %slice_select_fusion), channel_id=1, source_target_pairs={{0,1},{1,0},{2,3},{3,2},{4,5},{5,4},{6,7},{7,6},{8,9},{9,8},{10,11... | collective-permute-start | bytes 3145736 | tf_op jit(solution)/shard_map/ppermute | solution.py:117
  7.4 3.5 %collective-permute-start.3 = (bf16[128,1024]{1,0:T(8,128)(2,1)}, bf16[128,1024]{1,0:T(8,128)(2,1)}, u32[]{:S(2)}, u32[]{:S(2)}) collective-permute-start(bf16[128,1024]{1,0:T(8,128)(2,1)} %param.8), channel_id=1, source_target_pairs={{0,2},{2,0},{1,3},{3,1},{4,6},{6,4},{5,7},{7,5},{8,10},{10,8},{9,1... | collective-permute-start | bytes 786440 | tf_op jit(solution)/shard_map/ppermute | solution.py:117
  10.9 1.7 %constant_dynamic-slice_fusion.9 = (bf16[1024,512]{1,0:T(8,128)(2,1)S(1)}, bf16[1024,512]{1,0:T(8,128)(2,1)S(1)}) fusion(bf16[1024,1024]{1,0:T(8,128)(2,1)} %param.12, s32[]{:T(128)S(6)} %select_n.92, s32[]{:T(128)S(6)} %select_n.93), kind=kLoop, calls=%fused_computation.27 | loop fusion | bytes 4194312 | tf_op jit(solution)/shard_map/dynamic_slice | solution.py:356
  12.6 0.3 pad_maximum_fusion.basis
  12.9 0.0 copy-start
  12.9 0.0 collective-permute-done.x0
  12.9 2.5 %collective-permute-start.1 = (bf16[128,1024]{1,0:T(8,128)(2,1)S(1)}, bf16[128,1024]{1,0:T(8,128)(2,1)S(1)}, u32[]{:S(2)}, u32[]{:S(2)}) collective-permute-start(bf16[128,1024]{1,0:T(8,128)(2,1)S(1)} %collective-permute-done.x0), channel_id=1, source_target_pairs={{0,2},{2,0},{1,3},{3,1},{4,6},{6,4},{5,7},{7,5},{8,10},{10,8},{9,1... | collective-permute-start | bytes 786440 | tf_op jit(solution)/shard_map/ppermute | solution.py:117
  15.5 4.0 %collective-permute-done.3 = bf16[128,1024]{1,0:T(8,128)(2,1)} collective-permute-done((bf16[128,1024]{1,0:T(8,128)(2,1)}, bf16[128,1024]{1,0:T(8,128)(2,1)}, u32[]{:S(2)}, u32[]{:S(2)}) %collective-permute-start.3) | collective-permute-done | bytes 262176 | tf_op jit(solution)/shard_map/ppermute | solution.py:117
  19.5 3.2 %collective-permute-start.4 = (bf16[128,1024]{1,0:T(8,128)(2,1)}, bf16[128,1024]{1,0:T(8,128)(2,1)}, u32[]{:S(2)}, u32[]{:S(2)}) collective-permute-start(bf16[128,1024]{1,0:T(8,128)(2,1)} %collective-permute-done.3), channel_id=1, source_target_pairs={{0,8},{1,12},{2,0},{3,4},{4,10},{5,14},{6,2},{7,6},{8,9},{9,13},{1... | collective-permute-start | bytes 786440 | tf_op jit(solution)/shard_map/ppermute | solution.py:344
  22.7 0.0 collective-permute-done.2
  22.7 0.0 copy-done
  22.7 1.7 %broadcast_select_fusion.1 = (bf16[1024,512]{1,0:T(8,128)(2,1)S(1)}, bf16[1024,512]{1,0:T(8,128)(2,1)S(1)}) fusion(bf16[1024,512]{1,0:T(8,128)(2,1)} %collective-permute-done.2, pred[]{:T(512)S(6)} %eq.29, bf16[1024,1024]{1,0:T(8,128)(2,1)S(1)} %copy-done, s32[]{:T(128)S(6)} %select_n.97), kind=kLoop, calls=%fused_computation.10 | loop fusion | flops 1048576 | bytes 4194309 | tf_op jit(solution)/shard_map/jit(_where)/select_n | solution.py:365
  24.4 0.4 fusion.1
  24.8 0.1 fusion.2
  24.9 0.4 fusion
  25.3 0.0 copy-start.1
  25.3 0.3 pad_maximum_fusion.1.basis
  25.6 0.0 collective-permute-done.1.x1
  25.7 1.4 %collective-permute-start.5 = (bf16[128,1024]{1,0:T(8,128)(2,1)S(1)}, bf16[128,1024]{1,0:T(8,128)(2,1)S(1)}, u32[]{:S(2)}, u32[]{:S(2)}) collective-permute-start(bf16[128,1024]{1,0:T(8,128)(2,1)S(1)} %collective-permute-done.x0), channel_id=1, source_target_pairs={{0,1},{1,0},{2,3},{3,2},{4,5},{5,4},{6,7},{7,6},{8,9},{9,8},{10,11... | collective-permute-start | bytes 786440 | tf_op jit(solution)/shard_map/ppermute | solution.py:117
  27.1 0.1 collective-permute-start.6
  27.2 1.9 %collective-permute-done.4.x0 = bf16[128,1024]{1,0:T(8,128)(2,1)} collective-permute-done((bf16[128,1024]{1,0:T(8,128)(2,1)}, bf16[128,1024]{1,0:T(8,128)(2,1)}, u32[]{:S(2)}, u32[]{:S(2)}) %collective-permute-start.4) | collective-permute-done | bytes 262176 | tf_op jit(solution)/shard_map/ppermute | solution.py:344
  29.1 0.0 collective-permute-done.5.x2
  29.1 0.0 collective-permute-done.6.x3
  29.1 2.0 %rotate.2 = (bf16[528,512]{1,0:T(8,128)(2,1)}, f32[512,512]{1,0:T(8,128)S(1)}) custom-call(bf16[128,1024]{1,0:T(8,128)(2,1)S(1)} %collective-permute-done.x0, bf16[128,1024]{1,0:T(8,128)(2,1)S(1)} %collective-permute-done.1.x1, bf16[128,1024]{1,0:T(8,128)(2,1)S(1)} %collective-permute-done.5.x2, bf16[128,1024]{1,0:T(8,128)(2,1)S(1)} %collective-permute-done.6.x3, ...), custom_call_target="tpu_custom_call" | custom-call | flops 1073741824 | bytes 2097152 | tf_op jit(solution)/shard_map/rotate/pallas_call | solution.py:165
  31.1 3.4 %collective-permute-start.7 = (bf16[128,1024]{1,0:T(8,128)(2,1)}, bf16[128,1024]{1,0:T(8,128)(2,1)S(1)}, u32[]{:S(2)}, u32[]{:S(2)}) collective-permute-start(bf16[128,1024]{1,0:T(8,128)(2,1)} %collective-permute-done.4.x0), channel_id=1, source_target_pairs={{0,2},{2,0},{1,3},{3,1},{4,6},{6,4},{5,7},{7,5},{8,10},{10,8},{9,1... | collective-permute-start | bytes 786440 | tf_op jit(solution)/shard_map/ppermute | solution.py:117
  34.5 2.2 %collective-permute-start.10 = (bf16[528,512]{1,0:T(8,128)(2,1)}, bf16[528,512]{1,0:T(8,128)(2,1)}, u32[]{:S(2)}, u32[]{:S(2)}) collective-permute-start(bf16[528,512]{1,0:T(8,128)(2,1)} %get-tuple-element.72), channel_id=1, source_target_pairs={{0,4},{4,0},{8,12},{12,8},{1,5},{5,1},{9,13},{13,9},{2,6},{6,2},{1... | collective-permute-start | bytes 1622024 | tf_op jit(solution)/shard_map/ppermute | solution.py:117
  36.7 2.8 %collective-permute-done.7.x1 = bf16[128,1024]{1,0:T(8,128)(2,1)S(1)} collective-permute-done((bf16[128,1024]{1,0:T(8,128)(2,1)}, bf16[128,1024]{1,0:T(8,128)(2,1)S(1)}, u32[]{:S(2)}, u32[]{:S(2)}) %collective-permute-start.7) | collective-permute-done | bytes 262176 | tf_op jit(solution)/shard_map/ppermute | solution.py:117
  39.5 3.5 %collective-permute-start.8 = (bf16[128,1024]{1,0:T(8,128)(2,1)}, bf16[128,1024]{1,0:T(8,128)(2,1)}, u32[]{:S(2)}, u32[]{:S(2)}) collective-permute-start(bf16[128,1024]{1,0:T(8,128)(2,1)} %collective-permute-done.4.x0), channel_id=1, source_target_pairs={{0,1},{1,0},{2,3},{3,2},{4,5},{5,4},{6,7},{7,6},{8,9},{9,8},{10,11... | collective-permute-start | bytes 786440 | tf_op jit(solution)/shard_map/ppermute | solution.py:117
  43.0 0.0 collective-permute-start.9
  43.0 1.8 %collective-permute-done.8.x2 = bf16[128,1024]{1,0:T(8,128)(2,1)} collective-permute-done((bf16[128,1024]{1,0:T(8,128)(2,1)}, bf16[128,1024]{1,0:T(8,128)(2,1)}, u32[]{:S(2)}, u32[]{:S(2)}) %collective-permute-start.8) | collective-permute-done | bytes 262176 | tf_op jit(solution)/shard_map/ppermute | solution.py:117
  44.9 0.0 collective-permute-done.9.x3
  44.9 2.4 %rotate.3 = (bf16[512,256]{1,0:T(8,128)(2,1)S(1)}, bf16[512,256]{1,0:T(8,128)(2,1)S(1)}, bf16[512,256]{1,0:T(8,128)(2,1)S(1)}, f32[512,256]{1,0:T(8,128)S(1)}) custom-call(bf16[128,1024]{1,0:T(8,128)(2,1)} %collective-permute-done.4.x0, bf16[128,1024]{1,0:T(8,128)(2,1)S(1)} %collective-permute-done.7.x1, bf16[128,1024]{1,0:T(8,128)(2,1)} %collective-permute-done.8.x2, ...), custom_call_target="tpu_custom_call" | custom-call | flops 1073741824 | bytes 2097152 | tf_op jit(solution)/shard_map/rotate/pallas_call | solution.py:165
  47.2 1.2 %collective-permute-start.11 = (bf16[512,256]{1,0:T(8,128)(2,1)S(1)}, bf16[512,256]{1,0:T(8,128)(2,1)S(1)}, u32[]{:S(2)}, u32[]{:S(2)}) collective-permute-start(bf16[512,256]{1,0:T(8,128)(2,1)S(1)} %get-tuple-element.77), channel_id=1, source_target_pairs={{0,2},{2,0},{1,3},{3,1},{4,6},{6,4},{5,7},{7,5},{8,10},{10,8},{9,1... | collective-permute-start | bytes 786440 | tf_op jit(solution)/shard_map/ppermute | solution.py:117
  48.4 2.1 %collective-permute-start.12 = (bf16[512,256]{1,0:T(8,128)(2,1)S(1)}, bf16[512,256]{1,0:T(8,128)(2,1)S(1)}, u32[]{:S(2)}, u32[]{:S(2)}) collective-permute-start(bf16[512,256]{1,0:T(8,128)(2,1)S(1)} %get-tuple-element.78), channel_id=1, source_target_pairs={{0,4},{4,0},{8,12},{12,8},{1,5},{5,1},{9,13},{13,9},{2,6},{6,2},{1... | collective-permute-start | bytes 786440 | tf_op jit(solution)/shard_map/ppermute | solution.py:117
  50.6 1.4 %collective-permute-start.13 = (bf16[512,256]{1,0:T(8,128)(2,1)S(1)}, bf16[512,256]{1,0:T(8,128)(2,1)S(1)}, u32[]{:S(2)}, u32[]{:S(2)}) collective-permute-start(bf16[512,256]{1,0:T(8,128)(2,1)S(1)} %get-tuple-element.79), channel_id=1, source_target_pairs={{0,6},{2,4},{4,2},{6,0},{8,14},{10,12},{12,10},{14,8},{1,7},{3,5},... | collective-permute-start | bytes 786440 | tf_op jit(solution)/shard_map/ppermute | solution.py:382
  51.9 0.0 collective-permute-done.10.got
  51.9 1.1 shard_map.85.pair
  53.1 1.6 %collective-permute-start.14 = (bf16[528,512]{1,0:T(8,128)(2,1)S(1)}, bf16[528,512]{1,0:T(8,128)(2,1)S(1)}, u32[]{:S(2)}, u32[]{:S(2)}) collective-permute-start(bf16[528,512]{1,0:T(8,128)(2,1)S(1)} %shard_map.85.pair), channel_id=1, source_target_pairs={{0,8},{4,12},{8,0},{12,4},{1,9},{5,13},{9,1},{13,5},{2,10},{6,14},... | collective-permute-start | bytes 1622024 | tf_op jit(solution)/shard_map/ppermute | solution.py:117
  54.7 1.2 collective-permute-done.11
  55.9 10.3 %collective-permute-done.12 = bf16[512,256]{1,0:T(8,128)(2,1)S(1)} collective-permute-done((bf16[512,256]{1,0:T(8,128)(2,1)S(1)}, bf16[512,256]{1,0:T(8,128)(2,1)S(1)}, u32[]{:S(2)}, u32[]{:S(2)}) %collective-permute-start.12) | collective-permute-done | bytes 262176 | tf_op jit(solution)/shard_map/ppermute | solution.py:117
  66.2 6.2 %collective-permute-done.13 = bf16[512,256]{1,0:T(8,128)(2,1)S(1)} collective-permute-done((bf16[512,256]{1,0:T(8,128)(2,1)S(1)}, bf16[512,256]{1,0:T(8,128)(2,1)S(1)}, u32[]{:S(2)}, u32[]{:S(2)}) %collective-permute-start.13) | collective-permute-done | bytes 262176 | tf_op jit(solution)/shard_map/ppermute | solution.py:382
  72.4 0.1 select_convert_fusion
  72.5 0.2 collective-permute-start.15
  72.7 13.8 %collective-permute-done.14.across = bf16[528,512]{1,0:T(8,128)(2,1)S(1)} collective-permute-done((bf16[528,512]{1,0:T(8,128)(2,1)S(1)}, bf16[528,512]{1,0:T(8,128)(2,1)S(1)}, u32[]{:S(2)}, u32[]{:S(2)}) %collective-permute-start.14) | collective-permute-done | bytes 540704 | tf_op jit(solution)/shard_map/ppermute | solution.py:117
  86.4 0.1 shard_map.86.g
  86.6 4.3 %collective-permute-done.15 = bf16[512,256]{1,0:T(8,128)(2,1)S(1)} collective-permute-done((bf16[512,256]{1,0:T(8,128)(2,1)S(1)}, bf16[512,256]{1,0:T(8,128)(2,1)S(1)}, u32[]{:S(2)}, u32[]{:S(2)}) %collective-permute-start.15) | collective-permute-done | bytes 262176 | tf_op jit(solution)/shard_map/ppermute | solution.py:117
  90.8 0.2 add_convert_fusion.a0
  91.0 0.6 collective-permute-start.16
  91.6 0.7 collective-permute-start.19
  92.3 0.1 pad_add_fusion.place
  92.4 0.7 slice.27
  93.0 0.0 collective-permute-start.17
  93.1 5.1 %collective-permute-done.16.a1 = bf16[512,256]{1,0:T(8,128)(2,1)S(1)} collective-permute-done((bf16[512,256]{1,0:T(8,128)(2,1)S(1)}, bf16[512,256]{1,0:T(8,128)(2,1)S(1)}, u32[]{:S(2)}, u32[]{:S(2)}) %collective-permute-start.16) | collective-permute-done | bytes 262176 | tf_op jit(solution)/shard_map/ppermute | solution.py:117
  98.2 0.0 collective-permute-start.18
  98.2 0.0 collective-permute-done.17.a2
  98.2 1.5 %collective-permute-done.18.a3 = bf16[512,256]{1,0:T(8,128)(2,1)S(1)} collective-permute-done((bf16[512,256]{1,0:T(8,128)(2,1)S(1)}, bf16[512,256]{1,0:T(8,128)(2,1)S(1)}, u32[]{:S(2)}, u32[]{:S(2)}) %collective-permute-start.18) | collective-permute-done | bytes 262176 | tf_op jit(solution)/shard_map/ppermute | solution.py:117
  99.7 4.0 %outer_near.1 = (f32[1024,1024]{1,0:T(8,128)}, f32[512,128]{1,0:T(8,128)S(1)}, bf16[512,1024]{1,0:T(8,128)(2,1)S(1)}, bf16[1024,512]{1,0:T(8,128)(2,1)S(1)}, f32[1024,512]{1,0:T(8,128)S(1)}) custom-call(s32[3]{0:T(128)S(1)} %pad_add_fusion.place, bf16[512,256]{1,0:T(8,128)(2,1)S(1)} %add_convert_fusion.a0, bf16[512,256]{1,0:T(8,128)(2,1)S(1)} %collective-permute-done.16.a1, ...), custom_call_target="tpu_custom_call" | custom-call | flops 1073741824 | bytes 6291456 | tf_op jit(solution)/shard_map/outer_near/pallas_call | solution.py:273
  103.7 0.4 collective-permute-done.19.g
  104.1 2.3 %outer_far.1 = (f32[1024,1024]{1,0:T(8,128)}, f32[4,128]{1,0:T(4,128)S(1)}) custom-call(s32[3]{0:T(128)S(1)} %pad_add_fusion.place, bf16[512,1024]{1,0:T(8,128)(2,1)S(1)} %get-tuple-element.90.flat, bf16[1024,512]{1,0:T(8,128)(2,1)S(1)} %get-tuple-element.91.turned, bf16[512,512]{1,0:T(8,128)(2,1)S(1)} %collective-permute-done.19.g, ...), custom_call_target="tpu_custom_call", output_to_operand_aliasing={{0}: (5, {})} | custom-call | flops 1073741824 | bytes 2097152 | tf_op jit(solution)/shard_map/outer_far/pallas_call | solution.py:304
  106.4 0.1 select_reduce_fusion
  106.6 10.8 %all_to_all.11 = f32[16,1,136]{2,1,0:T(1,128)S(1)} all-to-all(f32[16,1,136]{2,1,0:T(1,128)S(1)} %all_to_all.7), channel_id=1, replica_groups=mesh['grp'=2,'seq'=4,'row'=2,'col'=2] {'seq','row','col'}, dimensions={0} | all-to-all | bytes 17408 | tf_op jit(solution)/shard_map/all_to_all | solution.py:420
  117.4 0.5 finish.1
  (19 shorter events, 0.1 us)
Async XLA Ops:
  0.6 12.3 %collective-permute-start = (bf16[128,1024]{1,0:T(8,128)(2,1)}, bf16[128,1024]{1,0:T(8,128)(2,1)S(1)}, u32[]{:S(2)}, u32[]{:S(2)}) collective-permute-start(bf16[128,1024]{1,0:T(8,128)(2,1)} %param.9), channel_id=1, source_target_pairs={{0,0},{1,4},{2,8},{3,12},{4,2},{5,6},{6,10},{7,14},{8,1},{9,5},{10... | collective-permute-start | bytes 786440 | tf_op jit(solution)/shard_map/ppermute | solution.py:344
  3.9 18.8 %collective-permute-start.2 = (bf16[1024,512]{1,0:T(8,128)(2,1)S(1)}, bf16[1024,512]{1,0:T(8,128)(2,1)}, u32[]{:S(2)}, u32[]{:S(2)}) collective-permute-start(bf16[1024,512]{1,0:T(8,128)(2,1)S(1)} %slice_select_fusion), channel_id=1, source_target_pairs={{0,1},{1,0},{2,3},{3,2},{4,5},{5,4},{6,7},{7,6},{8,9},{9,8},{10,11... | collective-permute-start | bytes 3145736 | tf_op jit(solution)/shard_map/ppermute | solution.py:117
  7.4 12.1 %collective-permute-start.3 = (bf16[128,1024]{1,0:T(8,128)(2,1)}, bf16[128,1024]{1,0:T(8,128)(2,1)}, u32[]{:S(2)}, u32[]{:S(2)}) collective-permute-start(bf16[128,1024]{1,0:T(8,128)(2,1)} %param.8), channel_id=1, source_target_pairs={{0,2},{2,0},{1,3},{3,1},{4,6},{6,4},{5,7},{7,5},{8,10},{10,8},{9,1... | collective-permute-start | bytes 786440 | tf_op jit(solution)/shard_map/ppermute | solution.py:117
  12.9 9.8 %copy-start = (bf16[1024,1024]{1,0:T(8,128)(2,1)S(1)}, bf16[1024,1024]{1,0:T(8,128)(2,1)}, u32[]{:S(2)}) copy-start(bf16[1024,1024]{1,0:T(8,128)(2,1)} %param.11) | copy-start | bytes 6291460
  12.9 12.7 %collective-permute-start.1 = (bf16[128,1024]{1,0:T(8,128)(2,1)S(1)}, bf16[128,1024]{1,0:T(8,128)(2,1)S(1)}, u32[]{:S(2)}, u32[]{:S(2)}) collective-permute-start(bf16[128,1024]{1,0:T(8,128)(2,1)S(1)} %collective-permute-done.x0), channel_id=1, source_target_pairs={{0,2},{2,0},{1,3},{3,1},{4,6},{6,4},{5,7},{7,5},{8,10},{10,8},{9,1... | collective-permute-start | bytes 786440 | tf_op jit(solution)/shard_map/ppermute | solution.py:117
  19.5 9.6 %collective-permute-start.4 = (bf16[128,1024]{1,0:T(8,128)(2,1)}, bf16[128,1024]{1,0:T(8,128)(2,1)}, u32[]{:S(2)}, u32[]{:S(2)}) collective-permute-start(bf16[128,1024]{1,0:T(8,128)(2,1)} %collective-permute-done.3), channel_id=1, source_target_pairs={{0,8},{1,12},{2,0},{3,4},{4,10},{5,14},{6,2},{7,6},{8,9},{9,13},{1... | collective-permute-start | bytes 786440 | tf_op jit(solution)/shard_map/ppermute | solution.py:344
  25.3 1.8 %copy-start.1 = (s32[128]{0:T(128)S(1)}, s32[128]{0:T(128)}, u32[]{:S(2)}) copy-start(s32[128]{0:T(128)} %param.10) | copy-start | bytes 1540
  25.7 3.5 %collective-permute-start.5 = (bf16[128,1024]{1,0:T(8,128)(2,1)S(1)}, bf16[128,1024]{1,0:T(8,128)(2,1)S(1)}, u32[]{:S(2)}, u32[]{:S(2)}) collective-permute-start(bf16[128,1024]{1,0:T(8,128)(2,1)S(1)} %collective-permute-done.x0), channel_id=1, source_target_pairs={{0,1},{1,0},{2,3},{3,2},{4,5},{5,4},{6,7},{7,6},{8,9},{9,8},{10,11... | collective-permute-start | bytes 786440 | tf_op jit(solution)/shard_map/ppermute | solution.py:117
  27.1 2.0 %collective-permute-start.6 = (bf16[128,1024]{1,0:T(8,128)(2,1)S(1)}, bf16[128,1024]{1,0:T(8,128)(2,1)S(1)}, u32[]{:S(2)}, u32[]{:S(2)}) collective-permute-start(bf16[128,1024]{1,0:T(8,128)(2,1)S(1)} %collective-permute-done.1.x1), channel_id=1, source_target_pairs={{0,1},{1,0},{2,3},{3,2},{4,5},{5,4},{6,7},{7,6},{8,9},{9,8},{10,11... | collective-permute-start | bytes 786440 | tf_op jit(solution)/shard_map/ppermute | solution.py:117
  31.1 8.4 %collective-permute-start.7 = (bf16[128,1024]{1,0:T(8,128)(2,1)}, bf16[128,1024]{1,0:T(8,128)(2,1)S(1)}, u32[]{:S(2)}, u32[]{:S(2)}) collective-permute-start(bf16[128,1024]{1,0:T(8,128)(2,1)} %collective-permute-done.4.x0), channel_id=1, source_target_pairs={{0,2},{2,0},{1,3},{3,1},{4,6},{6,4},{5,7},{7,5},{8,10},{10,8},{9,1... | collective-permute-start | bytes 786440 | tf_op jit(solution)/shard_map/ppermute | solution.py:117
  34.5 17.4 %collective-permute-start.10 = (bf16[528,512]{1,0:T(8,128)(2,1)}, bf16[528,512]{1,0:T(8,128)(2,1)}, u32[]{:S(2)}, u32[]{:S(2)}) collective-permute-start(bf16[528,512]{1,0:T(8,128)(2,1)} %get-tuple-element.72), channel_id=1, source_target_pairs={{0,4},{4,0},{8,12},{12,8},{1,5},{5,1},{9,13},{13,9},{2,6},{6,2},{1... | collective-permute-start | bytes 1622024 | tf_op jit(solution)/shard_map/ppermute | solution.py:117
  39.5 5.4 %collective-permute-start.8 = (bf16[128,1024]{1,0:T(8,128)(2,1)}, bf16[128,1024]{1,0:T(8,128)(2,1)}, u32[]{:S(2)}, u32[]{:S(2)}) collective-permute-start(bf16[128,1024]{1,0:T(8,128)(2,1)} %collective-permute-done.4.x0), channel_id=1, source_target_pairs={{0,1},{1,0},{2,3},{3,2},{4,5},{5,4},{6,7},{7,6},{8,9},{9,8},{10,11... | collective-permute-start | bytes 786440 | tf_op jit(solution)/shard_map/ppermute | solution.py:117
  43.0 1.8 %collective-permute-start.9 = (bf16[128,1024]{1,0:T(8,128)(2,1)S(1)}, bf16[128,1024]{1,0:T(8,128)(2,1)}, u32[]{:S(2)}, u32[]{:S(2)}) collective-permute-start(bf16[128,1024]{1,0:T(8,128)(2,1)S(1)} %collective-permute-done.7.x1), channel_id=1, source_target_pairs={{0,1},{1,0},{2,3},{3,2},{4,5},{5,4},{6,7},{7,6},{8,9},{9,8},{10,11... | collective-permute-start | bytes 786440 | tf_op jit(solution)/shard_map/ppermute | solution.py:117
  47.2 8.7 %collective-permute-start.11 = (bf16[512,256]{1,0:T(8,128)(2,1)S(1)}, bf16[512,256]{1,0:T(8,128)(2,1)S(1)}, u32[]{:S(2)}, u32[]{:S(2)}) collective-permute-start(bf16[512,256]{1,0:T(8,128)(2,1)S(1)} %get-tuple-element.77), channel_id=1, source_target_pairs={{0,2},{2,0},{1,3},{3,1},{4,6},{6,4},{5,7},{7,5},{8,10},{10,8},{9,1... | collective-permute-start | bytes 786440 | tf_op jit(solution)/shard_map/ppermute | solution.py:117
  48.4 17.8 %collective-permute-start.12 = (bf16[512,256]{1,0:T(8,128)(2,1)S(1)}, bf16[512,256]{1,0:T(8,128)(2,1)S(1)}, u32[]{:S(2)}, u32[]{:S(2)}) collective-permute-start(bf16[512,256]{1,0:T(8,128)(2,1)S(1)} %get-tuple-element.78), channel_id=1, source_target_pairs={{0,4},{4,0},{8,12},{12,8},{1,5},{5,1},{9,13},{13,9},{2,6},{6,2},{1... | collective-permute-start | bytes 786440 | tf_op jit(solution)/shard_map/ppermute | solution.py:117
  50.6 21.8 %collective-permute-start.13 = (bf16[512,256]{1,0:T(8,128)(2,1)S(1)}, bf16[512,256]{1,0:T(8,128)(2,1)S(1)}, u32[]{:S(2)}, u32[]{:S(2)}) collective-permute-start(bf16[512,256]{1,0:T(8,128)(2,1)S(1)} %get-tuple-element.79), channel_id=1, source_target_pairs={{0,6},{2,4},{4,2},{6,0},{8,14},{10,12},{12,10},{14,8},{1,7},{3,5},... | collective-permute-start | bytes 786440 | tf_op jit(solution)/shard_map/ppermute | solution.py:382
  53.1 33.3 %collective-permute-start.14 = (bf16[528,512]{1,0:T(8,128)(2,1)S(1)}, bf16[528,512]{1,0:T(8,128)(2,1)S(1)}, u32[]{:S(2)}, u32[]{:S(2)}) collective-permute-start(bf16[528,512]{1,0:T(8,128)(2,1)S(1)} %shard_map.85.pair), channel_id=1, source_target_pairs={{0,8},{4,12},{8,0},{12,4},{1,9},{5,13},{9,1},{13,5},{2,10},{6,14},... | collective-permute-start | bytes 1622024 | tf_op jit(solution)/shard_map/ppermute | solution.py:117
  72.5 18.3 %collective-permute-start.15 = (bf16[512,256]{1,0:T(8,128)(2,1)S(1)}, bf16[512,256]{1,0:T(8,128)(2,1)S(1)}, u32[]{:S(2)}, u32[]{:S(2)}) collective-permute-start(bf16[512,256]{1,0:T(8,128)(2,1)S(1)} %select_convert_fusion), channel_id=1, source_target_pairs={{0,8},{4,12},{8,0},{12,4},{1,9},{5,13},{9,1},{13,5},{2,10},{6,14},... | collective-permute-start | bytes 786440 | tf_op jit(solution)/shard_map/ppermute | solution.py:117
  91.0 7.2 %collective-permute-start.16 = (bf16[512,256]{1,0:T(8,128)(2,1)S(1)}, bf16[512,256]{1,0:T(8,128)(2,1)S(1)}, u32[]{:S(2)}, u32[]{:S(2)}) collective-permute-start(bf16[512,256]{1,0:T(8,128)(2,1)S(1)} %add_convert_fusion.a0), channel_id=1, source_target_pairs={{0,2},{2,0},{1,3},{3,1},{4,6},{6,4},{5,7},{7,5},{8,10},{10,8},{9,1... | collective-permute-start | bytes 786440 | tf_op jit(solution)/shard_map/ppermute | solution.py:117
  91.6 12.4 %collective-permute-start.19 = (bf16[512,512]{1,0:T(8,128)(2,1)S(1)}, bf16[512,512]{1,0:T(8,128)(2,1)S(1)}, u32[]{:S(2)}, u32[]{:S(2)}) collective-permute-start(bf16[512,512]{1,0:T(8,128)(2,1)S(1)} %shard_map.86.g), channel_id=1, source_target_pairs={{0,4},{4,0},{8,12},{12,8},{1,5},{5,1},{9,13},{13,9},{2,6},{6,2},{1... | collective-permute-start | bytes 1572872 | tf_op jit(solution)/shard_map/ppermute | solution.py:117
  93.0 5.2 %collective-permute-start.17 = (bf16[512,256]{1,0:T(8,128)(2,1)S(1)}, bf16[512,256]{1,0:T(8,128)(2,1)S(1)}, u32[]{:S(2)}, u32[]{:S(2)}) collective-permute-start(bf16[512,256]{1,0:T(8,128)(2,1)S(1)} %add_convert_fusion.a0), channel_id=1, source_target_pairs={{0,1},{1,0},{2,3},{3,2},{4,5},{5,4},{6,7},{7,6},{8,9},{9,8},{10,11... | collective-permute-start | bytes 786440 | tf_op jit(solution)/shard_map/ppermute | solution.py:117
  98.2 1.5 %collective-permute-start.18 = (bf16[512,256]{1,0:T(8,128)(2,1)S(1)}, bf16[512,256]{1,0:T(8,128)(2,1)S(1)}, u32[]{:S(2)}, u32[]{:S(2)}) collective-permute-start(bf16[512,256]{1,0:T(8,128)(2,1)S(1)} %collective-permute-done.16.a1), channel_id=1, source_target_pairs={{0,1},{1,0},{2,3},{3,2},{4,5},{5,4},{6,7},{7,6},{8,9},{9,8},{10,11... | collective-permute-start | bytes 786440 | tf_op jit(solution)/shard_map/ppermute | solution.py:117

commit v8 on v7

--- a/solution.py
+++ b/solution.py
@@ -262,7 +262,7 @@
 def finish_kernel(scale_score, scale_influence, parts, scores, influence):
     tok = scores.shape[0]
     scores[...] = jnp.sum(parts[:, :tok], axis=0) * scale_score
-    influence[...] = jnp.sum(parts[:, tok:], axis=0) * scale_influence
+    influence[...] = jnp.sum(parts[:, tok : tok + SOURCES], axis=0) * scale_influence
 
 
 def outer_near(place, acts, grads, eigvals):
@@ -374,7 +374,7 @@
     got_g = swap(send_g, "seq", 1)
     acts_here, keep_g = tie(acts_here, keep_g)
     acts_far = swap(acts_here, "row")
-    token, keep_g = stand(token, keep_g)
+    token, keep_g = tie(token, keep_g)
     token, acts_far, acts_here = tie(token, acts_far, acts_here)
     acts_both = swap(acts_far, "col")
     acts_near = swap(acts_here, "col")
@@ -401,7 +401,6 @@
     near_g = small_call(sum_kernel, count, pair_g, across_g)
     token, near_g = tie(token, near_g)
     far_g = swap(near_g, "seq", 1)
-    (token,) = stand(token)
     token, cross = tie(token, cross)
     own_a = (stay + cross.astype(jnp.float32)).astype(jnp.bfloat16)
     quarters = plane_gather(own_a)
@@ -415,8 +414,9 @@
     part = jnp.sum(jnp.where(chosen, slots[None], 0.0), axis=(1, 2))
     blocks = jnp.stack([lax.dynamic_index_in_dim(slots, u ^ j, keepdims=False) for j in range(seqs)])
     message = jnp.concatenate([blocks, jnp.broadcast_to(part[None, :], (seqs, SOURCES))], axis=1)
-    message = jnp.broadcast_to(message[:, None, :], (seqs, rows * cols, tok + SOURCES))
-    message = message.reshape(seqs * rows * cols, tok + SOURCES)
+    message = jnp.pad(message, ((0, 0), (0, tok - SOURCES)))
+    message = jnp.broadcast_to(message[:, None, :], (seqs, rows * cols, 2 * tok))
+    message = message.reshape(seqs * rows * cols, 2 * tok)
     parts = lax.all_to_all(message, PLANE, split_axis=0, concat_axis=0, tiled=True)
     scale_score = float(total_tokens) / float(width * width)
     vmem = pl.BlockSpec(memory_space=pltpu.VMEM)

time: 118 us -> 118 us (level)
  waiting for transfers between devices: 53.3 us -> 55.3 us
  starting transfers between devices: 32.8 us -> 30.8 us
    ppermute x17, starting transfers between devices: 26.6 us -> 24.7 us  [swap(): lax.ppermute(x, axis, [(i, i ^ step) for i in range(lax.axis_size(axis))])]
    unnamed x5 -> x7, local copies, waits for them, and re-layouts: 0.01 us -> 1.6 us
    dynamic_slice x1, local copies, waits for them, and re-layouts: 1.68 us -> 0.24 us  [local_pairs(): lax.dynamic_slice_in_dim(basis_out, at * half, half, axis=1)]
    ppermute x2, waiting for transfers between devices: 1.95 us -> 3.16 us  [turned(): return lax.ppermute(x, PLANE, pairs)]
    select_n x1, other arithmetic: 1.69 us -> 0.5 us  [local_pairs(): jnp.where(k == low, theirs, mine)]
  transfers between devices with their start and end apart: 20 -> 20, of which waited for: 12 -> 13; matrix products, arithmetic and copies ran while one was open for 6% -> 5% of each run, Pallas kernels for 6% -> 6%
where the time goes in v8:
time: 118 us
  waiting for transfers between devices  55.3 us (47%)
  starting transfers between devices  30.8 us (26%)
  Pallas kernels  12.5 us (11%)
  blocking collectives  10.8 us (9%)
  other arithmetic  5.07 us (4%)
  local copies, waits for them, and re-layouts  2.67 us (2%)
    ppermute x17, waiting for transfers between devices, swap(): lax.ppermute(x, axis, [(i, i ^ step) for i in range(lax.axis_size(axis))])  46 us
    ppermute x17, starting transfers between devices, swap(): lax.ppermute(x, axis, [(i, i ^ step) for i in range(lax.axis_size(axis))])  24.7 us
    all_to_all x1, blocking collectives, local_pairs(): lax.all_to_all(message, PLANE, split_axis=0, concat_axis=0, tiled=True)  10.8 us
    ppermute x1, waiting for transfers between devices, local_pairs(): lax.ppermute(to_both, ('seq', 'row'), [(i * rows + j, (i ^ 1) * rows + (j...  6.14 us
    ppermute x2, starting transfers between devices, turned(): return lax.ppermute(x, PLANE, pairs)  4.78 us
    pallas_call x2, Pallas kernels, rotate(): pl.pallas_call(functools.partial(rotate_kernel, notes=len(note), flips=fl...  4.34 us
    pallas_call x1, Pallas kernels, outer_near(): pl.pallas_call(near_kernel, out_shape=(jax.ShapeDtypeStruct(eigvals.shape...  3.96 us
    ppermute x2, waiting for transfers between devices, turned(): return lax.ppermute(x, PLANE, pairs)  3.16 us
  transfers between devices with their start and end apart: 20, of which 13 were waited for; matrix products, arithmetic and copies ran while one was open for 5% of the time, Pallas kernels for 6%

profile of v8, /device:TPU:0, one launch (start us, length us, event | category | flops | bytes accessed | tf_op | source)
XLA Modules:
  0.0 118.0 jit_solution(7113661987078232890)
XLA Ops:
  0.6 1.6 %collective-permute-start = (bf16[128,1024]{1,0:T(8,128)(2,1)}, bf16[128,1024]{1,0:T(8,128)(2,1)S(1)}, u32[]{:S(2)}, u32[]{:S(2)}) collective-permute-start(bf16[128,1024]{1,0:T(8,128)(2,1)} %param.9), channel_id=1, source_target_pairs={{0,0},{1,4},{2,8},{3,12},{4,2},{5,6},{6,10},{7,14},{8,1},{9,5},{10... | collective-permute-start | bytes 786440 | tf_op jit(solution)/shard_map/ppermute | solution.py:344
  2.2 2.6 %slice_select_fusion = bf16[1024,512]{1,0:T(8,128)(2,1)} fusion(bf16[1024,1024]{1,0:T(8,128)(2,1)} %param.11, pred[]{:T(512)S(6)} %eq.30), kind=kLoop, calls=%fused_computation.8 | loop fusion | flops 524288 | bytes 3145729 | tf_op jit(solution)/shard_map/jit(_where)/select_n | solution.py:354
  4.9 3.5 %collective-permute-start.2 = (bf16[1024,512]{1,0:T(8,128)(2,1)}, bf16[1024,512]{1,0:T(8,128)(2,1)S(1)}, u32[]{:S(2)}, u32[]{:S(2)}) collective-permute-start(bf16[1024,512]{1,0:T(8,128)(2,1)} %slice_select_fusion), channel_id=1, source_target_pairs={{0,1},{1,0},{2,3},{3,2},{4,5},{5,4},{6,7},{7,6},{8,9},{9,8},{10,11... | collective-permute-start | bytes 3145736 | tf_op jit(solution)/shard_map/ppermute | solution.py:117
  8.3 3.5 %collective-permute-start.3 = (bf16[128,1024]{1,0:T(8,128)(2,1)}, bf16[128,1024]{1,0:T(8,128)(2,1)}, u32[]{:S(2)}, u32[]{:S(2)}) collective-permute-start(bf16[128,1024]{1,0:T(8,128)(2,1)} %param.8), channel_id=1, source_target_pairs={{0,2},{2,0},{1,3},{3,1},{4,6},{6,4},{5,7},{7,5},{8,10},{10,8},{9,1... | collective-permute-start | bytes 786440 | tf_op jit(solution)/shard_map/ppermute | solution.py:117
  11.8 1.6 %copy-done.1 = bf16[1024,1024]{1,0:T(8,128)(2,1)S(1)} copy-done((bf16[1024,1024]{1,0:T(8,128)(2,1)S(1)}, bf16[1024,1024]{1,0:T(8,128)(2,1)}, u32[]{:S(2)}) %copy-start.1) | copy-done | bytes 2097176
  13.4 0.2 constant_dynamic-slice_fusion.9
  13.6 0.3 pad_maximum_fusion.basis
  14.0 0.0 copy-start
  14.0 0.0 collective-permute-done.x0
  14.0 1.5 %collective-permute-start.1 = (bf16[128,1024]{1,0:T(8,128)(2,1)S(1)}, bf16[128,1024]{1,0:T(8,128)(2,1)S(1)}, u32[]{:S(2)}, u32[]{:S(2)}) collective-permute-start(bf16[128,1024]{1,0:T(8,128)(2,1)S(1)} %collective-permute-done.x0), channel_id=1, source_target_pairs={{0,2},{2,0},{1,3},{3,1},{4,6},{6,4},{5,7},{7,5},{8,10},{10,8},{9,1... | collective-permute-start | bytes 786440 | tf_op jit(solution)/shard_map/ppermute | solution.py:117
  15.4 4.1 %collective-permute-done.3 = bf16[128,1024]{1,0:T(8,128)(2,1)} collective-permute-done((bf16[128,1024]{1,0:T(8,128)(2,1)}, bf16[128,1024]{1,0:T(8,128)(2,1)}, u32[]{:S(2)}, u32[]{:S(2)}) %collective-permute-start.3) | collective-permute-done | bytes 262176 | tf_op jit(solution)/shard_map/ppermute | solution.py:117
  19.5 3.2 %collective-permute-start.4 = (bf16[128,1024]{1,0:T(8,128)(2,1)}, bf16[128,1024]{1,0:T(8,128)(2,1)}, u32[]{:S(2)}, u32[]{:S(2)}) collective-permute-start(bf16[128,1024]{1,0:T(8,128)(2,1)} %collective-permute-done.3), channel_id=1, source_target_pairs={{0,8},{1,12},{2,0},{3,4},{4,10},{5,14},{6,2},{7,6},{8,9},{9,13},{1... | collective-permute-start | bytes 786440 | tf_op jit(solution)/shard_map/ppermute | solution.py:344
  22.7 0.0 collective-permute-done.2
  22.7 0.5 broadcast_select_fusion.1
  23.2 0.4 fusion.1
  23.6 0.1 fusion.2
  23.7 0.4 fusion
  24.1 0.0 copy-start.2
  24.1 0.3 pad_maximum_fusion.1.basis
  24.4 0.5 collective-permute-done.1.x1
  24.9 0.9 collective-permute-start.5
  25.9 0.1 collective-permute-start.6
  26.0 3.2 %collective-permute-done.4.x0 = bf16[128,1024]{1,0:T(8,128)(2,1)} collective-permute-done((bf16[128,1024]{1,0:T(8,128)(2,1)}, bf16[128,1024]{1,0:T(8,128)(2,1)}, u32[]{:S(2)}, u32[]{:S(2)}) %collective-permute-start.4) | collective-permute-done | bytes 262176 | tf_op jit(solution)/shard_map/ppermute | solution.py:344
  29.1 0.0 collective-permute-done.5.x2
  29.1 0.0 collective-permute-done.6.x3
  29.1 2.0 %rotate.2 = (bf16[528,512]{1,0:T(8,128)(2,1)}, f32[512,512]{1,0:T(8,128)S(1)}) custom-call(bf16[128,1024]{1,0:T(8,128)(2,1)S(1)} %collective-permute-done.x0, bf16[128,1024]{1,0:T(8,128)(2,1)S(1)} %collective-permute-done.1.x1, bf16[128,1024]{1,0:T(8,128)(2,1)S(1)} %collective-permute-done.5.x2, bf16[128,1024]{1,0:T(8,128)(2,1)S(1)} %collective-permute-done.6.x3, ...), custom_call_target="tpu_custom_call" | custom-call | flops 1073741824 | bytes 2097152 | tf_op jit(solution)/shard_map/rotate/pallas_call | solution.py:165
  31.1 3.5 %collective-permute-start.7 = (bf16[128,1024]{1,0:T(8,128)(2,1)}, bf16[128,1024]{1,0:T(8,128)(2,1)S(1)}, u32[]{:S(2)}, u32[]{:S(2)}) collective-permute-start(bf16[128,1024]{1,0:T(8,128)(2,1)} %collective-permute-done.4.x0), channel_id=1, source_target_pairs={{0,2},{2,0},{1,3},{3,1},{4,6},{6,4},{5,7},{7,5},{8,10},{10,8},{9,1... | collective-permute-start | bytes 786440 | tf_op jit(solution)/shard_map/ppermute | solution.py:117
  34.6 2.1 %collective-permute-start.10 = (bf16[528,512]{1,0:T(8,128)(2,1)}, bf16[528,512]{1,0:T(8,128)(2,1)}, u32[]{:S(2)}, u32[]{:S(2)}) collective-permute-start(bf16[528,512]{1,0:T(8,128)(2,1)} %get-tuple-element.72), channel_id=1, source_target_pairs={{0,4},{4,0},{8,12},{12,8},{1,5},{5,1},{9,13},{13,9},{2,6},{6,2},{1... | collective-permute-start | bytes 1622024 | tf_op jit(solution)/shard_map/ppermute | solution.py:117
  36.7 3.1 %collective-permute-done.7.x1 = bf16[128,1024]{1,0:T(8,128)(2,1)S(1)} collective-permute-done((bf16[128,1024]{1,0:T(8,128)(2,1)}, bf16[128,1024]{1,0:T(8,128)(2,1)S(1)}, u32[]{:S(2)}, u32[]{:S(2)}) %collective-permute-start.7) | collective-permute-done | bytes 262176 | tf_op jit(solution)/shard_map/ppermute | solution.py:117
  39.8 3.2 %collective-permute-start.8 = (bf16[128,1024]{1,0:T(8,128)(2,1)}, bf16[128,1024]{1,0:T(8,128)(2,1)}, u32[]{:S(2)}, u32[]{:S(2)}) collective-permute-start(bf16[128,1024]{1,0:T(8,128)(2,1)} %collective-permute-done.4.x0), channel_id=1, source_target_pairs={{0,1},{1,0},{2,3},{3,2},{4,5},{5,4},{6,7},{7,6},{8,9},{9,8},{10,11... | collective-permute-start | bytes 786440 | tf_op jit(solution)/shard_map/ppermute | solution.py:117
  43.0 0.0 collective-permute-start.9
  43.0 1.8 %collective-permute-done.8.x2 = bf16[128,1024]{1,0:T(8,128)(2,1)} collective-permute-done((bf16[128,1024]{1,0:T(8,128)(2,1)}, bf16[128,1024]{1,0:T(8,128)(2,1)}, u32[]{:S(2)}, u32[]{:S(2)}) %collective-permute-start.8) | collective-permute-done | bytes 262176 | tf_op jit(solution)/shard_map/ppermute | solution.py:117
  44.8 0.0 collective-permute-done.9.x3
  44.8 2.4 %rotate.3 = (bf16[512,256]{1,0:T(8,128)(2,1)S(1)}, bf16[512,256]{1,0:T(8,128)(2,1)S(1)}, bf16[512,256]{1,0:T(8,128)(2,1)S(1)}, f32[512,256]{1,0:T(8,128)S(1)}) custom-call(bf16[128,1024]{1,0:T(8,128)(2,1)} %collective-permute-done.4.x0, bf16[128,1024]{1,0:T(8,128)(2,1)S(1)} %collective-permute-done.7.x1, bf16[128,1024]{1,0:T(8,128)(2,1)} %collective-permute-done.8.x2, ...), custom_call_target="tpu_custom_call" | custom-call | flops 1073741824 | bytes 2097152 | tf_op jit(solution)/shard_map/rotate/pallas_call | solution.py:165
  47.2 1.4 %collective-permute-start.11 = (bf16[512,256]{1,0:T(8,128)(2,1)S(1)}, bf16[512,256]{1,0:T(8,128)(2,1)S(1)}, u32[]{:S(2)}, u32[]{:S(2)}) collective-permute-start(bf16[512,256]{1,0:T(8,128)(2,1)S(1)} %get-tuple-element.77), channel_id=1, source_target_pairs={{0,2},{2,0},{1,3},{3,1},{4,6},{6,4},{5,7},{7,5},{8,10},{10,8},{9,1... | collective-permute-start | bytes 786440 | tf_op jit(solution)/shard_map/ppermute | solution.py:117
  48.5 2.1 %collective-permute-start.12 = (bf16[512,256]{1,0:T(8,128)(2,1)S(1)}, bf16[512,256]{1,0:T(8,128)(2,1)S(1)}, u32[]{:S(2)}, u32[]{:S(2)}) collective-permute-start(bf16[512,256]{1,0:T(8,128)(2,1)S(1)} %get-tuple-element.78), channel_id=1, source_target_pairs={{0,4},{4,0},{8,12},{12,8},{1,5},{5,1},{9,13},{13,9},{2,6},{6,2},{1... | collective-permute-start | bytes 786440 | tf_op jit(solution)/shard_map/ppermute | solution.py:117
  50.6 1.4 %collective-permute-start.13 = (bf16[512,256]{1,0:T(8,128)(2,1)S(1)}, bf16[512,256]{1,0:T(8,128)(2,1)S(1)}, u32[]{:S(2)}, u32[]{:S(2)}) collective-permute-start(bf16[512,256]{1,0:T(8,128)(2,1)S(1)} %get-tuple-element.79), channel_id=1, source_target_pairs={{0,6},{2,4},{4,2},{6,0},{8,14},{10,12},{12,10},{14,8},{1,7},{3,5},... | collective-permute-start | bytes 786440 | tf_op jit(solution)/shard_map/ppermute | solution.py:382
  52.0 0.0 collective-permute-done.10.got
  52.0 1.2 %shard_map.85.pair = bf16[528,512]{1,0:T(8,128)(2,1)S(1)} custom-call(f32[512,512]{1,0:T(8,128)S(1)} %get-tuple-element.74.keep, bf16[528,512]{1,0:T(8,128)(2,1)} %collective-permute-done.10.got, bf16[16,512]{1,0:T(8,128)(2,1)S(1)} %pad.9.refs_0_.note), custom_call_target="tpu_custom_call" | custom-call | flops 270336 | bytes 2162688 | tf_op jit(solution)/shard_map/pallas_call | solution.py:194
  53.2 1.6 %collective-permute-start.14 = (bf16[528,512]{1,0:T(8,128)(2,1)S(1)}, bf16[528,512]{1,0:T(8,128)(2,1)S(1)}, u32[]{:S(2)}, u32[]{:S(2)}) collective-permute-start(bf16[528,512]{1,0:T(8,128)(2,1)S(1)} %shard_map.85.pair), channel_id=1, source_target_pairs={{0,8},{4,12},{8,0},{12,4},{1,9},{5,13},{9,1},{13,5},{2,10},{6,14},... | collective-permute-start | bytes 1622024 | tf_op jit(solution)/shard_map/ppermute | solution.py:117
  54.8 1.1 collective-permute-done.11
  55.8 10.4 %collective-permute-done.12 = bf16[512,256]{1,0:T(8,128)(2,1)S(1)} collective-permute-done((bf16[512,256]{1,0:T(8,128)(2,1)S(1)}, bf16[512,256]{1,0:T(8,128)(2,1)S(1)}, u32[]{:S(2)}, u32[]{:S(2)}) %collective-permute-start.12) | collective-permute-done | bytes 262176 | tf_op jit(solution)/shard_map/ppermute | solution.py:117
  66.2 6.1 %collective-permute-done.13 = bf16[512,256]{1,0:T(8,128)(2,1)S(1)} collective-permute-done((bf16[512,256]{1,0:T(8,128)(2,1)S(1)}, bf16[512,256]{1,0:T(8,128)(2,1)S(1)}, u32[]{:S(2)}, u32[]{:S(2)}) %collective-permute-start.13) | collective-permute-done | bytes 262176 | tf_op jit(solution)/shard_map/ppermute | solution.py:382
  72.4 0.1 select_convert_fusion
  72.5 0.2 collective-permute-start.15
  72.6 13.9 %collective-permute-done.14.across = bf16[528,512]{1,0:T(8,128)(2,1)S(1)} collective-permute-done((bf16[528,512]{1,0:T(8,128)(2,1)S(1)}, bf16[528,512]{1,0:T(8,128)(2,1)S(1)}, u32[]{:S(2)}, u32[]{:S(2)}) %collective-permute-start.14) | collective-permute-done | bytes 540704 | tf_op jit(solution)/shard_map/ppermute | solution.py:117
  86.6 0.1 shard_map.86.g
  86.7 4.2 %collective-permute-done.15 = bf16[512,256]{1,0:T(8,128)(2,1)S(1)} collective-permute-done((bf16[512,256]{1,0:T(8,128)(2,1)S(1)}, bf16[512,256]{1,0:T(8,128)(2,1)S(1)}, u32[]{:S(2)}, u32[]{:S(2)}) %collective-permute-start.15) | collective-permute-done | bytes 262176 | tf_op jit(solution)/shard_map/ppermute | solution.py:117
  90.9 0.2 add_convert_fusion.a0
  91.1 0.6 collective-permute-start.16
  91.7 0.7 collective-permute-start.19
  92.3 0.1 pad_add_fusion.place
  92.4 0.7 slice.27
  93.1 0.0 collective-permute-start.17
  93.1 5.1 %collective-permute-done.16.a1 = bf16[512,256]{1,0:T(8,128)(2,1)S(1)} collective-permute-done((bf16[512,256]{1,0:T(8,128)(2,1)S(1)}, bf16[512,256]{1,0:T(8,128)(2,1)S(1)}, u32[]{:S(2)}, u32[]{:S(2)}) %collective-permute-start.16) | collective-permute-done | bytes 262176 | tf_op jit(solution)/shard_map/ppermute | solution.py:117
  98.2 0.0 collective-permute-start.18
  98.2 0.0 collective-permute-done.17.a2
  98.2 1.5 %collective-permute-done.18.a3 = bf16[512,256]{1,0:T(8,128)(2,1)S(1)} collective-permute-done((bf16[512,256]{1,0:T(8,128)(2,1)S(1)}, bf16[512,256]{1,0:T(8,128)(2,1)S(1)}, u32[]{:S(2)}, u32[]{:S(2)}) %collective-permute-start.18) | collective-permute-done | bytes 262176 | tf_op jit(solution)/shard_map/ppermute | solution.py:117
  99.7 4.0 %outer_near.1 = (f32[1024,1024]{1,0:T(8,128)}, f32[512,128]{1,0:T(8,128)S(1)}, bf16[512,1024]{1,0:T(8,128)(2,1)S(1)}, bf16[1024,512]{1,0:T(8,128)(2,1)S(1)}, f32[1024,512]{1,0:T(8,128)S(1)}) custom-call(s32[3]{0:T(128)S(1)} %pad_add_fusion.place, bf16[512,256]{1,0:T(8,128)(2,1)S(1)} %add_convert_fusion.a0, bf16[512,256]{1,0:T(8,128)(2,1)S(1)} %collective-permute-done.16.a1, ...), custom_call_target="tpu_custom_call" | custom-call | flops 1073741824 | bytes 6291456 | tf_op jit(solution)/shard_map/outer_near/pallas_call | solution.py:273
  103.7 0.4 collective-permute-done.19.g
  104.0 2.3 %outer_far.1 = (f32[1024,1024]{1,0:T(8,128)}, f32[4,128]{1,0:T(4,128)S(1)}) custom-call(s32[3]{0:T(128)S(1)} %pad_add_fusion.place, bf16[512,1024]{1,0:T(8,128)(2,1)S(1)} %get-tuple-element.90.flat, bf16[1024,512]{1,0:T(8,128)(2,1)S(1)} %get-tuple-element.91.turned, bf16[512,512]{1,0:T(8,128)(2,1)S(1)} %collective-permute-done.19.g, ...), custom_call_target="tpu_custom_call", output_to_operand_aliasing={{0}: (5, {})} | custom-call | flops 1073741824 | bytes 2097152 | tf_op jit(solution)/shard_map/outer_far/pallas_call | solution.py:304
  106.4 0.1 select_reduce_fusion
  106.6 10.8 %all_to_all.11 = f32[16,1,256]{2,1,0:T(1,128)S(1)} all-to-all(f32[16,1,256]{2,1,0:T(1,128)S(1)} %all_to_all.7), channel_id=1, replica_groups=mesh['grp'=2,'seq'=4,'row'=2,'col'=2] {'seq','row','col'}, dimensions={0} | all-to-all | bytes 32768 | tf_op jit(solution)/shard_map/all_to_all | solution.py:420
  117.5 0.5 finish.1
  (20 shorter events, 0.1 us)
Async XLA Ops:
  0.6 13.3 %collective-permute-start = (bf16[128,1024]{1,0:T(8,128)(2,1)}, bf16[128,1024]{1,0:T(8,128)(2,1)S(1)}, u32[]{:S(2)}, u32[]{:S(2)}) collective-permute-start(bf16[128,1024]{1,0:T(8,128)(2,1)} %param.9), channel_id=1, source_target_pairs={{0,0},{1,4},{2,8},{3,12},{4,2},{5,6},{6,10},{7,14},{8,1},{9,5},{10... | collective-permute-start | bytes 786440 | tf_op jit(solution)/shard_map/ppermute | solution.py:344
  4.9 17.9 %collective-permute-start.2 = (bf16[1024,512]{1,0:T(8,128)(2,1)}, bf16[1024,512]{1,0:T(8,128)(2,1)S(1)}, u32[]{:S(2)}, u32[]{:S(2)}) collective-permute-start(bf16[1024,512]{1,0:T(8,128)(2,1)} %slice_select_fusion), channel_id=1, source_target_pairs={{0,1},{1,0},{2,3},{3,2},{4,5},{5,4},{6,7},{7,6},{8,9},{9,8},{10,11... | collective-permute-start | bytes 3145736 | tf_op jit(solution)/shard_map/ppermute | solution.py:117
  8.3 11.2 %collective-permute-start.3 = (bf16[128,1024]{1,0:T(8,128)(2,1)}, bf16[128,1024]{1,0:T(8,128)(2,1)}, u32[]{:S(2)}, u32[]{:S(2)}) collective-permute-start(bf16[128,1024]{1,0:T(8,128)(2,1)} %param.8), channel_id=1, source_target_pairs={{0,2},{2,0},{1,3},{3,1},{4,6},{6,4},{5,7},{7,5},{8,10},{10,8},{9,1... | collective-permute-start | bytes 786440 | tf_op jit(solution)/shard_map/ppermute | solution.py:117
  11.8 1.6 %copy-start.1 = (bf16[1024,1024]{1,0:T(8,128)(2,1)S(1)}, bf16[1024,1024]{1,0:T(8,128)(2,1)}, u32[]{:S(2)}) copy-start(bf16[1024,1024]{1,0:T(8,128)(2,1)} %param.12) | copy-start | bytes 6291460
  14.0 8.8 %copy-start = (bf16[1024,1024]{1,0:T(8,128)(2,1)S(1)}, bf16[1024,1024]{1,0:T(8,128)(2,1)}, u32[]{:S(2)}) copy-start(bf16[1024,1024]{1,0:T(8,128)(2,1)} %param.11) | copy-start | bytes 6291460
  14.0 11.0 %collective-permute-start.1 = (bf16[128,1024]{1,0:T(8,128)(2,1)S(1)}, bf16[128,1024]{1,0:T(8,128)(2,1)S(1)}, u32[]{:S(2)}, u32[]{:S(2)}) collective-permute-start(bf16[128,1024]{1,0:T(8,128)(2,1)S(1)} %collective-permute-done.x0), channel_id=1, source_target_pairs={{0,2},{2,0},{1,3},{3,1},{4,6},{6,4},{5,7},{7,5},{8,10},{10,8},{9,1... | collective-permute-start | bytes 786440 | tf_op jit(solution)/shard_map/ppermute | solution.py:117
  19.5 9.6 %collective-permute-start.4 = (bf16[128,1024]{1,0:T(8,128)(2,1)}, bf16[128,1024]{1,0:T(8,128)(2,1)}, u32[]{:S(2)}, u32[]{:S(2)}) collective-permute-start(bf16[128,1024]{1,0:T(8,128)(2,1)} %collective-permute-done.3), channel_id=1, source_target_pairs={{0,8},{1,12},{2,0},{3,4},{4,10},{5,14},{6,2},{7,6},{8,9},{9,13},{1... | collective-permute-start | bytes 786440 | tf_op jit(solution)/shard_map/ppermute | solution.py:344
  24.1 1.8 %copy-start.2 = (s32[128]{0:T(128)S(1)}, s32[128]{0:T(128)}, u32[]{:S(2)}) copy-start(s32[128]{0:T(128)} %param.10) | copy-start | bytes 1540
  24.9 4.2 %collective-permute-start.5 = (bf16[128,1024]{1,0:T(8,128)(2,1)S(1)}, bf16[128,1024]{1,0:T(8,128)(2,1)S(1)}, u32[]{:S(2)}, u32[]{:S(2)}) collective-permute-start(bf16[128,1024]{1,0:T(8,128)(2,1)S(1)} %collective-permute-done.x0), channel_id=1, source_target_pairs={{0,1},{1,0},{2,3},{3,2},{4,5},{5,4},{6,7},{7,6},{8,9},{9,8},{10,11... | collective-permute-start | bytes 786440 | tf_op jit(solution)/shard_map/ppermute | solution.py:117
  25.9 3.3 %collective-permute-start.6 = (bf16[128,1024]{1,0:T(8,128)(2,1)S(1)}, bf16[128,1024]{1,0:T(8,128)(2,1)S(1)}, u32[]{:S(2)}, u32[]{:S(2)}) collective-permute-start(bf16[128,1024]{1,0:T(8,128)(2,1)S(1)} %collective-permute-done.1.x1), channel_id=1, source_target_pairs={{0,1},{1,0},{2,3},{3,2},{4,5},{5,4},{6,7},{7,6},{8,9},{9,8},{10,11... | collective-permute-start | bytes 786440 | tf_op jit(solution)/shard_map/ppermute | solution.py:117
  31.1 8.6 %collective-permute-start.7 = (bf16[128,1024]{1,0:T(8,128)(2,1)}, bf16[128,1024]{1,0:T(8,128)(2,1)S(1)}, u32[]{:S(2)}, u32[]{:S(2)}) collective-permute-start(bf16[128,1024]{1,0:T(8,128)(2,1)} %collective-permute-done.4.x0), channel_id=1, source_target_pairs={{0,2},{2,0},{1,3},{3,1},{4,6},{6,4},{5,7},{7,5},{8,10},{10,8},{9,1... | collective-permute-start | bytes 786440 | tf_op jit(solution)/shard_map/ppermute | solution.py:117
  34.6 17.4 %collective-permute-start.10 = (bf16[528,512]{1,0:T(8,128)(2,1)}, bf16[528,512]{1,0:T(8,128)(2,1)}, u32[]{:S(2)}, u32[]{:S(2)}) collective-permute-start(bf16[528,512]{1,0:T(8,128)(2,1)} %get-tuple-element.72), channel_id=1, source_target_pairs={{0,4},{4,0},{8,12},{12,8},{1,5},{5,1},{9,13},{13,9},{2,6},{6,2},{1... | collective-permute-start | bytes 1622024 | tf_op jit(solution)/shard_map/ppermute | solution.py:117
  39.8 5.1 %collective-permute-start.8 = (bf16[128,1024]{1,0:T(8,128)(2,1)}, bf16[128,1024]{1,0:T(8,128)(2,1)}, u32[]{:S(2)}, u32[]{:S(2)}) collective-permute-start(bf16[128,1024]{1,0:T(8,128)(2,1)} %collective-permute-done.4.x0), channel_id=1, source_target_pairs={{0,1},{1,0},{2,3},{3,2},{4,5},{5,4},{6,7},{7,6},{8,9},{9,8},{10,11... | collective-permute-start | bytes 786440 | tf_op jit(solution)/shard_map/ppermute | solution.py:117
  43.0 1.8 %collective-permute-start.9 = (bf16[128,1024]{1,0:T(8,128)(2,1)S(1)}, bf16[128,1024]{1,0:T(8,128)(2,1)}, u32[]{:S(2)}, u32[]{:S(2)}) collective-permute-start(bf16[128,1024]{1,0:T(8,128)(2,1)S(1)} %collective-permute-done.7.x1), channel_id=1, source_target_pairs={{0,1},{1,0},{2,3},{3,2},{4,5},{5,4},{6,7},{7,6},{8,9},{9,8},{10,11... | collective-permute-start | bytes 786440 | tf_op jit(solution)/shard_map/ppermute | solution.py:117
  47.2 8.7 %collective-permute-start.11 = (bf16[512,256]{1,0:T(8,128)(2,1)S(1)}, bf16[512,256]{1,0:T(8,128)(2,1)S(1)}, u32[]{:S(2)}, u32[]{:S(2)}) collective-permute-start(bf16[512,256]{1,0:T(8,128)(2,1)S(1)} %get-tuple-element.77), channel_id=1, source_target_pairs={{0,2},{2,0},{1,3},{3,1},{4,6},{6,4},{5,7},{7,5},{8,10},{10,8},{9,1... | collective-permute-start | bytes 786440 | tf_op jit(solution)/shard_map/ppermute | solution.py:117
  48.5 17.7 %collective-permute-start.12 = (bf16[512,256]{1,0:T(8,128)(2,1)S(1)}, bf16[512,256]{1,0:T(8,128)(2,1)S(1)}, u32[]{:S(2)}, u32[]{:S(2)}) collective-permute-start(bf16[512,256]{1,0:T(8,128)(2,1)S(1)} %get-tuple-element.78), channel_id=1, source_target_pairs={{0,4},{4,0},{8,12},{12,8},{1,5},{5,1},{9,13},{13,9},{2,6},{6,2},{1... | collective-permute-start | bytes 786440 | tf_op jit(solution)/shard_map/ppermute | solution.py:117
  50.6 21.7 %collective-permute-start.13 = (bf16[512,256]{1,0:T(8,128)(2,1)S(1)}, bf16[512,256]{1,0:T(8,128)(2,1)S(1)}, u32[]{:S(2)}, u32[]{:S(2)}) collective-permute-start(bf16[512,256]{1,0:T(8,128)(2,1)S(1)} %get-tuple-element.79), channel_id=1, source_target_pairs={{0,6},{2,4},{4,2},{6,0},{8,14},{10,12},{12,10},{14,8},{1,7},{3,5},... | collective-permute-start | bytes 786440 | tf_op jit(solution)/shard_map/ppermute | solution.py:382
  53.2 33.4 %collective-permute-start.14 = (bf16[528,512]{1,0:T(8,128)(2,1)S(1)}, bf16[528,512]{1,0:T(8,128)(2,1)S(1)}, u32[]{:S(2)}, u32[]{:S(2)}) collective-permute-start(bf16[528,512]{1,0:T(8,128)(2,1)S(1)} %shard_map.85.pair), channel_id=1, source_target_pairs={{0,8},{4,12},{8,0},{12,4},{1,9},{5,13},{9,1},{13,5},{2,10},{6,14},... | collective-permute-start | bytes 1622024 | tf_op jit(solution)/shard_map/ppermute | solution.py:117
  72.5 18.4 %collective-permute-start.15 = (bf16[512,256]{1,0:T(8,128)(2,1)S(1)}, bf16[512,256]{1,0:T(8,128)(2,1)S(1)}, u32[]{:S(2)}, u32[]{:S(2)}) collective-permute-start(bf16[512,256]{1,0:T(8,128)(2,1)S(1)} %select_convert_fusion), channel_id=1, source_target_pairs={{0,8},{4,12},{8,0},{12,4},{1,9},{5,13},{9,1},{13,5},{2,10},{6,14},... | collective-permute-start | bytes 786440 | tf_op jit(solution)/shard_map/ppermute | solution.py:117
  91.1 7.1 %collective-permute-start.16 = (bf16[512,256]{1,0:T(8,128)(2,1)S(1)}, bf16[512,256]{1,0:T(8,128)(2,1)S(1)}, u32[]{:S(2)}, u32[]{:S(2)}) collective-permute-start(bf16[512,256]{1,0:T(8,128)(2,1)S(1)} %add_convert_fusion.a0), channel_id=1, source_target_pairs={{0,2},{2,0},{1,3},{3,1},{4,6},{6,4},{5,7},{7,5},{8,10},{10,8},{9,1... | collective-permute-start | bytes 786440 | tf_op jit(solution)/shard_map/ppermute | solution.py:117
  91.7 12.4 %collective-permute-start.19 = (bf16[512,512]{1,0:T(8,128)(2,1)S(1)}, bf16[512,512]{1,0:T(8,128)(2,1)S(1)}, u32[]{:S(2)}, u32[]{:S(2)}) collective-permute-start(bf16[512,512]{1,0:T(8,128)(2,1)S(1)} %shard_map.86.g), channel_id=1, source_target_pairs={{0,4},{4,0},{8,12},{12,8},{1,5},{5,1},{9,13},{13,9},{2,6},{6,2},{1... | collective-permute-start | bytes 1572872 | tf_op jit(solution)/shard_map/ppermute | solution.py:117
  93.1 5.1 %collective-permute-start.17 = (bf16[512,256]{1,0:T(8,128)(2,1)S(1)}, bf16[512,256]{1,0:T(8,128)(2,1)S(1)}, u32[]{:S(2)}, u32[]{:S(2)}) collective-permute-start(bf16[512,256]{1,0:T(8,128)(2,1)S(1)} %add_convert_fusion.a0), channel_id=1, source_target_pairs={{0,1},{1,0},{2,3},{3,2},{4,5},{5,4},{6,7},{7,6},{8,9},{9,8},{10,11... | collective-permute-start | bytes 786440 | tf_op jit(solution)/shard_map/ppermute | solution.py:117
  98.2 1.5 %collective-permute-start.18 = (bf16[512,256]{1,0:T(8,128)(2,1)S(1)}, bf16[512,256]{1,0:T(8,128)(2,1)S(1)}, u32[]{:S(2)}, u32[]{:S(2)}) collective-permute-start(bf16[512,256]{1,0:T(8,128)(2,1)S(1)} %collective-permute-done.16.a1), channel_id=1, source_target_pairs={{0,1},{1,0},{2,3},{3,2},{4,5},{5,4},{6,7},{7,6},{8,9},{9,8},{10,11... | collective-permute-start | bytes 786440 | tf_op jit(solution)/shard_map/ppermute | solution.py:117

commit v9 on v7

--- a/solution.py
+++ b/solution.py
@@ -379,6 +379,12 @@
     acts_both = swap(acts_far, "col")
     acts_near = swap(acts_here, "col")
     to_pair, to_both, to_x, keep_a = rotate([acts_here, acts_far, acts_near, acts_both], tiles, 3, flips=(1, 2))
+    token, keep_a = tie(token, keep_a)
+    token, got_g = tie(token, got_g)
+    count = seqs * tok
+    pair_g = small_call(pair_kernel, count + 16, keep_g, got_g, note(source_ids))
+    token, pair_g, to_x = tie(token, pair_g, to_x)
+    across_g = swap(pair_g, "seq", 2)
     from_both = lax.ppermute(
         to_both,
         ("seq", "row"),
@@ -386,12 +392,6 @@
     )
     from_pair = swap(to_pair, "seq", 1)
     from_x = swap(to_x, "row")
-    token, keep_a = tie(token, keep_a)
-    token, got_g = tie(token, got_g)
-    count = seqs * tok
-    pair_g = small_call(pair_kernel, count + 16, keep_g, got_g, note(source_ids))
-    token, pair_g = tie(token, pair_g)
-    across_g = swap(pair_g, "seq", 2)
     (token,) = stand(token)
     token, from_x, from_pair, from_both = tie(token, from_x, from_pair, from_both)
     same, swapped = added(keep_a, from_pair), added(from_x, from_both)

time: 118 us -> 118 us (level)
    ppermute x1, starting transfers between devices: 1.39 us -> 0.01 us  [local_pairs(): lax.ppermute(to_both, ('seq', 'row'), [(i * rows + j, (i ^ 1) * rows + (j...]
    ppermute x17, starting transfers between devices: 26.6 us -> 27.8 us  [swap(): lax.ppermute(x, axis, [(i, i ^ step) for i in range(lax.axis_size(axis))])]
  transfers between devices with their start and end apart: 20 -> 20, of which waited for: 12 -> 11; matrix products, arithmetic and copies ran while one was open for 6% -> 6% of each run, Pallas kernels for 6% -> 6%
where the time goes in v9:
time: 118 us
  waiting for transfers between devices  53.5 us (45%)
  starting transfers between devices  32.6 us (28%)
  Pallas kernels  12.4 us (11%)
  blocking collectives  10.8 us (9%)
  other arithmetic  5.32 us (5%)
  local copies, waits for them, and re-layouts  2.51 us (2%)
    ppermute x17, waiting for transfers between devices, swap(): lax.ppermute(x, axis, [(i, i ^ step) for i in range(lax.axis_size(axis))])  44.8 us
    ppermute x17, starting transfers between devices, swap(): lax.ppermute(x, axis, [(i, i ^ step) for i in range(lax.axis_size(axis))])  27.8 us
    all_to_all x1, blocking collectives, local_pairs(): lax.all_to_all(message, PLANE, split_axis=0, concat_axis=0, tiled=True)  10.8 us
    ppermute x1, waiting for transfers between devices, local_pairs(): lax.ppermute(to_both, ('seq', 'row'), [(i * rows + j, (i ^ 1) * rows + (j...  6.71 us
    ppermute x2, starting transfers between devices, turned(): return lax.ppermute(x, PLANE, pairs)  4.8 us
    pallas_call x2, Pallas kernels, rotate(): pl.pallas_call(functools.partial(rotate_kernel, notes=len(note), flips=fl...  4.32 us
    pallas_call x1, Pallas kernels, outer_near(): pl.pallas_call(near_kernel, out_shape=(jax.ShapeDtypeStruct(eigvals.shape...  3.96 us
  transfers between devices with their start and end apart: 20, of which 11 were waited for; matrix products, arithmetic and copies ran while one was open for 6% of the time, Pallas kernels for 6%

profile of v9, /device:TPU:0, one launch (start us, length us, event | category | flops | bytes accessed | tf_op | source)
XLA Modules:
  0.0 117.9 jit_solution(9891388150800878885)
XLA Ops:
  0.6 1.6 %collective-permute-start = (bf16[128,1024]{1,0:T(8,128)(2,1)}, bf16[128,1024]{1,0:T(8,128)(2,1)S(1)}, u32[]{:S(2)}, u32[]{:S(2)}) collective-permute-start(bf16[128,1024]{1,0:T(8,128)(2,1)} %param.9), channel_id=1, source_target_pairs={{0,0},{1,4},{2,8},{3,12},{4,2},{5,6},{6,10},{7,14},{8,1},{9,5},{10... | collective-permute-start | bytes 786440 | tf_op jit(solution)/shard_map/ppermute | solution.py:344
  2.2 1.7 %slice_select_fusion = bf16[1024,512]{1,0:T(8,128)(2,1)S(1)} fusion(bf16[1024,1024]{1,0:T(8,128)(2,1)} %param.11, pred[]{:T(512)S(6)} %eq.30), kind=kLoop, calls=%fused_computation.8 | loop fusion | flops 524288 | bytes 3145729 | tf_op jit(solution)/shard_map/jit(_where)/select_n | solution.py:354
  3.9 3.5 %collective-permute-start.2 = (bf16[1024,512]{1,0:T(8,128)(2,1)S(1)}, bf16[1024,512]{1,0:T(8,128)(2,1)}, u32[]{:S(2)}, u32[]{:S(2)}) collective-permute-start(bf16[1024,512]{1,0:T(8,128)(2,1)S(1)} %slice_select_fusion), channel_id=1, source_target_pairs={{0,1},{1,0},{2,3},{3,2},{4,5},{5,4},{6,7},{7,6},{8,9},{9,8},{10,11... | collective-permute-start | bytes 3145736 | tf_op jit(solution)/shard_map/ppermute | solution.py:117
  7.4 3.5 %collective-permute-start.3 = (bf16[128,1024]{1,0:T(8,128)(2,1)}, bf16[128,1024]{1,0:T(8,128)(2,1)}, u32[]{:S(2)}, u32[]{:S(2)}) collective-permute-start(bf16[128,1024]{1,0:T(8,128)(2,1)} %param.8), channel_id=1, source_target_pairs={{0,2},{2,0},{1,3},{3,1},{4,6},{6,4},{5,7},{7,5},{8,10},{10,8},{9,1... | collective-permute-start | bytes 786440 | tf_op jit(solution)/shard_map/ppermute | solution.py:117
  10.9 1.7 %constant_dynamic-slice_fusion.9 = (bf16[1024,512]{1,0:T(8,128)(2,1)S(1)}, bf16[1024,512]{1,0:T(8,128)(2,1)S(1)}) fusion(bf16[1024,1024]{1,0:T(8,128)(2,1)} %param.12, s32[]{:T(128)S(6)} %select_n.92, s32[]{:T(128)S(6)} %select_n.93), kind=kLoop, calls=%fused_computation.27 | loop fusion | bytes 4194312 | tf_op jit(solution)/shard_map/dynamic_slice | solution.py:356
  12.6 0.3 pad_maximum_fusion.basis
  12.9 0.0 copy-start
  12.9 0.0 collective-permute-done.x0
  12.9 2.5 %collective-permute-start.1 = (bf16[128,1024]{1,0:T(8,128)(2,1)S(1)}, bf16[128,1024]{1,0:T(8,128)(2,1)S(1)}, u32[]{:S(2)}, u32[]{:S(2)}) collective-permute-start(bf16[128,1024]{1,0:T(8,128)(2,1)S(1)} %collective-permute-done.x0), channel_id=1, source_target_pairs={{0,2},{2,0},{1,3},{3,1},{4,6},{6,4},{5,7},{7,5},{8,10},{10,8},{9,1... | collective-permute-start | bytes 786440 | tf_op jit(solution)/shard_map/ppermute | solution.py:117
  15.5 4.0 %collective-permute-done.3 = bf16[128,1024]{1,0:T(8,128)(2,1)} collective-permute-done((bf16[128,1024]{1,0:T(8,128)(2,1)}, bf16[128,1024]{1,0:T(8,128)(2,1)}, u32[]{:S(2)}, u32[]{:S(2)}) %collective-permute-start.3) | collective-permute-done | bytes 262176 | tf_op jit(solution)/shard_map/ppermute | solution.py:117
  19.5 3.2 %collective-permute-start.4 = (bf16[128,1024]{1,0:T(8,128)(2,1)}, bf16[128,1024]{1,0:T(8,128)(2,1)}, u32[]{:S(2)}, u32[]{:S(2)}) collective-permute-start(bf16[128,1024]{1,0:T(8,128)(2,1)} %collective-permute-done.3), channel_id=1, source_target_pairs={{0,8},{1,12},{2,0},{3,4},{4,10},{5,14},{6,2},{7,6},{8,9},{9,13},{1... | collective-permute-start | bytes 786440 | tf_op jit(solution)/shard_map/ppermute | solution.py:344
  22.7 0.0 collective-permute-done.2
  22.7 1.7 %broadcast_select_fusion.1 = (bf16[1024,512]{1,0:T(8,128)(2,1)S(1)}, bf16[1024,512]{1,0:T(8,128)(2,1)S(1)}) fusion(bf16[1024,512]{1,0:T(8,128)(2,1)} %collective-permute-done.2, pred[]{:T(512)S(6)} %eq.29, bf16[1024,1024]{1,0:T(8,128)(2,1)S(1)} %copy-done, s32[]{:T(128)S(6)} %select_n.97), kind=kLoop, calls=%fused_computation.10 | loop fusion | flops 1048576 | bytes 4194309 | tf_op jit(solution)/shard_map/jit(_where)/select_n | solution.py:365
  24.4 0.4 fusion.1
  24.8 0.1 fusion.2
  24.9 0.4 fusion
  25.3 0.0 copy-start.1
  25.3 0.3 pad_maximum_fusion.1.basis
  25.6 0.0 collective-permute-done.1.x1
  25.7 1.4 %collective-permute-start.5 = (bf16[128,1024]{1,0:T(8,128)(2,1)S(1)}, bf16[128,1024]{1,0:T(8,128)(2,1)S(1)}, u32[]{:S(2)}, u32[]{:S(2)}) collective-permute-start(bf16[128,1024]{1,0:T(8,128)(2,1)S(1)} %collective-permute-done.x0), channel_id=1, source_target_pairs={{0,1},{1,0},{2,3},{3,2},{4,5},{5,4},{6,7},{7,6},{8,9},{9,8},{10,11... | collective-permute-start | bytes 786440 | tf_op jit(solution)/shard_map/ppermute | solution.py:117
  27.1 0.1 collective-permute-start.6
  27.2 0.0 copy-done.1
  27.2 1.9 %collective-permute-done.4.x0 = bf16[128,1024]{1,0:T(8,128)(2,1)} collective-permute-done((bf16[128,1024]{1,0:T(8,128)(2,1)}, bf16[128,1024]{1,0:T(8,128)(2,1)}, u32[]{:S(2)}, u32[]{:S(2)}) %collective-permute-start.4) | collective-permute-done | bytes 262176 | tf_op jit(solution)/shard_map/ppermute | solution.py:344
  29.1 0.0 collective-permute-done.5.x2
  29.1 0.0 collective-permute-done.6.x3
  29.1 2.0 %rotate.2 = (bf16[528,512]{1,0:T(8,128)(2,1)}, f32[512,512]{1,0:T(8,128)S(1)}) custom-call(bf16[128,1024]{1,0:T(8,128)(2,1)S(1)} %collective-permute-done.x0, bf16[128,1024]{1,0:T(8,128)(2,1)S(1)} %collective-permute-done.1.x1, bf16[128,1024]{1,0:T(8,128)(2,1)S(1)} %collective-permute-done.5.x2, bf16[128,1024]{1,0:T(8,128)(2,1)S(1)} %collective-permute-done.6.x3, ...), custom_call_target="tpu_custom_call" | custom-call | flops 1073741824 | bytes 2097152 | tf_op jit(solution)/shard_map/rotate/pallas_call | solution.py:165
  31.1 3.4 %collective-permute-start.7 = (bf16[128,1024]{1,0:T(8,128)(2,1)}, bf16[128,1024]{1,0:T(8,128)(2,1)S(1)}, u32[]{:S(2)}, u32[]{:S(2)}) collective-permute-start(bf16[128,1024]{1,0:T(8,128)(2,1)} %collective-permute-done.4.x0), channel_id=1, source_target_pairs={{0,2},{2,0},{1,3},{3,1},{4,6},{6,4},{5,7},{7,5},{8,10},{10,8},{9,1... | collective-permute-start | bytes 786440 | tf_op jit(solution)/shard_map/ppermute | solution.py:117
  34.5 2.2 %collective-permute-start.10 = (bf16[528,512]{1,0:T(8,128)(2,1)}, bf16[528,512]{1,0:T(8,128)(2,1)}, u32[]{:S(2)}, u32[]{:S(2)}) collective-permute-start(bf16[528,512]{1,0:T(8,128)(2,1)} %get-tuple-element.73), channel_id=1, source_target_pairs={{0,4},{4,0},{8,12},{12,8},{1,5},{5,1},{9,13},{13,9},{2,6},{6,2},{1... | collective-permute-start | bytes 1622024 | tf_op jit(solution)/shard_map/ppermute | solution.py:117
  36.7 2.8 %collective-permute-done.7.x1 = bf16[128,1024]{1,0:T(8,128)(2,1)S(1)} collective-permute-done((bf16[128,1024]{1,0:T(8,128)(2,1)}, bf16[128,1024]{1,0:T(8,128)(2,1)S(1)}, u32[]{:S(2)}, u32[]{:S(2)}) %collective-permute-start.7) | collective-permute-done | bytes 262176 | tf_op jit(solution)/shard_map/ppermute | solution.py:117
  39.5 3.5 %collective-permute-start.8 = (bf16[128,1024]{1,0:T(8,128)(2,1)}, bf16[128,1024]{1,0:T(8,128)(2,1)}, u32[]{:S(2)}, u32[]{:S(2)}) collective-permute-start(bf16[128,1024]{1,0:T(8,128)(2,1)} %collective-permute-done.4.x0), channel_id=1, source_target_pairs={{0,1},{1,0},{2,3},{3,2},{4,5},{5,4},{6,7},{7,6},{8,9},{9,8},{10,11... | collective-permute-start | bytes 786440 | tf_op jit(solution)/shard_map/ppermute | solution.py:117
  43.0 0.0 collective-permute-start.9
  43.0 1.8 %collective-permute-done.8.x2 = bf16[128,1024]{1,0:T(8,128)(2,1)} collective-permute-done((bf16[128,1024]{1,0:T(8,128)(2,1)}, bf16[128,1024]{1,0:T(8,128)(2,1)}, u32[]{:S(2)}, u32[]{:S(2)}) %collective-permute-start.8) | collective-permute-done | bytes 262176 | tf_op jit(solution)/shard_map/ppermute | solution.py:117
  44.9 0.0 collective-permute-done.9.x3
  44.9 2.4 %rotate.3 = (bf16[512,256]{1,0:T(8,128)(2,1)S(1)}, bf16[512,256]{1,0:T(8,128)(2,1)S(1)}, bf16[512,256]{1,0:T(8,128)(2,1)S(1)}, f32[512,256]{1,0:T(8,128)S(1)}) custom-call(bf16[128,1024]{1,0:T(8,128)(2,1)} %collective-permute-done.4.x0, bf16[128,1024]{1,0:T(8,128)(2,1)S(1)} %collective-permute-done.7.x1, bf16[128,1024]{1,0:T(8,128)(2,1)} %collective-permute-done.8.x2, ...), custom_call_target="tpu_custom_call" | custom-call | flops 1073741824 | bytes 2097152 | tf_op jit(solution)/shard_map/rotate/pallas_call | solution.py:165
  47.2 3.2 %collective-permute-start.12 = (bf16[512,256]{1,0:T(8,128)(2,1)S(1)}, bf16[512,256]{1,0:T(8,128)(2,1)S(1)}, u32[]{:S(2)}, u32[]{:S(2)}) collective-permute-start(bf16[512,256]{1,0:T(8,128)(2,1)S(1)} %get-tuple-element.80), channel_id=1, source_target_pairs={{0,4},{4,0},{8,12},{12,8},{1,5},{5,1},{9,13},{13,9},{2,6},{6,2},{1... | collective-permute-start | bytes 786440 | tf_op jit(solution)/shard_map/ppermute | solution.py:117
  50.5 0.0 collective-permute-start.13
  50.5 0.0 collective-permute-done.10.got
  50.5 1.1 shard_map.85.pair
  51.6 1.6 %collective-permute-start.11 = (bf16[512,256]{1,0:T(8,128)(2,1)S(1)}, bf16[512,256]{1,0:T(8,128)(2,1)S(1)}, u32[]{:S(2)}, u32[]{:S(2)}) collective-permute-start(bf16[512,256]{1,0:T(8,128)(2,1)S(1)} %get-tuple-element.79), channel_id=1, source_target_pairs={{0,2},{2,0},{1,3},{3,1},{4,6},{6,4},{5,7},{7,5},{8,10},{10,8},{9,1... | collective-permute-start | bytes 786440 | tf_op jit(solution)/shard_map/ppermute | solution.py:117
  53.2 1.5 %collective-permute-start.14 = (bf16[528,512]{1,0:T(8,128)(2,1)S(1)}, bf16[528,512]{1,0:T(8,128)(2,1)S(1)}, u32[]{:S(2)}, u32[]{:S(2)}) collective-permute-start(bf16[528,512]{1,0:T(8,128)(2,1)S(1)} %shard_map.85.pair), channel_id=1, source_target_pairs={{0,8},{4,12},{8,0},{12,4},{1,9},{5,13},{9,1},{13,5},{2,10},{6,14},... | collective-permute-start | bytes 1622024 | tf_op jit(solution)/shard_map/ppermute | solution.py:117
  54.7 9.6 %collective-permute-done.12 = bf16[512,256]{1,0:T(8,128)(2,1)S(1)} collective-permute-done((bf16[512,256]{1,0:T(8,128)(2,1)S(1)}, bf16[512,256]{1,0:T(8,128)(2,1)S(1)}, u32[]{:S(2)}, u32[]{:S(2)}) %collective-permute-start.12) | collective-permute-done | bytes 262176 | tf_op jit(solution)/shard_map/ppermute | solution.py:117
  64.3 6.7 %collective-permute-done.13 = bf16[512,256]{1,0:T(8,128)(2,1)S(1)} collective-permute-done((bf16[512,256]{1,0:T(8,128)(2,1)S(1)}, bf16[512,256]{1,0:T(8,128)(2,1)S(1)}, u32[]{:S(2)}, u32[]{:S(2)}) %collective-permute-start.13) | collective-permute-done | bytes 262176 | tf_op jit(solution)/shard_map/ppermute | solution.py:388
  71.0 0.0 collective-permute-done.11
  71.0 0.1 select_convert_fusion
  71.2 0.1 collective-permute-start.15
  71.3 15.3 %collective-permute-done.14.across = bf16[528,512]{1,0:T(8,128)(2,1)S(1)} collective-permute-done((bf16[528,512]{1,0:T(8,128)(2,1)S(1)}, bf16[528,512]{1,0:T(8,128)(2,1)S(1)}, u32[]{:S(2)}, u32[]{:S(2)}) %collective-permute-start.14) | collective-permute-done | bytes 540704 | tf_op jit(solution)/shard_map/ppermute | solution.py:117
  86.5 0.1 shard_map.86.g
  86.6 4.3 %collective-permute-done.15 = bf16[512,256]{1,0:T(8,128)(2,1)S(1)} collective-permute-done((bf16[512,256]{1,0:T(8,128)(2,1)S(1)}, bf16[512,256]{1,0:T(8,128)(2,1)S(1)}, u32[]{:S(2)}, u32[]{:S(2)}) %collective-permute-start.15) | collective-permute-done | bytes 262176 | tf_op jit(solution)/shard_map/ppermute | solution.py:117
  90.9 0.2 add_convert_fusion.a0
  91.1 0.6 collective-permute-start.16
  91.6 0.7 collective-permute-start.19
  92.3 0.1 pad_add_fusion.place
  92.4 0.7 slice.27
  93.0 0.0 collective-permute-start.17
  93.0 5.2 %collective-permute-done.16.a1 = bf16[512,256]{1,0:T(8,128)(2,1)S(1)} collective-permute-done((bf16[512,256]{1,0:T(8,128)(2,1)S(1)}, bf16[512,256]{1,0:T(8,128)(2,1)S(1)}, u32[]{:S(2)}, u32[]{:S(2)}) %collective-permute-start.16) | collective-permute-done | bytes 262176 | tf_op jit(solution)/shard_map/ppermute | solution.py:117
  98.2 0.0 collective-permute-start.18
  98.3 0.0 collective-permute-done.17.a2
  98.3 1.5 %collective-permute-done.18.a3 = bf16[512,256]{1,0:T(8,128)(2,1)S(1)} collective-permute-done((bf16[512,256]{1,0:T(8,128)(2,1)S(1)}, bf16[512,256]{1,0:T(8,128)(2,1)S(1)}, u32[]{:S(2)}, u32[]{:S(2)}) %collective-permute-start.18) | collective-permute-done | bytes 262176 | tf_op jit(solution)/shard_map/ppermute | solution.py:117
  99.8 4.0 %outer_near.1 = (f32[1024,1024]{1,0:T(8,128)}, f32[512,128]{1,0:T(8,128)S(1)}, bf16[512,1024]{1,0:T(8,128)(2,1)S(1)}, bf16[1024,512]{1,0:T(8,128)(2,1)S(1)}, f32[1024,512]{1,0:T(8,128)S(1)}) custom-call(s32[3]{0:T(128)S(1)} %pad_add_fusion.place, bf16[512,256]{1,0:T(8,128)(2,1)S(1)} %add_convert_fusion.a0, bf16[512,256]{1,0:T(8,128)(2,1)S(1)} %collective-permute-done.16.a1, ...), custom_call_target="tpu_custom_call" | custom-call | flops 1073741824 | bytes 6291456 | tf_op jit(solution)/shard_map/outer_near/pallas_call | solution.py:273
  103.7 0.3 collective-permute-done.19.g
  104.1 2.3 %outer_far.1 = (f32[1024,1024]{1,0:T(8,128)}, f32[4,128]{1,0:T(4,128)S(1)}) custom-call(s32[3]{0:T(128)S(1)} %pad_add_fusion.place, bf16[512,1024]{1,0:T(8,128)(2,1)S(1)} %get-tuple-element.92.flat, bf16[1024,512]{1,0:T(8,128)(2,1)S(1)} %get-tuple-element.93.turned, bf16[512,512]{1,0:T(8,128)(2,1)S(1)} %collective-permute-done.19.g, ...), custom_call_target="tpu_custom_call", output_to_operand_aliasing={{0}: (5, {})} | custom-call | flops 1073741824 | bytes 2097152 | tf_op jit(solution)/shard_map/outer_far/pallas_call | solution.py:304
  106.4 0.1 select_reduce_fusion
  106.6 10.8 %all_to_all.11 = f32[16,1,136]{2,1,0:T(1,128)S(1)} all-to-all(f32[16,1,136]{2,1,0:T(1,128)S(1)} %all_to_all.7), channel_id=1, replica_groups=mesh['grp'=2,'seq'=4,'row'=2,'col'=2] {'seq','row','col'}, dimensions={0} | all-to-all | bytes 17408 | tf_op jit(solution)/shard_map/all_to_all | solution.py:420
  117.4 0.5 finish.1
  (19 shorter events, 0.1 us)
Async XLA Ops:
  0.6 12.3 %collective-permute-start = (bf16[128,1024]{1,0:T(8,128)(2,1)}, bf16[128,1024]{1,0:T(8,128)(2,1)S(1)}, u32[]{:S(2)}, u32[]{:S(2)}) collective-permute-start(bf16[128,1024]{1,0:T(8,128)(2,1)} %param.9), channel_id=1, source_target_pairs={{0,0},{1,4},{2,8},{3,12},{4,2},{5,6},{6,10},{7,14},{8,1},{9,5},{10... | collective-permute-start | bytes 786440 | tf_op jit(solution)/shard_map/ppermute | solution.py:344
  3.9 18.8 %collective-permute-start.2 = (bf16[1024,512]{1,0:T(8,128)(2,1)S(1)}, bf16[1024,512]{1,0:T(8,128)(2,1)}, u32[]{:S(2)}, u32[]{:S(2)}) collective-permute-start(bf16[1024,512]{1,0:T(8,128)(2,1)S(1)} %slice_select_fusion), channel_id=1, source_target_pairs={{0,1},{1,0},{2,3},{3,2},{4,5},{5,4},{6,7},{7,6},{8,9},{9,8},{10,11... | collective-permute-start | bytes 3145736 | tf_op jit(solution)/shard_map/ppermute | solution.py:117
  7.4 12.1 %collective-permute-start.3 = (bf16[128,1024]{1,0:T(8,128)(2,1)}, bf16[128,1024]{1,0:T(8,128)(2,1)}, u32[]{:S(2)}, u32[]{:S(2)}) collective-permute-start(bf16[128,1024]{1,0:T(8,128)(2,1)} %param.8), channel_id=1, source_target_pairs={{0,2},{2,0},{1,3},{3,1},{4,6},{6,4},{5,7},{7,5},{8,10},{10,8},{9,1... | collective-permute-start | bytes 786440 | tf_op jit(solution)/shard_map/ppermute | solution.py:117
  12.9 9.8 %copy-start = (bf16[1024,1024]{1,0:T(8,128)(2,1)S(1)}, bf16[1024,1024]{1,0:T(8,128)(2,1)}, u32[]{:S(2)}) copy-start(bf16[1024,1024]{1,0:T(8,128)(2,1)} %param.11) | copy-start | bytes 6291460
  12.9 12.7 %collective-permute-start.1 = (bf16[128,1024]{1,0:T(8,128)(2,1)S(1)}, bf16[128,1024]{1,0:T(8,128)(2,1)S(1)}, u32[]{:S(2)}, u32[]{:S(2)}) collective-permute-start(bf16[128,1024]{1,0:T(8,128)(2,1)S(1)} %collective-permute-done.x0), channel_id=1, source_target_pairs={{0,2},{2,0},{1,3},{3,1},{4,6},{6,4},{5,7},{7,5},{8,10},{10,8},{9,1... | collective-permute-start | bytes 786440 | tf_op jit(solution)/shard_map/ppermute | solution.py:117
  19.5 9.6 %collective-permute-start.4 = (bf16[128,1024]{1,0:T(8,128)(2,1)}, bf16[128,1024]{1,0:T(8,128)(2,1)}, u32[]{:S(2)}, u32[]{:S(2)}) collective-permute-start(bf16[128,1024]{1,0:T(8,128)(2,1)} %collective-permute-done.3), channel_id=1, source_target_pairs={{0,8},{1,12},{2,0},{3,4},{4,10},{5,14},{6,2},{7,6},{8,9},{9,13},{1... | collective-permute-start | bytes 786440 | tf_op jit(solution)/shard_map/ppermute | solution.py:344
  25.3 1.8 %copy-start.1 = (s32[128]{0:T(128)S(1)}, s32[128]{0:T(128)}, u32[]{:S(2)}) copy-start(s32[128]{0:T(128)} %param.10) | copy-start | bytes 1540
  25.7 3.5 %collective-permute-start.5 = (bf16[128,1024]{1,0:T(8,128)(2,1)S(1)}, bf16[128,1024]{1,0:T(8,128)(2,1)S(1)}, u32[]{:S(2)}, u32[]{:S(2)}) collective-permute-start(bf16[128,1024]{1,0:T(8,128)(2,1)S(1)} %collective-permute-done.x0), channel_id=1, source_target_pairs={{0,1},{1,0},{2,3},{3,2},{4,5},{5,4},{6,7},{7,6},{8,9},{9,8},{10,11... | collective-permute-start | bytes 786440 | tf_op jit(solution)/shard_map/ppermute | solution.py:117
  27.1 2.0 %collective-permute-start.6 = (bf16[128,1024]{1,0:T(8,128)(2,1)S(1)}, bf16[128,1024]{1,0:T(8,128)(2,1)S(1)}, u32[]{:S(2)}, u32[]{:S(2)}) collective-permute-start(bf16[128,1024]{1,0:T(8,128)(2,1)S(1)} %collective-permute-done.1.x1), channel_id=1, source_target_pairs={{0,1},{1,0},{2,3},{3,2},{4,5},{5,4},{6,7},{7,6},{8,9},{9,8},{10,11... | collective-permute-start | bytes 786440 | tf_op jit(solution)/shard_map/ppermute | solution.py:117
  31.1 8.4 %collective-permute-start.7 = (bf16[128,1024]{1,0:T(8,128)(2,1)}, bf16[128,1024]{1,0:T(8,128)(2,1)S(1)}, u32[]{:S(2)}, u32[]{:S(2)}) collective-permute-start(bf16[128,1024]{1,0:T(8,128)(2,1)} %collective-permute-done.4.x0), channel_id=1, source_target_pairs={{0,2},{2,0},{1,3},{3,1},{4,6},{6,4},{5,7},{7,5},{8,10},{10,8},{9,1... | collective-permute-start | bytes 786440 | tf_op jit(solution)/shard_map/ppermute | solution.py:117
  34.5 16.0 %collective-permute-start.10 = (bf16[528,512]{1,0:T(8,128)(2,1)}, bf16[528,512]{1,0:T(8,128)(2,1)}, u32[]{:S(2)}, u32[]{:S(2)}) collective-permute-start(bf16[528,512]{1,0:T(8,128)(2,1)} %get-tuple-element.73), channel_id=1, source_target_pairs={{0,4},{4,0},{8,12},{12,8},{1,5},{5,1},{9,13},{13,9},{2,6},{6,2},{1... | collective-permute-start | bytes 1622024 | tf_op jit(solution)/shard_map/ppermute | solution.py:117
  39.5 5.4 %collective-permute-start.8 = (bf16[128,1024]{1,0:T(8,128)(2,1)}, bf16[128,1024]{1,0:T(8,128)(2,1)}, u32[]{:S(2)}, u32[]{:S(2)}) collective-permute-start(bf16[128,1024]{1,0:T(8,128)(2,1)} %collective-permute-done.4.x0), channel_id=1, source_target_pairs={{0,1},{1,0},{2,3},{3,2},{4,5},{5,4},{6,7},{7,6},{8,9},{9,8},{10,11... | collective-permute-start | bytes 786440 | tf_op jit(solution)/shard_map/ppermute | solution.py:117
  43.0 1.8 %collective-permute-start.9 = (bf16[128,1024]{1,0:T(8,128)(2,1)S(1)}, bf16[128,1024]{1,0:T(8,128)(2,1)}, u32[]{:S(2)}, u32[]{:S(2)}) collective-permute-start(bf16[128,1024]{1,0:T(8,128)(2,1)S(1)} %collective-permute-done.7.x1), channel_id=1, source_target_pairs={{0,1},{1,0},{2,3},{3,2},{4,5},{5,4},{6,7},{7,6},{8,9},{9,8},{10,11... | collective-permute-start | bytes 786440 | tf_op jit(solution)/shard_map/ppermute | solution.py:117
  47.2 17.1 %collective-permute-start.12 = (bf16[512,256]{1,0:T(8,128)(2,1)S(1)}, bf16[512,256]{1,0:T(8,128)(2,1)S(1)}, u32[]{:S(2)}, u32[]{:S(2)}) collective-permute-start(bf16[512,256]{1,0:T(8,128)(2,1)S(1)} %get-tuple-element.80), channel_id=1, source_target_pairs={{0,4},{4,0},{8,12},{12,8},{1,5},{5,1},{9,13},{13,9},{2,6},{6,2},{1... | collective-permute-start | bytes 786440 | tf_op jit(solution)/shard_map/ppermute | solution.py:117
  50.5 20.6 %collective-permute-start.13 = (bf16[512,256]{1,0:T(8,128)(2,1)S(1)}, bf16[512,256]{1,0:T(8,128)(2,1)S(1)}, u32[]{:S(2)}, u32[]{:S(2)}) collective-permute-start(bf16[512,256]{1,0:T(8,128)(2,1)S(1)} %get-tuple-element.81), channel_id=1, source_target_pairs={{0,6},{2,4},{4,2},{6,0},{8,14},{10,12},{12,10},{14,8},{1,7},{3,5},... | collective-permute-start | bytes 786440 | tf_op jit(solution)/shard_map/ppermute | solution.py:388
  51.6 19.4 %collective-permute-start.11 = (bf16[512,256]{1,0:T(8,128)(2,1)S(1)}, bf16[512,256]{1,0:T(8,128)(2,1)S(1)}, u32[]{:S(2)}, u32[]{:S(2)}) collective-permute-start(bf16[512,256]{1,0:T(8,128)(2,1)S(1)} %get-tuple-element.79), channel_id=1, source_target_pairs={{0,2},{2,0},{1,3},{3,1},{4,6},{6,4},{5,7},{7,5},{8,10},{10,8},{9,1... | collective-permute-start | bytes 786440 | tf_op jit(solution)/shard_map/ppermute | solution.py:117
  53.2 33.3 %collective-permute-start.14 = (bf16[528,512]{1,0:T(8,128)(2,1)S(1)}, bf16[528,512]{1,0:T(8,128)(2,1)S(1)}, u32[]{:S(2)}, u32[]{:S(2)}) collective-permute-start(bf16[528,512]{1,0:T(8,128)(2,1)S(1)} %shard_map.85.pair), channel_id=1, source_target_pairs={{0,8},{4,12},{8,0},{12,4},{1,9},{5,13},{9,1},{13,5},{2,10},{6,14},... | collective-permute-start | bytes 1622024 | tf_op jit(solution)/shard_map/ppermute | solution.py:117
  71.2 19.7 %collective-permute-start.15 = (bf16[512,256]{1,0:T(8,128)(2,1)S(1)}, bf16[512,256]{1,0:T(8,128)(2,1)S(1)}, u32[]{:S(2)}, u32[]{:S(2)}) collective-permute-start(bf16[512,256]{1,0:T(8,128)(2,1)S(1)} %select_convert_fusion), channel_id=1, source_target_pairs={{0,8},{4,12},{8,0},{12,4},{1,9},{5,13},{9,1},{13,5},{2,10},{6,14},... | collective-permute-start | bytes 786440 | tf_op jit(solution)/shard_map/ppermute | solution.py:117
  91.1 7.2 %collective-permute-start.16 = (bf16[512,256]{1,0:T(8,128)(2,1)S(1)}, bf16[512,256]{1,0:T(8,128)(2,1)S(1)}, u32[]{:S(2)}, u32[]{:S(2)}) collective-permute-start(bf16[512,256]{1,0:T(8,128)(2,1)S(1)} %add_convert_fusion.a0), channel_id=1, source_target_pairs={{0,2},{2,0},{1,3},{3,1},{4,6},{6,4},{5,7},{7,5},{8,10},{10,8},{9,1... | collective-permute-start | bytes 786440 | tf_op jit(solution)/shard_map/ppermute | solution.py:117
  91.6 12.4 %collective-permute-start.19 = (bf16[512,512]{1,0:T(8,128)(2,1)S(1)}, bf16[512,512]{1,0:T(8,128)(2,1)S(1)}, u32[]{:S(2)}, u32[]{:S(2)}) collective-permute-start(bf16[512,512]{1,0:T(8,128)(2,1)S(1)} %shard_map.86.g), channel_id=1, source_target_pairs={{0,4},{4,0},{8,12},{12,8},{1,5},{5,1},{9,13},{13,9},{2,6},{6,2},{1... | collective-permute-start | bytes 1572872 | tf_op jit(solution)/shard_map/ppermute | solution.py:117
  93.0 5.3 %collective-permute-start.17 = (bf16[512,256]{1,0:T(8,128)(2,1)S(1)}, bf16[512,256]{1,0:T(8,128)(2,1)S(1)}, u32[]{:S(2)}, u32[]{:S(2)}) collective-permute-start(bf16[512,256]{1,0:T(8,128)(2,1)S(1)} %add_convert_fusion.a0), channel_id=1, source_target_pairs={{0,1},{1,0},{2,3},{3,2},{4,5},{5,4},{6,7},{7,6},{8,9},{9,8},{10,11... | collective-permute-start | bytes 786440 | tf_op jit(solution)/shard_map/ppermute | solution.py:117
  98.2 1.5 %collective-permute-start.18 = (bf16[512,256]{1,0:T(8,128)(2,1)S(1)}, bf16[512,256]{1,0:T(8,128)(2,1)S(1)}, u32[]{:S(2)}, u32[]{:S(2)}) collective-permute-start(bf16[512,256]{1,0:T(8,128)(2,1)S(1)} %collective-permute-done.16.a1), channel_id=1, source_target_pairs={{0,1},{1,0},{2,3},{3,2},{4,5},{5,4},{6,7},{7,6},{8,9},{9,8},{10,11... | collective-permute-start | bytes 786440 | tf_op jit(solution)/shard_map/ppermute | solution.py:117
